TPU v7x, 512 devices: a whole 4x8x8 slice. The times are simulated.
512 devices in a mesh: cfg: 2 (over core), head: 8 (over z), kv: 32 (over x, y).
Axes of the slice: x: 4, y: 8, z: 8, core: 2. Of those that a mesh axis runs over, the one named last changes fastest.
Arguments:
- queries: bfloat16 [32, 128, 5120], P(('cfg', 'head'), 'kv'), parts along dimension 0, may hold values from -20 to 20
- keys: bfloat16 [128, 128, 5120], P(('cfg', 'kv'), 'head'), parts along dimension 0, may hold values from -20 to 20
- values: bfloat16 [128, 128, 5120], P(('cfg', 'kv'), 'head'), parts along dimension 0, may hold values from -6 to 6
- mask_cols: int32 [16, 32], replicated, may hold values from 0 to 63, as said below
- mask_counts: int32 [16], replicated, may hold values from 16 to 32
Outputs:
- attended: bfloat16 [32, 128, 5120], P(('cfg', 'head'), 'kv'), parts along dimension 0
There are 2 independent parts, one for each index of `cfg`. A program takes and returns all parts, laid end to end along the dimension named above; an argument that names none is the same for every part. Nothing has to cross between parts.
Inputs may be any that keep to these rules, and one draw needn't show every extreme that they name: `mask_cols`: within a row the entries are distinct key blocks.
All inputs are finite; a program needn't handle non-finite values.
Results may differ from a plain program's by a relative error of at most 0.0055.
Values may be sent and summed in bfloat16 or wider, within the bound.
No kernel may reach another device: no remote copies, remote signals or barrier semaphores. Data moves between devices by JAX's collectives and lax.ppermute only.
A program may use at most 64 MiB of HBM per device.

v0:
```python
import jax
import jax.numpy as jnp
from jax import lax
from jax.sharding import PartitionSpec as P

DH = 128
D = 5120


def from_partner(block, axis, apart):
    count = lax.axis_size(axis)
    route = []
    for low in range(count):
        high = low | 1 << apart
        if high != low and high < count:
            route += [(low, high), (high, low)]
    return lax.ppermute(block, axis, route)


def finish_rows(lse_all, out_all):
    top = jnp.max(lse_all, axis=0)
    weight = jnp.exp(lse_all - top[None])
    norm = jnp.sum(weight, axis=0)
    summed = jnp.sum(out_all.astype(jnp.float32) * weight[..., None], axis=0)
    return (summed / norm[..., None]).astype(jnp.bfloat16)


def local(queries, keys, values, mask_cols, mask_counts):
    n_head = lax.axis_size("head")
    n_kv = lax.axis_size("kv")
    h_local = D // DH // n_head
    scale = 1.0 / DH**0.5
    query_heads = lax.all_to_all(queries, "head", split_axis=2, concat_axis=0, tiled=True)
    key_heads, value_heads = (
        lax.all_to_all(keys, "head", split_axis=2, concat_axis=1, tiled=True),
        lax.all_to_all(values, "head", split_axis=2, concat_axis=1, tiled=True),
    )
    query_all = lax.all_gather(query_heads, "kv", axis=1, tiled=True)
    qblocks = query_all.shape[0]
    kb_local = key_heads.shape[0]
    block = key_heads.shape[1]
    kv_index = lax.axis_index("kv")
    owned = kv_index * kb_local + jnp.arange(kb_local, dtype=jnp.int32)
    listed = jnp.arange(mask_cols.shape[1])[None, :] < mask_counts[:, None]
    allowed = jnp.any((mask_cols[:, :, None] == owned[None, None, :]) & listed[:, :, None], axis=1)
    key_open = jnp.repeat(allowed, block, axis=1)
    key_local = key_heads.reshape(kb_local * block, h_local, DH)
    value_local = value_heads.reshape(kb_local * block, h_local, DH)
    group = 4
    turns = qblocks // group
    query_groups = query_all.reshape(turns, group, block, h_local, DH)
    open_groups = key_open.reshape(turns, group, kb_local * block)

    def attend(item):
        query_group, open_group = item
        live = open_group[:, None, None, :]
        scores = (
            jnp.einsum("bqhd,khd->bhqk", query_group, key_local, preferred_element_type=jnp.float32)
            * scale
        )
        scores = jnp.where(live, scores, -1e30)
        group_top = jnp.max(scores, axis=-1)
        weights = jnp.where(live, jnp.exp(scores - group_top[..., None]), 0.0)
        group_total = jnp.sum(weights, axis=-1)
        partial_sum = jnp.einsum(
            "bhqk,khd->bqhd",
            weights.astype(jnp.bfloat16),
            value_local,
            preferred_element_type=jnp.float32,
        )
        safe = jnp.maximum(group_total.transpose(0, 2, 1), 1.0)
        group_out = (partial_sum / safe[..., None]).astype(jnp.bfloat16)
        group_lse = group_top.transpose(0, 2, 1) + jnp.log(safe)
        return (group_lse, group_out)

    lse, out = lax.map(attend, (query_groups, open_groups))
    lse = lse.reshape(qblocks, block, h_local)
    out = out.reshape(qblocks, block, h_local, DH)
    levels = n_kv.bit_length() - 1
    lse_all = lse[None]
    out_all = out[None]
    for level in range(levels - 1, -1, -1):
        half = lse_all.shape[2] // 2
        upper = kv_index >> level & 1 == 1
        keep_lse = jnp.where(upper, lse_all[:, :, half:], lse_all[:, :, :half])
        keep_out = jnp.where(upper, out_all[:, :, half:], out_all[:, :, :half])
        send_lse = jnp.where(upper, lse_all[:, :, :half], lse_all[:, :, half:])
        send_out = jnp.where(upper, out_all[:, :, :half], out_all[:, :, half:])
        got_lse = from_partner(send_lse, "kv", level)
        got_out = from_partner(send_out, "kv", level)
        lse_all = jnp.concatenate([keep_lse, got_lse], axis=0)
        out_all = jnp.concatenate([keep_out, got_out], axis=0)
    finished = finish_rows(lse_all, out_all)
    finished = finished.reshape(qblocks, finished.shape[1], h_local * DH)
    return lax.all_to_all(finished, "head", split_axis=0, concat_axis=2, tiled=True)


def solution(mesh):
    in_specs = (
        P(("cfg", "head"), "kv", None),
        P(("cfg", "kv"), "head", None),
        P(("cfg", "kv"), "head", None),
        P(),
        P(),
    )
    out_specs = P(("cfg", "head"), "kv", None)
    return jax.shard_map(local, mesh=mesh, in_specs=in_specs, out_specs=out_specs, check_vma=False)
```

profile of v0, /device:TPU:24, one launch (start us, length us, event | category | flops | bytes accessed | tf_op | source)
XLA Modules:
  0.0 451.1 jit_solution(2423637127275120146)
XLA Ops:
  6.5 4.1 copy.124
  10.6 5.1 %reshape.73 = bf16[8,2,2560]{2,1,0:T(2,128)(2,1)S(1)} reshape(bf16[5120,2,4]{2,1,0:T(2,128)(2,1)S(1)} %bitcast.113) | data formatting | bytes 163840
  15.7 18.7 %all_to_all.66 = bf16[8,2,2560]{2,1,0:T(2,128)(2,1)S(1)} all-to-all(bf16[8,2,2560]{2,1,0:T(2,128)(2,1)S(1)} %reshape.73), channel_id=1, replica_groups=mesh['cfg'=2,'head'=8,'kv'=32] {'head'}, dimensions={0} | all-to-all | bytes 163840 | tf_op jit(solution)/shard_map/all_to_all | solution.py:33
  34.4 5.6 %reshape.74 = bf16[5120,2,4]{2,1,0:T(2,128)(2,1)S(1)} reshape(bf16[8,2,2560]{2,1,0:T(2,128)(2,1)S(1)} %all_to_all.66) | data formatting | bytes 163840
  40.0 1.8 copy.125
  42.5 1.8 copy.128
  44.4 3.4 reshape.75
  47.7 3.4 all-to-all-start.1
  51.2 1.8 copy.130
  53.0 3.4 reshape.77
  56.4 6.9 %all-to-all-done.1 = bf16[8,2,10240]{2,1,0:T(2,128)(2,1)S(1)} async-done(((bf16[8,2,10240]{2,1,0:T(2,128)(2,1)}), bf16[8,2,10240]{2,1,0:T(2,128)(2,1)S(1)}, u32[]{:S(2)}, u32[]{:S(2)}) %all-to-all-start.1) | async-done | bytes 327712 | tf_op jit(solution)/shard_map/all_to_all | solution.py:35
  63.3 3.6 all-to-all-start.2
  67.5 1.9 reshape.76
  72.1 5.8 %all-to-all-done.2 = bf16[8,2,10240]{2,1,0:T(2,128)(2,1)S(1)} async-done(((bf16[8,2,10240]{2,1,0:T(2,128)(2,1)}), bf16[8,2,10240]{2,1,0:T(2,128)(2,1)S(1)}, u32[]{:S(2)}, u32[]{:S(2)}) %all-to-all-start.2) | async-done | bytes 327712 | tf_op jit(solution)/shard_map/all_to_all | solution.py:36
  77.9 1.9 reshape.78
  82.5 39.1 %all-gather.2.cloned.1.call-done = bf16[16,128,640]{2,0,1:T(8,128)(2,1)} async-done(((bf16[16,4,640]{2,0,1:T(8,128)(2,1)}), bf16[16,128,640]{2,0,1:T(8,128)(2,1)}) %all-gather.2.cloned.1.call-update) | async-done | bytes 2621456 | tf_op jit(solution)/shard_map/all_gather | solution.py:38
  121.6 4.0 copy.127
  125.5 27.7 %while.12 = (s32[]{:T(128)}, f32[4,4,128,5]{2,1,0,3:T(4,128)S(1)}, bf16[4,4,128,5,128]{4,2,3,1,0:T(8,128)(2,1)}, pred[4,4,256]{2,1,0:T(4,128)(4,1)S(1)}, bf16[4,...) while((s32[]{:T(128)}, f32[4,4,128,5]{2,1,0,3:T(4,128)S(1)}, ...), condition=%wide.region_4.5_spmd, body=%wide.region_1.4_spmd.sunk | while | flops 344721920 | bytes 36152512 | solution.py:76
  134.3 1.6 bitcast_reduce_fusion.2
  141.3 1.6 bitcast_reduce_fusion.2
  148.2 1.6 bitcast_reduce_fusion.2
  153.2 3.0 broadcast_select_fusion.1
  156.2 4.3 collective-permute-start
  160.5 26.3 %collective-permute-done = bf16[1,16,64,5,128]{4,2,3,1,0:T(8,128)(2,1)S(1)} collective-permute-done((bf16[1,16,64,5,128]{4,2,3,1,0:T(8,128)(2,1)}, bf16[1,16,64,5,128]{4,2,3,1,0:T(8,128)(2,1)S(1)}, u32[]{:S(2)}, u32[]{:S(2)}) %collective-permute-start) | collective-permute-done | bytes 1310752 | tf_op jit(solution)/shard_map/ppermute | solution.py:17
  187.9 2.7 broadcast_select_fusion.3
  190.6 1.9 collective-permute-start.1
  192.5 26.3 %collective-permute-done.1 = bf16[2,16,32,5,128]{4,2,3,1,0:T(8,128)(2,1)S(1)} collective-permute-done((bf16[2,16,32,5,128]{4,2,3,1,0:T(8,128)(2,1)}, bf16[2,16,32,5,128]{4,2,3,1,0:T(8,128)(2,1)S(1)}, u32[]{:S(2)}, u32[]{:S(2)}) %collective-permute-start.1) | collective-permute-done | bytes 1310752 | tf_op jit(solution)/shard_map/ppermute | solution.py:17
  219.9 2.6 broadcast_select_fusion.5
  222.5 4.5 %collective-permute-start.2 = (bf16[4,16,16,5,128]{4,2,3,1,0:T(8,128)(2,1)}, bf16[4,16,16,5,128]{4,2,3,1,0:T(8,128)(2,1)S(1)}, u32[]{:S(2)}, u32[]{:S(2)}) collective-permute-start(bf16[4,16,16,5,128]{4,2,3,1,0:T(8,128)(2,1)} %get-tuple-element.119), channel_id=1, source_target_pairs={{0,4},{4,0},{1,5},{5,1},{2,6},{6,2},{3,7},{7,3},{8,12},{12,8},{9,1... | collective-permute-start | bytes 3932168 | tf_op jit(solution)/shard_map/ppermute | solution.py:17
  227.0 31.8 %collective-permute-done.2 = bf16[4,16,16,5,128]{4,2,3,1,0:T(8,128)(2,1)S(1)} collective-permute-done((bf16[4,16,16,5,128]{4,2,3,1,0:T(8,128)(2,1)}, bf16[4,16,16,5,128]{4,2,3,1,0:T(8,128)(2,1)S(1)}, u32[]{:S(2)}, u32[]{:S(2)}) %collective-permute-start.2) | collective-permute-done | bytes 1310752 | tf_op jit(solution)/shard_map/ppermute | solution.py:17
  259.9 2.8 broadcast_select_fusion.7
  262.7 27.0 %collective-permute-start.3 = (bf16[8,16,8,5,128]{4,2,3,1,0:T(8,128)(2,1)}, bf16[8,16,8,5,128]{4,2,3,1,0:T(8,128)(2,1)}, u32[]{:S(2)}, u32[]{:S(2)}) collective-permute-start(bf16[8,16,8,5,128]{4,2,3,1,0:T(8,128)(2,1)} %get-tuple-element.117), channel_id=1, source_target_pairs={{0,2},{2,0},{1,3},{3,1},{4,6},{6,4},{5,7},{7,5},{8,10},{10,8},{9,1... | collective-permute-start | bytes 3932168 | tf_op jit(solution)/shard_map/ppermute | solution.py:17
  289.7 56.3 %collective-permute-done.3 = bf16[8,16,8,5,128]{4,2,3,1,0:T(8,128)(2,1)} collective-permute-done((bf16[8,16,8,5,128]{4,2,3,1,0:T(8,128)(2,1)}, bf16[8,16,8,5,128]{4,2,3,1,0:T(8,128)(2,1)}, u32[]{:S(2)}, u32[]{:S(2)}) %collective-permute-start.3) | collective-permute-done | bytes 1310752 | tf_op jit(solution)/shard_map/ppermute | solution.py:17
  346.1 4.1 broadcast_select_fusion.9
  350.2 1.9 collective-permute-start.4
  352.2 1.9 collective-permute-start.5
  354.1 5.5 %collective-permute-done.5 = f32[1,16,64,5]{2,1,3,0:T(8,128)S(1)} collective-permute-done((f32[1,16,64,5]{2,1,3,0:T(8,128)S(1)}, f32[1,16,64,5]{2,1,3,0:T(8,128)S(1)}, u32[]{:S(2)}, u32[]{:S(2)}) %collective-permute-start.5) | collective-permute-done | bytes 20512 | tf_op jit(solution)/shard_map/ppermute | solution.py:17
  359.7 1.9 collective-permute-start.6
  361.6 4.4 collective-permute-done.6
  366.2 4.5 collective-permute-start.7
  370.7 17.6 %collective-permute-done.7 = f32[4,16,16,5]{2,1,3,0:T(8,128)S(1)} collective-permute-done((f32[4,16,16,5]{2,1,3,0:T(8,128)S(1)}, f32[4,16,16,5]{2,1,3,0:T(8,128)S(1)}, u32[]{:S(2)}, u32[]{:S(2)}) %collective-permute-start.7) | collective-permute-done | bytes 20512 | tf_op jit(solution)/shard_map/ppermute | solution.py:17
  388.5 7.6 %collective-permute-start.8 = (f32[8,16,8,5]{2,1,3,0:T(8,128)S(1)}, f32[8,16,8,5]{2,1,3,0:T(8,128)S(1)}, u32[]{:S(2)}, u32[]{:S(2)}) collective-permute-start(f32[8,16,8,5]{2,1,3,0:T(8,128)S(1)} %get-tuple-element.126), channel_id=1, source_target_pairs={{0,2},{2,0},{1,3},{3,1},{4,6},{6,4},{5,7},{7,5},{8,10},{10,8},{9,1... | collective-permute-start | bytes 61448 | tf_op jit(solution)/shard_map/ppermute | solution.py:17
  396.1 12.7 %collective-permute-done.8 = f32[8,16,8,5]{2,1,3,0:T(8,128)S(1)} collective-permute-done((f32[8,16,8,5]{2,1,3,0:T(8,128)S(1)}, f32[8,16,8,5]{2,1,3,0:T(8,128)S(1)}, u32[]{:S(2)}, u32[]{:S(2)}) %collective-permute-start.8) | collective-permute-done | bytes 20512 | tf_op jit(solution)/shard_map/ppermute | solution.py:17
  409.8 2.1 collective-permute-start.9
  412.6 5.2 %collective-permute-done.9 = f32[16,16,4,5]{1,0,3,2:T(8,128)S(1)} collective-permute-done((f32[16,16,4,5]{1,0,3,2:T(8,128)S(1)}, f32[16,16,4,5]{1,0,3,2:T(8,128)S(1)}, u32[]{:S(2)}, u32[]{:S(2)}) %collective-permute-start.9) | collective-permute-done | bytes 20512 | tf_op jit(solution)/shard_map/ppermute | solution.py:17
  418.8 2.8 copy.143
  421.7 5.9 %multiply_reduce_fusion = f32[16,4,5,128]{3,1,2,0:T(4,128)S(1)} fusion(bf16[16,16,4,5,128]{4,2,3,1,0:T(4,128)(2,1)} %collective-permute-done.4, bf16[16,16,4,5,128]{4,2,3,1,0:T(4,128)(2,1)S(1)} %get-tuple-element.114, f32[32,16,4,5]{2,3,1,0:T(8,128)S(1)} %copy.143), kind=kLoop, calls=%fused_computation.30 | loop fusion | flops 5201920 | bytes 2826240 | tf_op jit(solution)/shard_map/reduce_sum | solution.py:24
  427.8 15.8 %all_to_all.67 = bf16[16,4,640]{2,1,0:T(4,128)(2,1)S(1)} all-to-all(bf16[16,4,640]{2,1,0:T(4,128)(2,1)S(1)} %fusion.34), channel_id=1, replica_groups=mesh['cfg'=2,'head'=8,'kv'=32] {'head'}, dimensions={0} | all-to-all | bytes 163840 | tf_op jit(solution)/shard_map/all_to_all | solution.py:95
  (105 shorter events, 36.5 us)
Async XLA Ops:
  6.5 115.0 %all-gather.2.cloned.1.call-start = ((), (), s32[]{:S(2)}) async-start(), calls=%async_computation.4 | async-start | bytes 2703360 | tf_op jit(solution)/shard_map/all_gather | solution.py:38
  34.4 8.1 %copy-start.6 = (bf16[2,16,5120]{2,1,0:T(8,128)(2,1)S(1)}, bf16[2,16,5120]{2,1,0:T(8,128)(2,1)}, u32[]{:S(2)}) copy-start(bf16[2,16,5120]{2,1,0:T(8,128)(2,1)} %param.8) | copy-start | bytes 983044
  42.5 8.7 %copy-start.7 = (bf16[2,16,5120]{2,1,0:T(8,128)(2,1)S(1)}, bf16[2,16,5120]{2,1,0:T(8,128)(2,1)}, u32[]{:S(2)}) copy-start(bf16[2,16,5120]{2,1,0:T(8,128)(2,1)} %param.9) | copy-start | bytes 983044
  47.7 15.6 %all-to-all-start.1 = ((bf16[8,2,10240]{2,1,0:T(2,128)(2,1)}), bf16[8,2,10240]{2,1,0:T(2,128)(2,1)S(1)}, u32[]{:S(2)}, u32[]{:S(2)}) async-start(bf16[8,2,10240]{2,1,0:T(2,128)(2,1)} %reshape.75), calls=%async_computation.1 | async-start | bytes 655360 | tf_op jit(solution)/shard_map/all_to_all | solution.py:35
  51.2 15.8 %copy-start.9 = (s32[16]{0:T(128)S(1)}, s32[16]{0:T(128)}, u32[]{:S(2)}) copy-start(s32[16]{0:T(128)} %param.11) | copy-start | bytes 196
  51.2 15.9 %copy-start.8 = (s32[16,32]{1,0:T(8,128)S(1)}, s32[16,32]{1,0:T(8,128)}, u32[]{:S(2)}) copy-start(s32[16,32]{1,0:T(8,128)} %param.10) | copy-start | bytes 6148
  63.3 14.5 %all-to-all-start.2 = ((bf16[8,2,10240]{2,1,0:T(2,128)(2,1)}), bf16[8,2,10240]{2,1,0:T(2,128)(2,1)S(1)}, u32[]{:S(2)}, u32[]{:S(2)}) async-start(bf16[8,2,10240]{2,1,0:T(2,128)(2,1)} %reshape.77), calls=%async_computation.2 | async-start | bytes 655360 | tf_op jit(solution)/shard_map/all_to_all | solution.py:36
  125.5 1.5 copy-start
  127.4 3.0 copy-start.5
  130.5 2.0 copy-start.1
  132.4 1.5 copy-start
  134.3 3.0 copy-start.5
  137.4 2.0 copy-start.1
  139.4 1.5 copy-start
  141.3 3.0 copy-start.5
  144.3 2.0 copy-start.1
  146.3 1.5 copy-start
  148.2 3.0 copy-start.5
  151.2 2.0 copy-start.1
  156.2 30.6 %collective-permute-start = (bf16[1,16,64,5,128]{4,2,3,1,0:T(8,128)(2,1)}, bf16[1,16,64,5,128]{4,2,3,1,0:T(8,128)(2,1)S(1)}, u32[]{:S(2)}, u32[]{:S(2)}) collective-permute-start(bf16[1,16,64,5,128]{4,2,3,1,0:T(8,128)(2,1)} %get-tuple-element.123), channel_id=1, source_target_pairs={{0,16},{16,0},{1,17},{17,1},{2,18},{18,2},{3,19},{19,3},{4,20},{20... | collective-permute-start | bytes 3932168 | tf_op jit(solution)/shard_map/ppermute | solution.py:17
  186.8 1.1 copy-start.2
  190.6 28.2 %collective-permute-start.1 = (bf16[2,16,32,5,128]{4,2,3,1,0:T(8,128)(2,1)}, bf16[2,16,32,5,128]{4,2,3,1,0:T(8,128)(2,1)S(1)}, u32[]{:S(2)}, u32[]{:S(2)}) collective-permute-start(bf16[2,16,32,5,128]{4,2,3,1,0:T(8,128)(2,1)} %get-tuple-element.121), channel_id=1, source_target_pairs={{0,8},{8,0},{1,9},{9,1},{2,10},{10,2},{3,11},{11,3},{4,12},{12,4},... | collective-permute-start | bytes 3932168 | tf_op jit(solution)/shard_map/ppermute | solution.py:17
  218.8 1.1 copy-start.3
  222.5 36.4 %collective-permute-start.2 = (bf16[4,16,16,5,128]{4,2,3,1,0:T(8,128)(2,1)}, bf16[4,16,16,5,128]{4,2,3,1,0:T(8,128)(2,1)S(1)}, u32[]{:S(2)}, u32[]{:S(2)}) collective-permute-start(bf16[4,16,16,5,128]{4,2,3,1,0:T(8,128)(2,1)} %get-tuple-element.119), channel_id=1, source_target_pairs={{0,4},{4,0},{1,5},{5,1},{2,6},{6,2},{3,7},{7,3},{8,12},{12,8},{9,1... | collective-permute-start | bytes 3932168 | tf_op jit(solution)/shard_map/ppermute | solution.py:17
  258.8 1.1 copy-start.4
  262.7 83.4 %collective-permute-start.3 = (bf16[8,16,8,5,128]{4,2,3,1,0:T(8,128)(2,1)}, bf16[8,16,8,5,128]{4,2,3,1,0:T(8,128)(2,1)}, u32[]{:S(2)}, u32[]{:S(2)}) collective-permute-start(bf16[8,16,8,5,128]{4,2,3,1,0:T(8,128)(2,1)} %get-tuple-element.117), channel_id=1, source_target_pairs={{0,2},{2,0},{1,3},{3,1},{4,6},{6,4},{5,7},{7,5},{8,10},{10,8},{9,1... | collective-permute-start | bytes 3932168 | tf_op jit(solution)/shard_map/ppermute | solution.py:17
  350.2 71.6 %collective-permute-start.4 = (bf16[16,16,4,5,128]{4,2,3,1,0:T(4,128)(2,1)}, bf16[16,16,4,5,128]{4,2,3,1,0:T(4,128)(2,1)}, u32[]{:S(2)}, u32[]{:S(2)}) collective-permute-start(bf16[16,16,4,5,128]{4,2,3,1,0:T(4,128)(2,1)} %get-tuple-element.115), channel_id=1, source_target_pairs={{0,1},{1,0},{2,3},{3,2},{4,5},{5,4},{6,7},{7,6},{8,9},{9,8},{10,11... | collective-permute-start | bytes 3932168 | tf_op jit(solution)/shard_map/ppermute | solution.py:17
  352.2 7.4 %collective-permute-start.5 = (f32[1,16,64,5]{2,1,3,0:T(8,128)S(1)}, f32[1,16,64,5]{2,1,3,0:T(8,128)S(1)}, u32[]{:S(2)}, u32[]{:S(2)}) collective-permute-start(f32[1,16,64,5]{2,1,3,0:T(8,128)S(1)} %get-tuple-element.132), channel_id=1, source_target_pairs={{0,16},{16,0},{1,17},{17,1},{2,18},{18,2},{3,19},{19,3},{4,20},{20... | collective-permute-start | bytes 61448 | tf_op jit(solution)/shard_map/ppermute | solution.py:17
  359.7 6.3 %collective-permute-start.6 = (f32[2,16,32,5]{2,1,3,0:T(8,128)S(1)}, f32[2,16,32,5]{2,1,3,0:T(8,128)S(1)}, u32[]{:S(2)}, u32[]{:S(2)}) collective-permute-start(f32[2,16,32,5]{2,1,3,0:T(8,128)S(1)} %get-tuple-element.130), channel_id=1, source_target_pairs={{0,8},{8,0},{1,9},{9,1},{2,10},{10,2},{3,11},{11,3},{4,12},{12,4},... | collective-permute-start | bytes 61448 | tf_op jit(solution)/shard_map/ppermute | solution.py:17
  366.2 22.1 %collective-permute-start.7 = (f32[4,16,16,5]{2,1,3,0:T(8,128)S(1)}, f32[4,16,16,5]{2,1,3,0:T(8,128)S(1)}, u32[]{:S(2)}, u32[]{:S(2)}) collective-permute-start(f32[4,16,16,5]{2,1,3,0:T(8,128)S(1)} %get-tuple-element.128), channel_id=1, source_target_pairs={{0,4},{4,0},{1,5},{5,1},{2,6},{6,2},{3,7},{7,3},{8,12},{12,8},{9,1... | collective-permute-start | bytes 61448 | tf_op jit(solution)/shard_map/ppermute | solution.py:17
  388.5 20.3 %collective-permute-start.8 = (f32[8,16,8,5]{2,1,3,0:T(8,128)S(1)}, f32[8,16,8,5]{2,1,3,0:T(8,128)S(1)}, u32[]{:S(2)}, u32[]{:S(2)}) collective-permute-start(f32[8,16,8,5]{2,1,3,0:T(8,128)S(1)} %get-tuple-element.126), channel_id=1, source_target_pairs={{0,2},{2,0},{1,3},{3,1},{4,6},{6,4},{5,7},{7,5},{8,10},{10,8},{9,1... | collective-permute-start | bytes 61448 | tf_op jit(solution)/shard_map/ppermute | solution.py:17
  409.8 8.0 %collective-permute-start.9 = (f32[16,16,4,5]{1,0,3,2:T(8,128)S(1)}, f32[16,16,4,5]{1,0,3,2:T(8,128)S(1)}, u32[]{:S(2)}, u32[]{:S(2)}) collective-permute-start(f32[16,16,4,5]{1,0,3,2:T(8,128)S(1)} %copy.137), channel_id=1, source_target_pairs={{0,1},{1,0},{2,3},{3,2},{4,5},{5,4},{6,7},{7,6},{8,9},{9,8},{10,11... | collective-permute-start | bytes 61448 | tf_op jit(solution)/shard_map/ppermute | solution.py:17
Sparse Core Ops, SparseCore 0:
  42.6 78.8 all-gather.1
where the time goes:
time: 452 us; the launch traced here: 451 us
  waiting for transfers between devices  238 us (53%)
  starting transfers between devices  64.8 us (14%)
  local copies, waits for them, and re-layouts  60.3 us (13%)
  blocking collectives  34.5 us (8%)
  other arithmetic  28.8 us (6%)
  between operations  13.8 us (3%)
  matrix products  10.8 us (2%)
    ppermute x10, waiting for transfers between devices, from_partner(): return lax.ppermute(block, axis, route)  186 us
    ppermute x10, starting transfers between devices, from_partner(): return lax.ppermute(block, axis, route)  57.8 us
    all_gather x1, waiting for transfers between devices, local(): query_all = lax.all_gather(query_heads, 'kv', axis=1, tiled=True)  39.1 us
    unnamed x23, local copies, waits for them, and re-layouts  32.2 us
    all_to_all x1, blocking collectives, local(): lax.all_to_all(queries, 'head', split_axis=2, concat_axis=0, tiled=True)  18.7 us
    all_to_all x1, blocking collectives, local(): lax.all_to_all(finished, 'head', split_axis=0, concat_axis=2, tiled=True)  15.8 us
    select_n x5, other arithmetic, local(): keep_out = jnp.where(upper, out_all[:, :, half:], out_all[:, :, :half])  15.1 us
  transfers between devices with their start and end apart: 13, of which 12 were waited for; matrix products, arithmetic and copies ran while one was open for 6% of the time, Pallas kernels for 0%

commit v1 on v0

v1 whole, which is shorter than its diff:
```python
import functools

import jax
import jax.numpy as jnp
from jax import lax
from jax.experimental import pallas as pl
from jax.experimental.pallas import tpu as pltpu
from jax.sharding import Mesh
from jax.sharding import PartitionSpec as P

DH = 128
LOG2E = 1.4426950408889634
CLOSED = -1e30
VMEM_LIMIT = 48 * 1024 * 1024


def pack_kernel(q_ref, k_ref, v_ref, out_ref):
    n_head, _, width = out_ref.shape
    blocks, tokens, _ = k_ref.shape
    qb, qt, _ = q_ref.shape
    queries = jnp.concatenate([q_ref[i].astype(jnp.float32) for i in range(qb)], axis=0)
    queries = queries.astype(jnp.bfloat16)
    for z in range(n_head):
        columns = pl.ds(z * width, width)
        for b in range(blocks):
            out_ref[z, pl.ds(b * tokens, tokens), :] = k_ref[b, :, columns]
            out_ref[z, pl.ds((blocks + b) * tokens, tokens), :] = v_ref[b, :, columns]
        out_ref[z, pl.ds(2 * blocks * tokens, qb * qt), :] = queries[:, z * width : (z + 1) * width]


def attend_kernel(kv_rows, q_ref, kv_ref, bias_ref, out_ref):
    n_x, n_z = kv_ref.shape[0], kv_ref.shape[1]
    rows, width = q_ref.shape
    heads = width // DH
    keys = n_z * kv_rows
    period = bias_ref.shape[0]
    scale = LOG2E / DH**0.5
    lane = lax.broadcasted_iota(jnp.int32, (rows, DH), 1)
    stats = jnp.zeros((rows, DH), jnp.float32)
    for h in range(heads):
        columns = pl.ds(h * DH, DH)
        query = q_ref[:, columns]
        scores = []
        for x in range(n_x):
            key = kv_ref[x, :, pl.ds(0, kv_rows), columns].reshape(keys, DH)
            s = lax.dot_general(query, key, (((1,), (1,)), ((), ())), preferred_element_type=jnp.float32)
            s = s.reshape(rows // period, period, keys) + bias_ref[:, x][None]
            scores.append(s.reshape(rows, keys))
        top = functools.reduce(jnp.maximum, scores)
        top = jnp.max(top, axis=1, keepdims=True)
        total = jnp.zeros((rows, 1), jnp.float32)
        partial = jnp.zeros((rows, DH), jnp.float32)
        for x in range(n_x):
            value = kv_ref[x, :, pl.ds(kv_rows, kv_rows), columns].reshape(keys, DH)
            weight = jnp.exp2((scores[x] - top) * scale)
            total = total + jnp.sum(weight, axis=1, keepdims=True)
            partial = partial + jnp.dot(
                weight.astype(jnp.bfloat16), value, preferred_element_type=jnp.float32
            )
        out_ref[:, columns] = (partial / total).astype(jnp.bfloat16)
        lse = top * (1.0 / DH**0.5) + jnp.log(total)
        high = lse.astype(jnp.bfloat16).astype(jnp.float32)
        rest = lse - high
        middle = rest.astype(jnp.bfloat16).astype(jnp.float32)
        low = rest - middle
        for part, value in enumerate((high, middle, low)):
            stats = jnp.where(lane == h + part * heads, value, stats)
    out_ref[:, pl.ds(width, DH)] = stats.astype(jnp.bfloat16)


def merge_kernel(n_y, heads, part_ref, out_ref):
    n_z = part_ref.shape[0] // n_y
    width = heads * DH
    qb, qt, _ = out_ref.shape
    for z in range(n_z):
        lse = []
        for y in range(n_y):
            stats = part_ref[y * n_z + z, :, pl.ds(width, DH)].astype(jnp.float32)
            lse.append(
                stats[:, :heads] + stats[:, heads : 2 * heads] + stats[:, 2 * heads : 3 * heads]
            )
        top = functools.reduce(jnp.maximum, lse)
        weight = [jnp.exp(item - top) for item in lse]
        norm = functools.reduce(jnp.add, weight)
        for h in range(heads):
            summed = jnp.zeros((qb * qt, DH), jnp.float32)
            for y in range(n_y):
                out = part_ref[y * n_z + z, :, pl.ds(h * DH, DH)].astype(jnp.float32)
                summed = summed + out * weight[y][:, h : h + 1]
            done = summed / norm[:, h : h + 1]
            for i in range(qb):
                out_ref[i, :, pl.ds(z * width + h * DH, DH)] = done[i * qt : (i + 1) * qt].astype(
                    jnp.bfloat16
                )


def call(kernel, out_shape, *args, flops=0):
    vmem = pl.BlockSpec(memory_space=pltpu.VMEM)
    size = sum(a.size * a.dtype.itemsize for a in args)
    size += sum(o.size * o.dtype.itemsize for o in jax.tree.leaves(out_shape))
    return pl.pallas_call(
        kernel,
        out_shape=out_shape,
        in_specs=[vmem] * len(args),
        out_specs=jax.tree.map(lambda _: vmem, out_shape),
        compiler_params=pltpu.CompilerParams(vmem_limit_bytes=VMEM_LIMIT),
        cost_estimate=pl.CostEstimate(flops=flops, bytes_accessed=size, transcendentals=0),
    )(*args)


def local(queries, keys, values, mask_cols, mask_counts):
    n_z, n_x, n_y = lax.axis_size("head"), lax.axis_size("x"), lax.axis_size("y")
    qb, qt, d = queries.shape
    blocks, tokens, _ = keys.shape
    width = d // n_z
    heads = width // DH
    kv_rows = blocks * tokens
    own_rows = qb * qt
    struct = functools.partial(jax.ShapeDtypeStruct, dtype=jnp.bfloat16)

    packed = call(pack_kernel, struct((n_z, 2 * kv_rows + own_rows, width)), queries, keys, values)
    sorted_ = lax.all_to_all(packed, "head", 0, 0)
    query = sorted_[:, 2 * kv_rows :].reshape(n_z * own_rows, width)
    kv = sorted_[:, : 2 * kv_rows]
    query_all = lax.all_to_all(
        jnp.broadcast_to(query[None], (n_y,) + query.shape), "y", 0, 0
    )
    kv_all = lax.all_gather(kv, "x")

    owned = (jnp.arange(n_x)[:, None] * n_y + lax.axis_index("y")) * blocks + jnp.arange(blocks)
    listed = jnp.arange(mask_cols.shape[1])[None, :] < mask_counts[:, None]
    hit = (mask_cols[:, :, None, None] == owned[None, None]) & listed[:, :, None, None]
    allowed = jnp.any(hit, axis=1)
    bias = jnp.where(allowed, 0.0, CLOSED).astype(jnp.float32)
    bias = jnp.broadcast_to(
        bias[:, None, :, None, :, None], (n_z * qb, qt, n_x, n_z, blocks, tokens)
    ).reshape(n_z * own_rows, n_x, n_z * kv_rows)

    rows = n_y * n_z * own_rows
    part = call(
        functools.partial(attend_kernel, kv_rows),
        struct((rows, width + DH)),
        query_all.reshape(rows, width),
        kv_all,
        bias,
        flops=4 * rows * n_x * n_z * kv_rows * width,
    )
    part = lax.all_to_all(
        part.reshape(n_y * n_z, own_rows, width + DH), ("y", "head"), 0, 0
    )
    return call(functools.partial(merge_kernel, n_y, heads), struct((qb, qt, d)), part)


def solution(mesh):
    cfg, head, kv = (mesh.shape[name] for name in ("cfg", "head", "kv"))
    n_x = 4
    fine = Mesh(mesh.devices.reshape(cfg, head, n_x, kv // n_x), ("cfg", "head", "x", "y"))
    token = P(("cfg", "head"), ("x", "y"), None)
    block = P(("cfg", "x", "y"), "head", None)
    return jax.shard_map(
        local,
        mesh=fine,
        in_specs=(token, block, block, P(), P()),
        out_specs=token,
        check_vma=False,
    )
```

time: 452 us -> 133 us (0.29)
  the two profiles are of different devices: /device:TPU:24 before, /device:TPU:16 now
where the time goes in v1:
time: 133 us
  blocking collectives  70.2 us (53%)
  waiting for transfers between devices  24.4 us (18%)
  between operations  13.4 us (10%)
  local copies, waits for them, and re-layouts  9.9 us (7%)
  starting transfers between devices  7.43 us (6%)
  Pallas kernels  6.91 us (5%)
    all_to_all x1, blocking collectives, local(): lax.all_to_all(part.reshape(n_y * n_z, own_rows, width + DH), ('y', 'head...  38 us
    all_to_all x1, blocking collectives, local(): sorted_ = lax.all_to_all(packed, 'head', 0, 0)  32.2 us
    all_gather x1, waiting for transfers between devices, local(): kv_all = lax.all_gather(kv, 'x')  13.1 us
    all_to_all x1, waiting for transfers between devices, local(): lax.all_to_all(jnp.broadcast_to(query[None], (n_y,) + query.shape), 'y',...  11.3 us
    all_to_all x1, starting transfers between devices, local(): lax.all_to_all(jnp.broadcast_to(query[None], (n_y,) + query.shape), 'y',...  7.43 us
    pallas_call x3, Pallas kernels, call(): pl.pallas_call(kernel, out_shape=out_shape, in_specs=[vmem] * len(args),...  6.91 us
    unnamed x12, local copies, waits for them, and re-layouts  4.58 us
    reshape x1, local copies, waits for them, and re-layouts, local(): bias = jnp.broadcast_to(bias[:, None, :, None, :, None], (n_z * qb, qt, n...  2.77 us
  transfers between devices with their start and end apart: 2, of which 2 were waited for; matrix products, arithmetic and copies ran while one was open for 4% of the time, Pallas kernels for 0%

profile of v1, /device:TPU:16, one launch (start us, length us, event | category | flops | bytes accessed | tf_op | source)
XLA Modules:
  0.0 132.7 jit_solution(298799724992235592)
XLA Ops:
  6.5 0.0 all-gather.3.cloned.1.call-start
  6.5 0.0 copy-start
  6.5 1.0 copy-done
  7.5 0.0 copy-start.1
  7.5 1.0 copy-done.1
  8.5 0.0 copy-start.2
  8.5 0.9 copy-done.2
  9.4 0.1 shard_map.55
  9.4 0.0 copy-start.5
  9.4 0.0 copy-start.4
  9.5 32.2 %all_to_all.15 = bf16[8,72,640]{2,1,0:T(8,128)(2,1)S(1)} all-to-all(bf16[8,72,640]{2,1,0:T(8,128)(2,1)S(1)} %shard_map.55), channel_id=1, replica_groups=mesh['cfg'=2,'head'=8,'x'=4,'y'=8] {'head'}, dimensions={0} | all-to-all | bytes 1474560 | tf_op jit(solution)/shard_map/all_to_all | solution.py:122
  41.6 0.9 slice.9
  42.5 0.0 all-gather.3.cloned.1.call-update
  42.6 0.9 broadcast_in_dim.15
  43.5 7.4 %all-to-all-start.1 = ((bf16[8,64,640]{2,1,0:T(8,128)(2,1)}), bf16[8,64,640]{2,1,0:T(8,128)(2,1)S(1)}, u32[]{:S(2)}, u32[]{:S(2)}) async-start(bf16[8,64,640]{2,1,0:T(8,128)(2,1)} %broadcast_in_dim.15), calls=%async_computation.1 | async-start | bytes 1310720 | tf_op jit(solution)/shard_map/all_to_all | solution.py:125
  50.9 0.1 iota_add_fusion
  51.0 0.0 copy-done.5
  51.0 0.1 iota_compare_fusion
  51.1 0.0 copy-done.4
  51.1 0.3 and_reduce_fusion
  51.4 0.1 copy.6
  51.5 0.6 broadcast_in_dim.32
  52.1 2.8 %reshape.64.bias_ref = f32[64,4,256]{2,1,0:T(4,128)S(1)} reshape(f32[16,4,4,8,2,16]{5,4,3,2,1,0:T(2,128)S(1)} %broadcast_in_dim.32) | data formatting | bytes 524288 | tf_op jit(solution)/shard_map/reshape | solution.py:137
  54.9 11.3 %all-to-all-done.1 = bf16[8,64,640]{2,1,0:T(8,128)(2,1)S(1)} async-done(((bf16[8,64,640]{2,1,0:T(8,128)(2,1)}), bf16[8,64,640]{2,1,0:T(8,128)(2,1)S(1)}, u32[]{:S(2)}, u32[]{:S(2)}) %all-to-all-start.1) | async-done | bytes 655392 | tf_op jit(solution)/shard_map/all_to_all | solution.py:125
  66.2 13.1 %all-gather.3.cloned.1.call-done = bf16[32,64,640]{2,1,0:T(8,128)(2,1)} async-done(((bf16[8,64,640]{2,1,0:T(8,128)(2,1)}), bf16[32,64,640]{2,1,0:T(8,128)(2,1)}) %all-gather.3.cloned.1.call-update) | async-done | bytes 2621456 | tf_op jit(solution)/shard_map/all_gather | solution.py:128
  79.2 0.0 copy-start.3
  79.2 1.7 %copy-done.3 = bf16[32,64,640]{2,1,0:T(8,128)(2,1)S(1)} copy-done((bf16[32,64,640]{2,1,0:T(8,128)(2,1)S(1)}, bf16[32,64,640]{2,1,0:T(8,128)(2,1)}, u32[]{:S(2)}) %copy-start.3) | copy-done | bytes 2621464
  81.0 4.9 %shard_map.56 = bf16[512,768]{1,0:T(8,128)(2,1)S(1)} custom-call(bf16[512,640]{1,0:T(8,128)(2,1)S(1)} %bitcast.6, bf16[4,8,64,640]{3,2,1,0:T(8,128)(2,1)S(1)} %bitcast.7, f32[64,4,256]{2,1,0:T(4,128)S(1)} %reshape.64.bias_ref), custom_call_target="tpu_custom_call" | custom-call | flops 1342177280 | bytes 4325376 | tf_op jit(solution)/shard_map/pallas_call | solution.py:101
  85.9 38.0 %all_to_all.16.part_ref = bf16[64,8,768]{2,1,0:T(8,128)(2,1)S(1)} all-to-all(bf16[64,8,768]{2,1,0:T(8,128)(2,1)S(1)} %bitcast.5), channel_id=1, replica_groups=mesh['cfg'=2,'head'=8,'x'=4,'y'=8] {'y','head'}, dimensions={0} | all-to-all | bytes 1572864 | tf_op jit(solution)/shard_map/all_to_all | solution.py:148
  123.9 2.0 %shard_map.57 = bf16[2,4,5120]{2,1,0:T(4,128)(2,1)} custom-call(bf16[64,8,768]{2,1,0:T(8,128)(2,1)S(1)} %all_to_all.16.part_ref), custom_call_target="tpu_custom_call" | custom-call | bytes 868352 | tf_op jit(solution)/shard_map/pallas_call | solution.py:101
  (3 shorter events, 0.0 us)
Async XLA Ops:
  6.5 72.7 %all-gather.3.cloned.1.call-start = ((), (), s32[]{:S(2)}) async-start(), calls=%async_computation.3 | async-start | bytes 3276800 | tf_op jit(solution)/shard_map/all_gather | solution.py:128
  6.5 1.0 copy-start
  7.5 1.0 copy-start.1
  8.5 0.9 copy-start.2
  9.4 41.6 %copy-start.5 = (s32[16]{0:T(128)S(1)}, s32[16]{0:T(128)}, u32[]{:S(2)}) copy-start(s32[16]{0:T(128)} %param.9) | copy-start | bytes 196
  9.4 41.6 %copy-start.4 = (s32[16,32]{1,0:T(8,128)S(1)}, s32[16,32]{1,0:T(8,128)}, u32[]{:S(2)}) copy-start(s32[16,32]{1,0:T(8,128)} %param.8) | copy-start | bytes 6148
  43.5 22.7 %all-to-all-start.1 = ((bf16[8,64,640]{2,1,0:T(8,128)(2,1)}), bf16[8,64,640]{2,1,0:T(8,128)(2,1)S(1)}, u32[]{:S(2)}, u32[]{:S(2)}) async-start(bf16[8,64,640]{2,1,0:T(8,128)(2,1)} %broadcast_in_dim.15), calls=%async_computation.1 | async-start | bytes 1310720 | tf_op jit(solution)/shard_map/all_to_all | solution.py:125
  79.2 1.7 %copy-start.3 = (bf16[32,64,640]{2,1,0:T(8,128)(2,1)S(1)}, bf16[32,64,640]{2,1,0:T(8,128)(2,1)}, u32[]{:S(2)}) copy-start(bf16[32,64,640]{2,1,0:T(8,128)(2,1)} %all-gather.3.cloned.1.call-done) | copy-start | bytes 7864324
Sparse Core Ops, SparseCore 0:
  42.7 36.5 all-gather.2

commit v2 on v1

v2 whole, which is shorter than its diff:
```python
import functools

import jax
import jax.numpy as jnp
from jax import lax
from jax.experimental import pallas as pl
from jax.experimental.pallas import tpu as pltpu
from jax.sharding import Mesh
from jax.sharding import PartitionSpec as P

DH = 128
LOG2E = 1.4426950408889634
CLOSED = -1e30
VMEM_LIMIT = 40 * 1024 * 1024
STAT_ROWS = 16
BF = jnp.bfloat16
F32 = jnp.float32


def pack_kernel(q_hbm, k_hbm, v_hbm, out_ref, q_ref, k_ref, v_ref, sems):
    copies = [
        pltpu.make_async_copy(k_hbm, k_ref, sems.at[0]),
        pltpu.make_async_copy(v_hbm, v_ref, sems.at[1]),
        pltpu.make_async_copy(q_hbm, q_ref, sems.at[2]),
    ]
    for copy in copies:
        copy.start()
    n_z, heads = out_ref.shape[:2]
    blocks, tokens, _ = k_ref.shape
    qb, qt, _ = q_ref.shape
    for part, ref in enumerate((k_ref, v_ref)):
        copies[part].wait()
        for z in range(n_z):
            for h in range(heads):
                columns = pl.ds((z * heads + h) * DH, DH)
                for b in range(blocks):
                    rows = pl.ds((part * blocks + b) * tokens, tokens)
                    out_ref[z, h, rows, :] = ref[b, :, columns]
    copies[2].wait()
    queries = jnp.concatenate([q_ref[i].astype(F32) for i in range(qb)], axis=0).astype(BF)
    for z in range(n_z):
        for h in range(heads):
            first = (z * heads + h) * DH
            out_ref[z, h, pl.ds(2 * blocks * tokens, qb * qt), :] = queries[:, first : first + DH]


def unpack_kernel(kv_rows, sorted_ref, k_ref, v_ref, q_ref):
    n_z, heads, rows, _ = sorted_ref.shape
    own = rows - 2 * kv_rows
    for h in range(heads):
        for z in range(n_z):
            k_ref[h, pl.ds(z * kv_rows, kv_rows), :] = sorted_ref[z, h, pl.ds(0, kv_rows), :]
            v_ref[h, pl.ds(z * kv_rows, kv_rows), :] = sorted_ref[z, h, pl.ds(kv_rows, kv_rows), :]
        query = jnp.concatenate(
            [sorted_ref[z, h, pl.ds(2 * kv_rows, own), :].astype(F32) for z in range(n_z)], axis=0
        ).astype(BF)
        for y in range(q_ref.shape[0]):
            q_ref[y, h] = query


def attend_kernel(kv_rows, tokens, base, pieces, first, last, *refs):
    refs = list(refs)
    q_ref, bias_ref = refs[:2]
    kv = [refs[2 + 2 * i : 4 + 2 * i] for i in range(pieces)]
    rest = refs[2 + 2 * pieces :]
    if not first:
        top_in, total_in, acc_in = rest[:3]
        rest = rest[3:]
    n_to, heads, period, _ = q_ref.shape
    rows, keys = n_to * period, kv[0][0].shape[1]
    scale = LOG2E / DH**0.5
    lane = lax.broadcasted_iota(jnp.int32, (rows, DH), 1)
    blocks = kv_rows // tokens
    block = lax.broadcasted_iota(jnp.int32, (period, keys), 1) // tokens % blocks
    bias = []
    for i in range(pieces):
        place = (base + i) * blocks
        item = jnp.broadcast_to(bias_ref[:, place : place + 1], (period, keys))
        for b in range(1, blocks):
            item = jnp.where(block == b, bias_ref[:, place + b : place + b + 1], item)
        bias.append(item)
    tops = jnp.zeros((rows, DH), F32)
    totals = jnp.ones((rows, DH), F32)
    for h in range(heads):
        query = q_ref[:, h].reshape(rows, DH)
        scores = []
        for i in range(pieces):
            s = lax.dot_general(
                query, kv[i][0][h], (((1,), (1,)), ((), ())), preferred_element_type=F32
            )
            s = s.reshape(n_to, period, keys) + bias[i][None]
            scores.append(s.reshape(rows, keys))
        top = jnp.max(functools.reduce(jnp.maximum, scores), axis=1, keepdims=True)
        sums = jnp.zeros((rows, keys), F32)
        partial = jnp.zeros((rows, DH), F32)
        if not first:
            before = top_in[:, h : h + 1]
            top = jnp.maximum(top, before)
            fade = jnp.exp2((before - top) * scale)
            partial = acc_in[h] * fade
        for i in range(pieces):
            weight = jnp.exp2((scores[i] - top) * scale)
            sums = sums + weight
            partial = partial + jnp.dot(weight.astype(BF), kv[i][1][h], preferred_element_type=F32)
        total = jnp.sum(sums, axis=1, keepdims=True)
        if not first:
            total = total + total_in[:, h : h + 1] * fade
        tops = jnp.where(lane == h, top, tops)
        totals = jnp.where(lane == h, total, totals)
        if not last:
            rest[2][h] = partial
            continue
        out = (partial / total).astype(BF)
        for to in range(n_to):
            rest[0][to, pl.ds(h * period, period), :] = out[to * period : (to + 1) * period]
    if not last:
        rest[0][...] = tops
        rest[1][...] = totals
        return
    out_ref = rest[0]
    lse = tops * (1.0 / DH**0.5) + jnp.log(totals)
    high = lse.astype(BF).astype(F32)
    rest = lse - high
    middle = rest.astype(BF).astype(F32)
    stats = high + pltpu.roll(middle, heads, 1) + pltpu.roll(rest - middle, 2 * heads, 1)
    turned = stats.T[:STAT_ROWS]
    per = DH // period
    for to in range(n_to):
        item = turned[:, to // per * DH : (to // per + 1) * DH]
        if to % per:
            item = pltpu.roll(item, DH - to % per * period, 1)
        out_ref[to, pl.ds(heads * period, STAT_ROWS), :] = item.astype(BF)


def merge_kernel(heads, part_ref, out_ref):
    n_from = part_ref.shape[0]
    n_z, own, _ = out_ref.shape
    rows = n_z * own
    stats = jnp.concatenate(
        [part_ref[y, pl.ds(heads * rows, STAT_ROWS), :].astype(F32) for y in range(n_from)], axis=0
    ).T[:rows]
    lse = stats + pltpu.roll(stats, DH - heads, 1) + pltpu.roll(stats, DH - 2 * heads, 1)
    top = lse
    for step in (STAT_ROWS, 2 * STAT_ROWS, 4 * STAT_ROWS):
        top = jnp.maximum(top, pltpu.roll(top, step, 1))
    weight = jnp.exp(lse - top)
    norm = weight
    for step in (STAT_ROWS, 2 * STAT_ROWS, 4 * STAT_ROWS):
        norm = norm + pltpu.roll(norm, step, 1)
    weight = weight / norm
    for h in range(heads):
        summed = jnp.zeros((rows, DH), F32)
        for y in range(n_from):
            place = y * STAT_ROWS + h
            out = part_ref[y, pl.ds(h * rows, rows), :].astype(F32)
            summed = summed + out * weight[:, place : place + 1]
        done = summed.astype(BF)
        for z in range(n_z):
            out_ref[z, :, pl.ds(h * DH, DH)] = done[z * own : (z + 1) * own]


def finish_kernel(in_ref, out_ref):
    n_z, _, width = in_ref.shape
    qb, qt, _ = out_ref.shape
    for z in range(n_z):
        rows = in_ref[z].astype(F32)
        for i in range(qb):
            out_ref[i, :, pl.ds(z * width, width)] = rows[i * qt : (i + 1) * qt].astype(BF)


def call(kernel, out_shape, *args, flops=0, scratch=(), space=pltpu.VMEM, vmem=VMEM_LIMIT):
    whole = pl.BlockSpec(memory_space=pltpu.VMEM)
    size = sum(a.size * a.dtype.itemsize for a in args)
    size += sum(o.size * o.dtype.itemsize for o in jax.tree.leaves(out_shape))
    return pl.pallas_call(
        kernel,
        out_shape=out_shape,
        in_specs=[pl.BlockSpec(memory_space=space)] * len(args),
        out_specs=jax.tree.map(lambda _: whole, out_shape),
        scratch_shapes=list(scratch),
        compiler_params=pltpu.CompilerParams(vmem_limit_bytes=vmem),
        cost_estimate=pl.CostEstimate(flops=flops, bytes_accessed=size, transcendentals=0),
    )(*args)


def shift(block, axis, by):
    count = lax.axis_size(axis)
    return lax.ppermute(block, axis, [(i, (i + by) % count) for i in range(count)])


def local(queries, keys, values, mask_cols, mask_counts):
    n_z, n_x, n_y = lax.axis_size("head"), lax.axis_size("x"), lax.axis_size("y")
    qb, qt, d = queries.shape
    blocks, tokens, _ = keys.shape
    heads = d // n_z // DH
    kv_rows = blocks * tokens
    own = qb * qt
    period = n_z * own
    rows = n_y * period
    n_keys = n_z * kv_rows
    struct = jax.ShapeDtypeStruct

    packed = call(
        pack_kernel,
        struct((n_z, heads, 2 * kv_rows + own, DH), BF),
        queries,
        keys,
        values,
        scratch=[
            pltpu.VMEM(queries.shape, BF),
            pltpu.VMEM(keys.shape, BF),
            pltpu.VMEM(values.shape, BF),
            pltpu.SemaphoreType.DMA((3,)),
        ],
        space=pltpu.HBM, vmem=62 * 1024 * 1024,
    )
    sorted_ = lax.all_to_all(packed, "head", 0, 0)
    key, value, query = call(
        functools.partial(unpack_kernel, kv_rows),
        (
            struct((heads, n_keys, DH), BF),
            struct((heads, n_keys, DH), BF),
            struct((n_y, heads, period, DH), BF),
        ),
        sorted_,
    )

    key_left = shift(key, "x", 1)
    value_right = shift(value, "x", -1)
    query_all = lax.all_to_all(query, "y", 0, 0)
    key_right = shift(key, "x", -1)
    value_left = shift(value, "x", 1)
    key_far = shift(key_left, "x", 1)
    value_far = shift(value_right, "x", -1)

    x = lax.axis_index("x")
    places = jnp.stack([x, (x + n_x - 1) % n_x, (x + 1) % n_x, (x + 2) % n_x])
    owned = (places[:, None] * n_y + lax.axis_index("y")) * blocks + jnp.arange(blocks)
    owned = owned.reshape(-1)
    listed = jnp.arange(mask_cols.shape[1])[None, :] < mask_counts[:, None]
    hit = (mask_cols[:, :, None] == owned) & listed[:, :, None]
    bias = jnp.where(jnp.any(hit, axis=1), 0.0, CLOSED).astype(F32)
    bias = jnp.repeat(bias, qt, axis=0)

    flops = 4 * rows * n_keys * heads * DH
    part = call(
        functools.partial(attend_kernel, kv_rows, tokens, 0, 4, True, True),
        struct((n_y, heads * period + STAT_ROWS, DH), BF),
        query_all,
        bias,
        key,
        value,
        key_left,
        value_left,
        key_right,
        value_right,
        key_far,
        value_far,
        flops=4 * flops,
    )
    part = lax.all_to_all(part, "y", 0, 0)
    merged = call(
        functools.partial(merge_kernel, heads), struct((n_z, own, heads * DH), BF), part
    )
    merged = lax.all_to_all(merged, "head", 0, 0)
    return call(finish_kernel, struct((qb, qt, d), BF), merged)


def solution(mesh):
    cfg, head, kv = (mesh.shape[name] for name in ("cfg", "head", "kv"))
    n_x = 4
    fine = Mesh(mesh.devices.reshape(cfg, head, n_x, kv // n_x), ("cfg", "head", "x", "y"))
    token = P(("cfg", "head"), ("x", "y"), None)
    block = P(("cfg", "x", "y"), "head", None)
    return jax.shard_map(
        local,
        mesh=fine,
        in_specs=(token, block, block, P(), P()),
        out_specs=token,
        check_vma=False,
    )
```

time: 133 us -> 113 us (0.85)
  the two profiles are of different devices: /device:TPU:16 before, /device:TPU:2 now
where the time goes in v2:
time: 113 us
  blocking collectives  70 us (62%)
  starting transfers between devices  24.6 us (22%)
  Pallas kernels  9.08 us (8%)
  waiting for transfers between devices  7.6 us (7%)
    all_to_all x1, blocking collectives, local(): sorted_ = lax.all_to_all(packed, 'head', 0, 0)  32.4 us
    all_to_all x1, blocking collectives, local(): part = lax.all_to_all(part, 'y', 0, 0)  25.3 us
    ppermute x6, starting transfers between devices, shift(): lax.ppermute(block, axis, [(i, (i + by) % count) for i in range(count)])  17.5 us
    all_to_all x1, blocking collectives, local(): merged = lax.all_to_all(merged, 'head', 0, 0)  12.3 us
    pallas_call x5, Pallas kernels, call(): pl.pallas_call(kernel, out_shape=out_shape, in_specs=[pl.BlockSpec(memory...  9.08 us
    ppermute x6, waiting for transfers between devices, shift(): lax.ppermute(block, axis, [(i, (i + by) % count) for i in range(count)])  7.6 us
    all_to_all x1, starting transfers between devices, local(): query_all = lax.all_to_all(query, 'y', 0, 0)  7.1 us
  transfers between devices with their start and end apart: 7, of which 4 were waited for; matrix products, arithmetic and copies ran while one was open for 1% of the time, Pallas kernels for 0%

profile of v2, /device:TPU:2, one launch (start us, length us, event | category | flops | bytes accessed | tf_op | source)
XLA Modules:
  0.0 112.7 jit_solution(6424493215548642171)
XLA Ops:
  0.0 2.1 %shard_map.55 = bf16[8,5,72,128]{3,2,1,0:T(8,128)(2,1)} custom-call(bf16[2,4,5120]{2,1,0:T(4,128)(2,1)} %q_hbm.1, bf16[2,16,5120]{2,1,0:T(8,128)(2,1)} %k_hbm.1, bf16[2,16,5120]{2,1,0:T(8,128)(2,1)} %v_hbm.1), custom_call_target="tpu_custom_call" | custom-call | bytes 1474560 | tf_op jit(solution)/shard_map/pallas_call | solution.py:175
  2.1 32.4 %all_to_all.20.sorted_ref = bf16[8,5,72,128]{3,2,1,0:T(8,128)(2,1)S(1)} all-to-all(bf16[8,5,72,128]{3,2,1,0:T(8,128)(2,1)} %shard_map.55), channel_id=1, replica_groups=mesh['cfg'=2,'head'=8,'x'=4,'y'=8] {'head'}, dimensions={0} | all-to-all | bytes 1474560 | tf_op jit(solution)/shard_map/all_to_all | solution.py:217
  34.4 1.0 shard_map.56
  35.4 7.1 %all-to-all-start.1 = ((bf16[8,5,64,128]{3,2,1,0:T(8,128)(2,1)}), bf16[8,5,64,128]{3,2,1,0:T(8,128)(2,1)S(1)}, u32[]{:S(2)}, u32[]{:S(2)}) async-start(bf16[8,5,64,128]{3,2,1,0:T(8,128)(2,1)} %get-tuple-element.8), calls=%async_computation.1 | async-start | bytes 1310720 | tf_op jit(solution)/shard_map/all_to_all | solution.py:230
  42.5 0.0 copy-start
  42.5 0.1 fusion.1
  42.6 3.4 %collective-permute-start = (bf16[5,256,128]{2,1,0:T(8,128)(2,1)S(1)}, bf16[5,256,128]{2,1,0:T(8,128)(2,1)S(1)}, u32[]{:S(2)}, u32[]{:S(2)}) collective-permute-start(bf16[5,256,128]{2,1,0:T(8,128)(2,1)S(1)} %get-tuple-element.9.refs_2_), channel_id=1, source_target_pairs={{0,8},{8,16},{16,24},{24,0},{1,9},{9,17},{17,25},{25,1},{2,10},{10... | collective-permute-start | bytes 983048 | tf_op jit(solution)/shard_map/ppermute | solution.py:188
  46.0 2.4 %collective-permute-start.3 = (bf16[5,256,128]{2,1,0:T(8,128)(2,1)S(1)}, bf16[5,256,128]{2,1,0:T(8,128)(2,1)S(1)}, u32[]{:S(2)}, u32[]{:S(2)}) collective-permute-start(bf16[5,256,128]{2,1,0:T(8,128)(2,1)S(1)} %get-tuple-element.10.refs_3_), channel_id=1, source_target_pairs={{0,24},{8,0},{16,8},{24,16},{1,25},{9,1},{17,9},{25,17},{2,26},{10... | collective-permute-start | bytes 983048 | tf_op jit(solution)/shard_map/ppermute | solution.py:188
  48.4 0.1 iota_add_fusion
  48.5 0.0 copy-start.1
  48.5 0.1 add.61
  48.6 0.6 copy-done.1
  49.2 0.1 iota_compare_fusion
  49.2 3.6 %collective-permute-start.2 = (bf16[5,256,128]{2,1,0:T(8,128)(2,1)S(1)}, bf16[5,256,128]{2,1,0:T(8,128)(2,1)S(1)}, u32[]{:S(2)}, u32[]{:S(2)}) collective-permute-start(bf16[5,256,128]{2,1,0:T(8,128)(2,1)S(1)} %get-tuple-element.9.refs_2_), channel_id=1, source_target_pairs={{0,24},{8,0},{16,8},{24,16},{1,25},{9,1},{17,9},{25,17},{2,26},{10... | collective-permute-start | bytes 983048 | tf_op jit(solution)/shard_map/ppermute | solution.py:188
  52.9 2.2 %collective-permute-start.1 = (bf16[5,256,128]{2,1,0:T(8,128)(2,1)S(1)}, bf16[5,256,128]{2,1,0:T(8,128)(2,1)S(1)}, u32[]{:S(2)}, u32[]{:S(2)}) collective-permute-start(bf16[5,256,128]{2,1,0:T(8,128)(2,1)S(1)} %get-tuple-element.10.refs_3_), channel_id=1, source_target_pairs={{0,8},{8,16},{16,24},{24,0},{1,9},{9,17},{17,25},{25,1},{2,10},{10... | collective-permute-start | bytes 983048 | tf_op jit(solution)/shard_map/ppermute | solution.py:188
  55.1 0.0 collective-permute-done.refs_4_
  55.1 3.4 %collective-permute-start.4 = (bf16[5,256,128]{2,1,0:T(8,128)(2,1)S(1)}, bf16[5,256,128]{2,1,0:T(8,128)(2,1)S(1)}, u32[]{:S(2)}, u32[]{:S(2)}) collective-permute-start(bf16[5,256,128]{2,1,0:T(8,128)(2,1)S(1)} %collective-permute-done.refs_4_), channel_id=1, source_target_pairs={{0,8},{8,16},{16,24},{24,0},{1,9},{9,17},{17,25},{25,1},{2,10},{10... | collective-permute-start | bytes 983048 | tf_op jit(solution)/shard_map/ppermute | solution.py:188
  58.5 0.0 collective-permute-done.3.refs_7_
  58.5 2.4 %collective-permute-start.5 = (bf16[5,256,128]{2,1,0:T(8,128)(2,1)S(1)}, bf16[5,256,128]{2,1,0:T(8,128)(2,1)S(1)}, u32[]{:S(2)}, u32[]{:S(2)}) collective-permute-start(bf16[5,256,128]{2,1,0:T(8,128)(2,1)S(1)} %collective-permute-done.3.refs_7_), channel_id=1, source_target_pairs={{0,24},{8,0},{16,8},{24,16},{1,25},{9,1},{17,9},{25,17},{2,26},{10... | collective-permute-start | bytes 983048 | tf_op jit(solution)/shard_map/ppermute | solution.py:188
  61.0 0.0 copy-done
  61.0 0.4 and_reduce_fusion
  61.4 2.5 %collective-permute-done.2.refs_6_ = bf16[5,256,128]{2,1,0:T(8,128)(2,1)S(1)} collective-permute-done((bf16[5,256,128]{2,1,0:T(8,128)(2,1)S(1)}, bf16[5,256,128]{2,1,0:T(8,128)(2,1)S(1)}, u32[]{:S(2)}, u32[]{:S(2)}) %collective-permute-start.2) | collective-permute-done | bytes 327712 | tf_op jit(solution)/shard_map/ppermute | solution.py:188
  63.9 0.9 collective-permute-done.1.refs_5_
  64.8 3.5 %collective-permute-done.4.refs_8_ = bf16[5,256,128]{2,1,0:T(8,128)(2,1)S(1)} collective-permute-done((bf16[5,256,128]{2,1,0:T(8,128)(2,1)S(1)}, bf16[5,256,128]{2,1,0:T(8,128)(2,1)S(1)}, u32[]{:S(2)}, u32[]{:S(2)}) %collective-permute-start.4) | collective-permute-done | bytes 327712 | tf_op jit(solution)/shard_map/ppermute | solution.py:188
  68.3 0.7 collective-permute-done.5.refs_9_
  69.0 0.0 all-to-all-done.1.refs_0_
  69.0 4.3 %shard_map.57 = bf16[8,336,128]{2,1,0:T(8,128)(2,1)S(1)} custom-call(bf16[8,5,64,128]{3,2,1,0:T(8,128)(2,1)S(1)} %all-to-all-done.1.refs_0_, f32[64,8]{1,0:T(8,128)S(1)} %bitcast.5, bf16[5,256,128]{2,1,0:T(8,128)(2,1)S(1)} %get-tuple-element.9.refs_2_, bf16[5,256,128]{2,1,0:T(8,128)(2,1)S(1)} %get-tuple-element.10.refs_3_, ...), custom_call_target="tpu_custom_call" | custom-call | flops 1342177280 | bytes 3966976 | tf_op jit(solution)/shard_map/pallas_call | solution.py:175
  73.3 25.3 %all_to_all.21.part_ref = bf16[8,336,128]{2,1,0:T(8,128)(2,1)S(1)} all-to-all(bf16[8,336,128]{2,1,0:T(8,128)(2,1)S(1)} %shard_map.57), channel_id=1, replica_groups=mesh['cfg'=2,'head'=8,'x'=4,'y'=8] {'y'}, dimensions={0} | all-to-all | bytes 1376256 | tf_op jit(solution)/shard_map/all_to_all | solution.py:261
  98.6 1.1 shard_map.58
  99.7 12.3 %all_to_all.22.in_ref = bf16[8,8,640]{2,1,0:T(8,128)(2,1)S(1)} all-to-all(bf16[8,8,640]{2,1,0:T(8,128)(2,1)S(1)} %shard_map.58), channel_id=1, replica_groups=mesh['cfg'=2,'head'=8,'x'=4,'y'=8] {'head'}, dimensions={0} | all-to-all | bytes 163840 | tf_op jit(solution)/shard_map/all_to_all | solution.py:265
  112.0 0.6 shard_map.59
  (2 shorter events, 0.0 us)
Async XLA Ops:
  35.4 33.6 %all-to-all-start.1 = ((bf16[8,5,64,128]{3,2,1,0:T(8,128)(2,1)}), bf16[8,5,64,128]{3,2,1,0:T(8,128)(2,1)S(1)}, u32[]{:S(2)}, u32[]{:S(2)}) async-start(bf16[8,5,64,128]{3,2,1,0:T(8,128)(2,1)} %get-tuple-element.8), calls=%async_computation.1 | async-start | bytes 1310720 | tf_op jit(solution)/shard_map/all_to_all | solution.py:230
  42.5 18.5 %copy-start = (s32[16,32]{1,0:T(8,128)S(1)}, s32[16,32]{1,0:T(8,128)}, u32[]{:S(2)}) copy-start(s32[16,32]{1,0:T(8,128)} %param.8) | copy-start | bytes 6148
  42.6 12.5 %collective-permute-start = (bf16[5,256,128]{2,1,0:T(8,128)(2,1)S(1)}, bf16[5,256,128]{2,1,0:T(8,128)(2,1)S(1)}, u32[]{:S(2)}, u32[]{:S(2)}) collective-permute-start(bf16[5,256,128]{2,1,0:T(8,128)(2,1)S(1)} %get-tuple-element.9.refs_2_), channel_id=1, source_target_pairs={{0,8},{8,16},{16,24},{24,0},{1,9},{9,17},{17,25},{25,1},{2,10},{10... | collective-permute-start | bytes 983048 | tf_op jit(solution)/shard_map/ppermute | solution.py:188
  46.0 12.5 %collective-permute-start.3 = (bf16[5,256,128]{2,1,0:T(8,128)(2,1)S(1)}, bf16[5,256,128]{2,1,0:T(8,128)(2,1)S(1)}, u32[]{:S(2)}, u32[]{:S(2)}) collective-permute-start(bf16[5,256,128]{2,1,0:T(8,128)(2,1)S(1)} %get-tuple-element.10.refs_3_), channel_id=1, source_target_pairs={{0,24},{8,0},{16,8},{24,16},{1,25},{9,1},{17,9},{25,17},{2,26},{10... | collective-permute-start | bytes 983048 | tf_op jit(solution)/shard_map/ppermute | solution.py:188
  48.5 0.7 copy-start.1
  49.2 14.6 %collective-permute-start.2 = (bf16[5,256,128]{2,1,0:T(8,128)(2,1)S(1)}, bf16[5,256,128]{2,1,0:T(8,128)(2,1)S(1)}, u32[]{:S(2)}, u32[]{:S(2)}) collective-permute-start(bf16[5,256,128]{2,1,0:T(8,128)(2,1)S(1)} %get-tuple-element.9.refs_2_), channel_id=1, source_target_pairs={{0,24},{8,0},{16,8},{24,16},{1,25},{9,1},{17,9},{25,17},{2,26},{10... | collective-permute-start | bytes 983048 | tf_op jit(solution)/shard_map/ppermute | solution.py:188
  52.9 11.9 %collective-permute-start.1 = (bf16[5,256,128]{2,1,0:T(8,128)(2,1)S(1)}, bf16[5,256,128]{2,1,0:T(8,128)(2,1)S(1)}, u32[]{:S(2)}, u32[]{:S(2)}) collective-permute-start(bf16[5,256,128]{2,1,0:T(8,128)(2,1)S(1)} %get-tuple-element.10.refs_3_), channel_id=1, source_target_pairs={{0,8},{8,16},{16,24},{24,0},{1,9},{9,17},{17,25},{25,1},{2,10},{10... | collective-permute-start | bytes 983048 | tf_op jit(solution)/shard_map/ppermute | solution.py:188
  55.1 13.2 %collective-permute-start.4 = (bf16[5,256,128]{2,1,0:T(8,128)(2,1)S(1)}, bf16[5,256,128]{2,1,0:T(8,128)(2,1)S(1)}, u32[]{:S(2)}, u32[]{:S(2)}) collective-permute-start(bf16[5,256,128]{2,1,0:T(8,128)(2,1)S(1)} %collective-permute-done.refs_4_), channel_id=1, source_target_pairs={{0,8},{8,16},{16,24},{24,0},{1,9},{9,17},{17,25},{25,1},{2,10},{10... | collective-permute-start | bytes 983048 | tf_op jit(solution)/shard_map/ppermute | solution.py:188
  58.5 10.5 %collective-permute-start.5 = (bf16[5,256,128]{2,1,0:T(8,128)(2,1)S(1)}, bf16[5,256,128]{2,1,0:T(8,128)(2,1)S(1)}, u32[]{:S(2)}, u32[]{:S(2)}) collective-permute-start(bf16[5,256,128]{2,1,0:T(8,128)(2,1)S(1)} %collective-permute-done.3.refs_7_), channel_id=1, source_target_pairs={{0,24},{8,0},{16,8},{24,16},{1,25},{9,1},{17,9},{25,17},{2,26},{10... | collective-permute-start | bytes 983048 | tf_op jit(solution)/shard_map/ppermute | solution.py:188

commit v3 on v2

v3 whole, which is shorter than its diff:
```python
import functools

import jax
import jax.numpy as jnp
from jax import lax
from jax.experimental import pallas as pl
from jax.experimental.pallas import tpu as pltpu
from jax.sharding import Mesh
from jax.sharding import PartitionSpec as P

DH = 128
SCALE = 1.4426950408889634 / DH**0.5
CLOSED = -1e30
VMEM_LIMIT = 20 * 1024 * 1024
STAT_ROWS = 16
BF = jnp.bfloat16
F32 = jnp.float32


def pack_kernel(q_hbm, k_hbm, v_hbm, out_ref, q_ref, k_ref, v_ref, sems):
    copies = [
        pltpu.make_async_copy(k_hbm, k_ref, sems.at[0]),
        pltpu.make_async_copy(v_hbm, v_ref, sems.at[1]),
        pltpu.make_async_copy(q_hbm, q_ref, sems.at[2]),
    ]
    for copy in copies:
        copy.start()
    n_z, heads = out_ref.shape[:2]
    blocks, tokens, _ = k_ref.shape
    qb, qt, _ = q_ref.shape
    for part, ref in enumerate((k_ref, v_ref)):
        copies[part].wait()
        for z in range(n_z):
            for h in range(heads):
                columns = pl.ds((z * heads + h) * DH, DH)
                for b in range(blocks):
                    rows = pl.ds((part * blocks + b) * tokens, tokens)
                    out_ref[z, h, rows, :] = ref[b, :, columns]
    copies[2].wait()
    queries = jnp.concatenate([q_ref[i].astype(F32) for i in range(qb)], axis=0).astype(BF)
    for z in range(n_z):
        for h in range(heads):
            first = (z * heads + h) * DH
            out_ref[z, h, pl.ds(2 * blocks * tokens, qb * qt), :] = queries[:, first : first + DH]


def unpack_kernel(kv_rows, sorted_ref, kv_ref):
    n_z, heads, _, _ = sorted_ref.shape
    for h in range(heads):
        for z in range(n_z):
            for part in range(2):
                rows = sorted_ref[z, h, pl.ds(part * kv_rows, kv_rows), :]
                kv_ref[part, h, pl.ds(z * kv_rows, kv_rows), :] = rows


def spread_kernel(kv_rows, sorted_ref, q_ref):
    n_z, heads, rows, _ = sorted_ref.shape
    for h in range(heads):
        query = jnp.concatenate(
            [sorted_ref[z, h, pl.ds(2 * kv_rows, rows - 2 * kv_rows), :].astype(F32) for z in range(n_z)],
            axis=0,
        ).astype(BF)
        for to in range(q_ref.shape[0]):
            q_ref[to, h] = query


def block_bias(bias_ref, piece, blocks, tokens, keys):
    place = piece * blocks
    block = lax.broadcasted_iota(jnp.int32, (bias_ref.shape[0], keys), 1) // tokens % blocks
    bias = jnp.broadcast_to(bias_ref[:, place : place + 1], block.shape)
    for b in range(1, blocks):
        bias = jnp.where(block == b, bias_ref[:, place + b : place + b + 1], bias)
    return bias


def scores_of(query, key, bias):
    s = lax.dot_general(query, key, (((1,), (1,)), ((), ())), preferred_element_type=F32)
    period, keys = bias.shape
    return (s.reshape(-1, period, keys) + bias[None]).reshape(s.shape)


def weigh(scores, top, value):
    weight = jnp.exp2((scores - top) * SCALE).astype(BF)
    ones = jnp.ones(value.shape, BF)
    return jnp.dot(weight, jnp.concatenate([value, ones], axis=1), preferred_element_type=F32)


def attend_kernel(blocks, tokens, q_ref, bias_ref, *refs):
    pieces, (top_ref, total_ref, sum_ref) = refs[:-3], refs[-3:]
    n_to, heads, period, _ = q_ref.shape
    rows, keys = n_to * period, pieces[0].shape[2]
    bias = [block_bias(bias_ref, i, blocks, tokens, keys) for i in range(len(pieces))]
    for h in range(heads):
        query = q_ref[:, h].reshape(rows, DH)
        scores = [scores_of(query, ref[0, h], item) for ref, item in zip(pieces, bias, strict=True)]
        top = jnp.max(functools.reduce(jnp.maximum, scores), axis=1, keepdims=True)
        both = jnp.zeros((rows, 2 * DH), F32)
        for s, ref in zip(scores, pieces, strict=True):
            both = both + weigh(s, top, ref[1, h])
        top_ref[h] = jnp.broadcast_to(top, (rows, DH))
        sum_ref[h] = both[:, :DH]
        total_ref[h] = both[:, DH:]


def last_kernel(blocks, tokens, piece, q_ref, bias_ref, key_ref, value_ref, top_ref, total_ref, sum_ref, out_ref):
    n_to, heads, period, _ = q_ref.shape
    rows, keys = n_to * period, key_ref.shape[1]
    bias = block_bias(bias_ref, piece, blocks, tokens, keys)
    lane = lax.broadcasted_iota(jnp.int32, (rows, DH), 1)
    tops = jnp.zeros((rows, DH), F32)
    totals = jnp.ones((rows, DH), F32)
    own = out_ref.shape[1] // (heads + 1)

    def put(h, item):
        for i in range(rows // own):
            out_ref[i, pl.ds(h * own, own), :] = item[i * own : (i + 1) * own]

    for h in range(heads):
        scores = scores_of(q_ref[:, h].reshape(rows, DH), key_ref[h], bias)
        before = top_ref[h]
        top = jnp.maximum(jnp.max(scores, axis=1, keepdims=True), before)
        fade = jnp.exp2((before - top) * SCALE)
        both = weigh(scores, jnp.concatenate([top] * (keys // DH), axis=1), value_ref[h])
        total = total_ref[h] * fade + both[:, DH:]
        out = ((sum_ref[h] * fade + both[:, :DH]) / total).astype(BF)
        put(h, out)
        tops = jnp.where(lane == h, top, tops)
        totals = jnp.where(lane == h, total, totals)
    lse = tops * (1.0 / DH**0.5) + jnp.log(totals)
    high = lse.astype(BF).astype(F32)
    rest = lse - high
    middle = rest.astype(BF).astype(F32)
    stats = high + pltpu.roll(middle, heads, 1) + pltpu.roll(rest - middle, 2 * heads, 1)
    put(heads, stats.astype(BF))


def merge_kernel(n_from, part_ref, out_ref):
    n_z, heads = part_ref.shape[0] // n_from, part_ref.shape[1] // (out_ref.shape[0] * out_ref.shape[1]) - 1
    qb, qt, _ = out_ref.shape
    own = qb * qt
    for z in range(n_z):
        lse = []
        for y in range(n_from):
            stats = part_ref[y * n_z + z, pl.ds(heads * own, own), :].astype(F32)
            lse.append(stats + pltpu.roll(stats, DH - heads, 1) + pltpu.roll(stats, DH - 2 * heads, 1))
        top = functools.reduce(jnp.maximum, lse)
        weight = [jnp.exp(item - top) for item in lse]
        norm = functools.reduce(jnp.add, weight)
        weight = [item / norm for item in weight]
        for h in range(heads):
            summed = jnp.zeros((own, DH), F32)
            for y in range(n_from):
                out = part_ref[y * n_z + z, pl.ds(h * own, own), :].astype(F32)
                summed = summed + out * weight[y][:, h : h + 1]
            for i in range(qb):
                place = pl.ds((z * heads + h) * DH, DH)
                out_ref[i, :, place] = summed[i * qt : (i + 1) * qt].astype(BF)


def call(kernel, out_shape, *args, flops=0, scratch=(), space=pltpu.VMEM, vmem=VMEM_LIMIT):
    whole = pl.BlockSpec(memory_space=pltpu.VMEM)
    size = sum(a.size * a.dtype.itemsize for a in args)
    size += sum(o.size * o.dtype.itemsize for o in jax.tree.leaves(out_shape))
    return pl.pallas_call(
        kernel,
        out_shape=out_shape,
        in_specs=[pl.BlockSpec(memory_space=space)] * len(args),
        out_specs=jax.tree.map(lambda _: whole, out_shape),
        scratch_shapes=list(scratch),
        compiler_params=pltpu.CompilerParams(vmem_limit_bytes=vmem),
        cost_estimate=pl.CostEstimate(flops=flops, bytes_accessed=size, transcendentals=0),
    )(*args)


def shift(block, axis, by):
    count = lax.axis_size(axis)
    return lax.ppermute(block, axis, [(i, (i + by) % count) for i in range(count)])


def local(queries, keys, values, mask_cols, mask_counts):
    n_z, n_x, n_y = lax.axis_size("head"), lax.axis_size("x"), lax.axis_size("y")
    qb, qt, d = queries.shape
    blocks, tokens, _ = keys.shape
    heads = d // n_z // DH
    kv_rows = blocks * tokens
    own = qb * qt
    period = n_z * own
    rows = n_y * period
    n_keys = n_z * kv_rows
    struct = jax.ShapeDtypeStruct

    packed = call(
        pack_kernel,
        struct((n_z, heads, 2 * kv_rows + own, DH), BF),
        queries,
        keys,
        values,
        scratch=[
            pltpu.VMEM(queries.shape, BF),
            pltpu.VMEM(keys.shape, BF),
            pltpu.VMEM(values.shape, BF),
            pltpu.SemaphoreType.DMA((3,)),
        ],
        space=pltpu.HBM, vmem=62 * 1024 * 1024,
    )
    sorted_ = lax.all_to_all(packed, "head", 0, 0)
    kv = call(
        functools.partial(unpack_kernel, kv_rows), struct((2, heads, n_keys, DH), BF), sorted_
    )
    query = call(
        functools.partial(spread_kernel, kv_rows), struct((n_y, heads, period, DH), BF), sorted_
    )

    pair_left = shift(kv, "x", 1)
    pair_right = shift(kv, "x", -1)
    query_all = lax.all_to_all(query, "y", 0, 0)
    key_far = shift(pair_left[0], "x", 1)
    value_far = shift(pair_right[1], "x", -1)

    x = lax.axis_index("x")
    places = jnp.stack([x, (x + n_x - 1) % n_x, (x + 1) % n_x, (x + 2) % n_x])
    owned = (places[:, None] * n_y + lax.axis_index("y")) * blocks + jnp.arange(blocks)
    owned = owned.reshape(-1)
    listed = jnp.arange(mask_cols.shape[1])[None, :] < mask_counts[:, None]
    hit = (mask_cols[:, :, None] == owned) & listed[:, :, None]
    bias = jnp.where(jnp.any(hit, axis=1), 0.0, CLOSED).astype(F32)
    bias = jnp.repeat(bias, qt, axis=0)

    flops = 4 * rows * n_keys * heads * DH
    state = call(
        functools.partial(attend_kernel, blocks, tokens),
        (struct((heads, rows, DH), F32),) * 3,
        query_all,
        bias,
        kv,
        pair_left,
        pair_right,
        flops=3 * flops,
    )
    part = call(
        functools.partial(last_kernel, blocks, tokens, 3),
        struct((n_y * n_z, (heads + 1) * own, DH), BF),
        query_all,
        bias,
        key_far,
        value_far,
        *state,
        flops=flops,
    )
    part = lax.all_to_all(part, ("y", "head"), 0, 0)
    return call(functools.partial(merge_kernel, n_y), struct((qb, qt, d), BF), part)


def solution(mesh):
    cfg, head, kv = (mesh.shape[name] for name in ("cfg", "head", "kv"))
    n_x = 4
    fine = Mesh(mesh.devices.reshape(cfg, head, n_x, kv // n_x), ("cfg", "head", "x", "y"))
    token = P(("cfg", "head"), ("x", "y"), None)
    block = P(("cfg", "x", "y"), "head", None)
    return jax.shard_map(
        local,
        mesh=fine,
        in_specs=(token, block, block, P(), P()),
        out_specs=token,
        check_vma=False,
    )
```

time: 113 us -> 102 us (0.903)
  the two profiles are of different devices: /device:TPU:2 before, /device:TPU:22 now
where the time goes in v3:
time: 102 us
  blocking collectives  64.3 us (63%)
  starting transfers between devices  19.3 us (19%)
  Pallas kernels  9.27 us (9%)
  waiting for transfers between devices  6.75 us (7%)
  local copies, waits for them, and re-layouts  1.59 us (2%)
    all_to_all x1, blocking collectives, local(): sorted_ = lax.all_to_all(packed, 'head', 0, 0)  32.4 us
    all_to_all x1, blocking collectives, local(): part = lax.all_to_all(part, ('y', 'head'), 0, 0)  31.9 us
    ppermute x4, starting transfers between devices, shift(): lax.ppermute(block, axis, [(i, (i + by) % count) for i in range(count)])  11.8 us
    pallas_call x6, Pallas kernels, call(): pl.pallas_call(kernel, out_shape=out_shape, in_specs=[pl.BlockSpec(memory...  9.27 us
    all_to_all x1, starting transfers between devices, local(): query_all = lax.all_to_all(query, 'y', 0, 0)  7.56 us
    all_to_all x1, waiting for transfers between devices, local(): query_all = lax.all_to_all(query, 'y', 0, 0)  5 us
  transfers between devices with their start and end apart: 5, of which 2 were waited for; matrix products, arithmetic and copies ran while one was open for 2% of the time, Pallas kernels for 4%

profile of v3, /device:TPU:22, one launch (start us, length us, event | category | flops | bytes accessed | tf_op | source)
XLA Modules:
  0.0 102.0 jit_solution(10870034130643003866)
XLA Ops:
  0.0 2.1 %shard_map.55 = bf16[8,5,72,128]{3,2,1,0:T(8,128)(2,1)} custom-call(bf16[2,4,5120]{2,1,0:T(4,128)(2,1)} %q_hbm.1, bf16[2,16,5120]{2,1,0:T(8,128)(2,1)} %k_hbm.1, bf16[2,16,5120]{2,1,0:T(8,128)(2,1)} %v_hbm.1), custom_call_target="tpu_custom_call" | custom-call | bytes 1474560 | tf_op jit(solution)/shard_map/pallas_call | solution.py:164
  2.1 32.4 %all_to_all.15.sorted_ref = bf16[8,5,72,128]{3,2,1,0:T(8,128)(2,1)S(1)} all-to-all(bf16[8,5,72,128]{3,2,1,0:T(8,128)(2,1)} %shard_map.55), channel_id=1, replica_groups=mesh['cfg'=2,'head'=8,'x'=4,'y'=8] {'head'}, dimensions={0} | all-to-all | bytes 1474560 | tf_op jit(solution)/shard_map/all_to_all | solution.py:206
  34.5 2.4 %collective-permute-start = (bf16[2,5,256,128]{3,2,1,0:T(8,128)(2,1)S(1)}, bf16[2,5,256,128]{3,2,1,0:T(8,128)(2,1)S(1)}, u32[]{:S(2)}, u32[]{:S(2)}) collective-permute-start(bf16[2,5,256,128]{3,2,1,0:T(8,128)(2,1)S(1)} %shard_map.57.refs_0_), channel_id=1, source_target_pairs={{0,8},{8,16},{16,24},{24,0},{1,9},{9,17},{17,25},{25,1},{2,10},{10... | collective-permute-start | bytes 1966088 | tf_op jit(solution)/shard_map/ppermute | solution.py:177
  36.9 0.1 fusion.1
  37.0 0.0 copy-start.1
  37.0 3.6 %collective-permute-start.2 = (bf16[2,5,256,128]{3,2,1,0:T(8,128)(2,1)S(1)}, bf16[2,5,256,128]{3,2,1,0:T(8,128)(2,1)S(1)}, u32[]{:S(2)}, u32[]{:S(2)}) collective-permute-start(bf16[2,5,256,128]{3,2,1,0:T(8,128)(2,1)S(1)} %shard_map.57.refs_0_), channel_id=1, source_target_pairs={{0,24},{8,0},{16,8},{24,16},{1,25},{9,1},{17,9},{25,17},{2,26},{10... | collective-permute-start | bytes 1966088 | tf_op jit(solution)/shard_map/ppermute | solution.py:177
  40.6 0.9 shard_map.56
  41.5 0.0 copy-start
  41.5 7.6 %all-to-all-start.1 = ((bf16[8,5,64,128]{3,2,1,0:T(8,128)(2,1)}), bf16[8,5,64,128]{3,2,1,0:T(8,128)(2,1)S(1)}, u32[]{:S(2)}, u32[]{:S(2)}) async-start(bf16[8,5,64,128]{3,2,1,0:T(8,128)(2,1)} %shard_map.56), calls=%async_computation.1 | async-start | bytes 1310720 | tf_op jit(solution)/shard_map/all_to_all | solution.py:216
  49.1 0.1 iota_add_fusion
  49.1 0.1 add.61
  49.2 0.0 copy-done.1
  49.2 0.1 iota_compare_fusion
  49.3 1.7 %collective-permute-done.refs_1_ = bf16[2,5,256,128]{3,2,1,0:T(8,128)(2,1)S(1)} collective-permute-done((bf16[2,5,256,128]{3,2,1,0:T(8,128)(2,1)S(1)}, bf16[2,5,256,128]{3,2,1,0:T(8,128)(2,1)S(1)}, u32[]{:S(2)}, u32[]{:S(2)}) %collective-permute-start) | collective-permute-done | bytes 655392 | tf_op jit(solution)/shard_map/ppermute | solution.py:177
  51.0 0.7 slice_bitcast_fusion.1
  51.8 3.6 %collective-permute-start.1 = (bf16[5,256,128]{2,1,0:T(8,128)(2,1)}, bf16[5,256,128]{2,1,0:T(8,128)(2,1)S(1)}, u32[]{:S(2)}, u32[]{:S(2)}) collective-permute-start(bf16[5,256,128]{2,1,0:T(8,128)(2,1)} %slice_bitcast_fusion.1), channel_id=1, source_target_pairs={{0,8},{8,16},{16,24},{24,0},{1,9},{9,17},{17,25},{25,1},{2,10},{10... | collective-permute-start | bytes 983048 | tf_op jit(solution)/shard_map/ppermute | solution.py:177
  55.4 0.0 collective-permute-done.2.refs_2_
  55.4 0.7 slice_bitcast_fusion
  56.1 2.2 %collective-permute-start.3 = (bf16[5,256,128]{2,1,0:T(8,128)(2,1)}, bf16[5,256,128]{2,1,0:T(8,128)(2,1)S(1)}, u32[]{:S(2)}, u32[]{:S(2)}) collective-permute-start(bf16[5,256,128]{2,1,0:T(8,128)(2,1)} %slice_bitcast_fusion), channel_id=1, source_target_pairs={{0,24},{8,0},{16,8},{24,16},{1,25},{9,1},{17,9},{25,17},{2,26},{10... | collective-permute-start | bytes 983048 | tf_op jit(solution)/shard_map/ppermute | solution.py:177
  58.4 0.0 copy-done
  58.4 0.4 and_reduce_fusion
  58.8 5.0 %all-to-all-done.1.q_ref = bf16[8,5,64,128]{3,2,1,0:T(8,128)(2,1)S(1)} async-done(((bf16[8,5,64,128]{3,2,1,0:T(8,128)(2,1)}), bf16[8,5,64,128]{3,2,1,0:T(8,128)(2,1)S(1)}, u32[]{:S(2)}, u32[]{:S(2)}) %all-to-all-start.1) | async-done | bytes 655392 | tf_op jit(solution)/shard_map/all_to_all | solution.py:216
  63.8 2.8 %shard_map.58 = (f32[5,512,128]{2,1,0:T(8,128)S(1)}, f32[5,512,128]{2,1,0:T(8,128)S(1)}, f32[5,512,128]{2,1,0:T(8,128)S(1)}) custom-call(bf16[8,5,64,128]{3,2,1,0:T(8,128)(2,1)S(1)} %all-to-all-done.1.q_ref, f32[64,8]{1,0:T(8,128)S(1)} %bitcast.9, bf16[2,5,256,128]{3,2,1,0:T(8,128)(2,1)S(1)} %shard_map.57.refs_0_, ...), custom_call_target="tpu_custom_call" | custom-call | flops 1006632960 | bytes 6555648 | tf_op jit(solution)/shard_map/pallas_call | solution.py:164
  66.6 0.0 collective-permute-done.1.key_ref
  66.7 0.0 collective-permute-done.3.value_ref
  66.7 1.4 %shard_map.59 = bf16[64,48,128]{2,1,0:T(8,128)(2,1)S(1)} custom-call(bf16[8,5,64,128]{3,2,1,0:T(8,128)(2,1)S(1)} %all-to-all-done.1.q_ref, f32[64,8]{1,0:T(8,128)S(1)} %bitcast.10, bf16[5,256,128]{2,1,0:T(8,128)(2,1)S(1)} %collective-permute-done.1.key_ref, bf16[5,256,128]{2,1,0:T(8,128)(2,1)S(1)} %collective-permute-done.3.value_ref, ...), custom_call_target="tpu_custom_call" | custom-call | flops 335544320 | bytes 6031360 | tf_op jit(solution)/shard_map/pallas_call | solution.py:164
  68.1 31.9 %all_to_all.16.part_ref = bf16[64,48,128]{2,1,0:T(8,128)(2,1)S(1)} all-to-all(bf16[64,48,128]{2,1,0:T(8,128)(2,1)S(1)} %shard_map.59), channel_id=1, replica_groups=mesh['cfg'=2,'head'=8,'x'=4,'y'=8] {'y','head'}, dimensions={0} | all-to-all | bytes 1572864 | tf_op jit(solution)/shard_map/all_to_all | solution.py:250
  100.0 2.0 %shard_map.60 = bf16[2,4,5120]{2,1,0:T(4,128)(2,1)} custom-call(bf16[64,48,128]{2,1,0:T(8,128)(2,1)S(1)} %all_to_all.16.part_ref), custom_call_target="tpu_custom_call" | custom-call | bytes 868352 | tf_op jit(solution)/shard_map/pallas_call | solution.py:164
  (3 shorter events, 0.1 us)
Async XLA Ops:
  34.5 16.6 %collective-permute-start = (bf16[2,5,256,128]{3,2,1,0:T(8,128)(2,1)S(1)}, bf16[2,5,256,128]{3,2,1,0:T(8,128)(2,1)S(1)}, u32[]{:S(2)}, u32[]{:S(2)}) collective-permute-start(bf16[2,5,256,128]{3,2,1,0:T(8,128)(2,1)S(1)} %shard_map.57.refs_0_), channel_id=1, source_target_pairs={{0,8},{8,16},{16,24},{24,0},{1,9},{9,17},{17,25},{25,1},{2,10},{10... | collective-permute-start | bytes 1966088 | tf_op jit(solution)/shard_map/ppermute | solution.py:177
  37.0 12.2 %copy-start.1 = (s32[16]{0:T(128)S(1)}, s32[16]{0:T(128)}, u32[]{:S(2)}) copy-start(s32[16]{0:T(128)} %param.9) | copy-start | bytes 196
  37.0 18.4 %collective-permute-start.2 = (bf16[2,5,256,128]{3,2,1,0:T(8,128)(2,1)S(1)}, bf16[2,5,256,128]{3,2,1,0:T(8,128)(2,1)S(1)}, u32[]{:S(2)}, u32[]{:S(2)}) collective-permute-start(bf16[2,5,256,128]{3,2,1,0:T(8,128)(2,1)S(1)} %shard_map.57.refs_0_), channel_id=1, source_target_pairs={{0,24},{8,0},{16,8},{24,16},{1,25},{9,1},{17,9},{25,17},{2,26},{10... | collective-permute-start | bytes 1966088 | tf_op jit(solution)/shard_map/ppermute | solution.py:177
  41.5 16.9 %copy-start = (s32[16,32]{1,0:T(8,128)S(1)}, s32[16,32]{1,0:T(8,128)}, u32[]{:S(2)}) copy-start(s32[16,32]{1,0:T(8,128)} %param.8) | copy-start | bytes 6148
  41.5 22.3 %all-to-all-start.1 = ((bf16[8,5,64,128]{3,2,1,0:T(8,128)(2,1)}), bf16[8,5,64,128]{3,2,1,0:T(8,128)(2,1)S(1)}, u32[]{:S(2)}, u32[]{:S(2)}) async-start(bf16[8,5,64,128]{3,2,1,0:T(8,128)(2,1)} %shard_map.56), calls=%async_computation.1 | async-start | bytes 1310720 | tf_op jit(solution)/shard_map/all_to_all | solution.py:216
  51.8 14.9 %collective-permute-start.1 = (bf16[5,256,128]{2,1,0:T(8,128)(2,1)}, bf16[5,256,128]{2,1,0:T(8,128)(2,1)S(1)}, u32[]{:S(2)}, u32[]{:S(2)}) collective-permute-start(bf16[5,256,128]{2,1,0:T(8,128)(2,1)} %slice_bitcast_fusion.1), channel_id=1, source_target_pairs={{0,8},{8,16},{16,24},{24,0},{1,9},{9,17},{17,25},{25,1},{2,10},{10... | collective-permute-start | bytes 983048 | tf_op jit(solution)/shard_map/ppermute | solution.py:177
  56.1 10.5 %collective-permute-start.3 = (bf16[5,256,128]{2,1,0:T(8,128)(2,1)}, bf16[5,256,128]{2,1,0:T(8,128)(2,1)S(1)}, u32[]{:S(2)}, u32[]{:S(2)}) collective-permute-start(bf16[5,256,128]{2,1,0:T(8,128)(2,1)} %slice_bitcast_fusion), channel_id=1, source_target_pairs={{0,24},{8,0},{16,8},{24,16},{1,25},{9,1},{17,9},{25,17},{2,26},{10... | collective-permute-start | bytes 983048 | tf_op jit(solution)/shard_map/ppermute | solution.py:177

commit v4 on v3

--- a/solution.py
+++ b/solution.py
@@ -50,7 +50,7 @@
         for z in range(n_z):
             for part in range(2):
                 rows = sorted_ref[z, h, pl.ds(part * kv_rows, kv_rows), :]
-                kv_ref[part, h, pl.ds(z * kv_rows, kv_rows), :] = rows
+                kv_ref[h, part, pl.ds(z * kv_rows, kv_rows), :] = rows
 
 
 def spread_kernel(kv_rows, sorted_ref, q_ref):
@@ -62,6 +62,10 @@
         ).astype(BF)
         for to in range(q_ref.shape[0]):
             q_ref[to, h] = query
+
+
+def take_kernel(first, pair_ref, out_ref):
+    out_ref[...] = pair_ref[pl.ds(first, out_ref.shape[0])]
 
 
 def block_bias(bias_ref, piece, blocks, tokens, keys):
@@ -92,19 +96,19 @@
     bias = [block_bias(bias_ref, i, blocks, tokens, keys) for i in range(len(pieces))]
     for h in range(heads):
         query = q_ref[:, h].reshape(rows, DH)
-        scores = [scores_of(query, ref[0, h], item) for ref, item in zip(pieces, bias, strict=True)]
+        scores = [scores_of(query, ref[h, 0], item) for ref, item in zip(pieces, bias, strict=True)]
         top = jnp.max(functools.reduce(jnp.maximum, scores), axis=1, keepdims=True)
         both = jnp.zeros((rows, 2 * DH), F32)
         for s, ref in zip(scores, pieces, strict=True):
-            both = both + weigh(s, top, ref[1, h])
+            both = both + weigh(s, top, ref[h, 1])
         top_ref[h] = jnp.broadcast_to(top, (rows, DH))
         sum_ref[h] = both[:, :DH]
         total_ref[h] = both[:, DH:]
 
 
-def last_kernel(blocks, tokens, piece, q_ref, bias_ref, key_ref, value_ref, top_ref, total_ref, sum_ref, out_ref):
+def last_kernel(blocks, tokens, piece, q_ref, bias_ref, low_ref, high_ref, top_ref, total_ref, sum_ref, out_ref):
     n_to, heads, period, _ = q_ref.shape
-    rows, keys = n_to * period, key_ref.shape[1]
+    rows, keys = n_to * period, low_ref.shape[2]
     bias = block_bias(bias_ref, piece, blocks, tokens, keys)
     lane = lax.broadcasted_iota(jnp.int32, (rows, DH), 1)
     tops = jnp.zeros((rows, DH), F32)
@@ -116,11 +120,13 @@
             out_ref[i, pl.ds(h * own, own), :] = item[i * own : (i + 1) * own]
 
     for h in range(heads):
-        scores = scores_of(q_ref[:, h].reshape(rows, DH), key_ref[h], bias)
+        cut = low_ref.shape[0]
+        pair = low_ref.at[h] if h < cut else high_ref.at[h - cut]
+        scores = scores_of(q_ref[:, h].reshape(rows, DH), pair[0], bias)
         before = top_ref[h]
         top = jnp.maximum(jnp.max(scores, axis=1, keepdims=True), before)
         fade = jnp.exp2((before - top) * SCALE)
-        both = weigh(scores, jnp.concatenate([top] * (keys // DH), axis=1), value_ref[h])
+        both = weigh(scores, jnp.concatenate([top] * (keys // DH), axis=1), pair[1])
         total = total_ref[h] * fade + both[:, DH:]
         out = ((sum_ref[h] * fade + both[:, :DH]) / total).astype(BF)
         put(h, out)
@@ -135,32 +141,34 @@
 
 
 def merge_kernel(n_from, part_ref, out_ref):
-    n_z, heads = part_ref.shape[0] // n_from, part_ref.shape[1] // (out_ref.shape[0] * out_ref.shape[1]) - 1
+    n_z = part_ref.shape[0] // n_from
     qb, qt, _ = out_ref.shape
     own = qb * qt
-    for z in range(n_z):
-        lse = []
-        for y in range(n_from):
-            stats = part_ref[y * n_z + z, pl.ds(heads * own, own), :].astype(F32)
-            lse.append(stats + pltpu.roll(stats, DH - heads, 1) + pltpu.roll(stats, DH - 2 * heads, 1))
-        top = functools.reduce(jnp.maximum, lse)
-        weight = [jnp.exp(item - top) for item in lse]
-        norm = functools.reduce(jnp.add, weight)
-        weight = [item / norm for item in weight]
-        for h in range(heads):
-            summed = jnp.zeros((own, DH), F32)
-            for y in range(n_from):
-                out = part_ref[y * n_z + z, pl.ds(h * own, own), :].astype(F32)
-                summed = summed + out * weight[y][:, h : h + 1]
+    heads = part_ref.shape[1] // own - 1
+
+    def rows_of(item):
+        rows = part_ref[:, pl.ds(item * own, own), :].astype(F32)
+        return rows.reshape(n_from, n_z * own, DH)
+
+    stats = rows_of(heads)
+    lse = stats + pltpu.roll(stats, DH - heads, 2) + pltpu.roll(stats, DH - 2 * heads, 2)
+    weight = jnp.exp(lse - jnp.max(lse, axis=0, keepdims=True))
+    weight = weight / jnp.sum(weight, axis=0, keepdims=True)
+    for h in range(heads):
+        summed = jnp.sum(rows_of(h) * weight[:, :, h : h + 1], axis=0)
+        for z in range(n_z):
             for i in range(qb):
                 place = pl.ds((z * heads + h) * DH, DH)
-                out_ref[i, :, place] = summed[i * qt : (i + 1) * qt].astype(BF)
-
-
-def call(kernel, out_shape, *args, flops=0, scratch=(), space=pltpu.VMEM, vmem=VMEM_LIMIT):
+                first = z * own + i * qt
+                out_ref[i, :, place] = summed[first : first + qt].astype(BF)
+
+
+def call(kernel, out_shape, *args, flops=0, light=False, scratch=(), space=pltpu.VMEM, vmem=VMEM_LIMIT):
     whole = pl.BlockSpec(memory_space=pltpu.VMEM)
     size = sum(a.size * a.dtype.itemsize for a in args)
     size += sum(o.size * o.dtype.itemsize for o in jax.tree.leaves(out_shape))
+    if light:
+        size = 0
     return pl.pallas_call(
         kernel,
         out_shape=out_shape,
@@ -205,7 +213,7 @@
     )
     sorted_ = lax.all_to_all(packed, "head", 0, 0)
     kv = call(
-        functools.partial(unpack_kernel, kv_rows), struct((2, heads, n_keys, DH), BF), sorted_
+        functools.partial(unpack_kernel, kv_rows), struct((heads, 2, n_keys, DH), BF), sorted_
     )
     query = call(
         functools.partial(spread_kernel, kv_rows), struct((n_y, heads, period, DH), BF), sorted_
@@ -214,8 +222,20 @@
     pair_left = shift(kv, "x", 1)
     pair_right = shift(kv, "x", -1)
     query_all = lax.all_to_all(query, "y", 0, 0)
-    key_far = shift(pair_left[0], "x", 1)
-    value_far = shift(pair_right[1], "x", -1)
+    cut = (heads + 1) // 2
+    far_low, far_high = (
+        shift(
+            call(
+                functools.partial(take_kernel, first),
+                struct((count,) + kv.shape[1:], BF),
+                pair,
+                flops=2 * 10**10,
+            ),
+            "x",
+            by,
+        )
+        for pair, first, count, by in ((pair_left, 0, cut, 1), (pair_right, cut, heads - cut, -1))
+    )
 
     x = lax.axis_index("x")
     places = jnp.stack([x, (x + n_x - 1) % n_x, (x + 1) % n_x, (x + 2) % n_x])
@@ -235,15 +255,15 @@
         kv,
         pair_left,
         pair_right,
-        flops=3 * flops,
+        light=True,
     )
     part = call(
         functools.partial(last_kernel, blocks, tokens, 3),
         struct((n_y * n_z, (heads + 1) * own, DH), BF),
         query_all,
         bias,
-        key_far,
-        value_far,
+        far_low,
+        far_high,
         *state,
         flops=flops,
     )

time: 102 us -> 101 us (level)
  the two profiles are of different devices: /device:TPU:22 before, /device:TPU:16 now
where the time goes in v4:
time: 101 us
  blocking collectives  62.4 us (62%)
  starting transfers between devices  21.6 us (21%)
  Pallas kernels  10 us (10%)
  waiting for transfers between devices  5.62 us (6%)
    all_to_all x1, blocking collectives, local(): sorted_ = lax.all_to_all(packed, 'head', 0, 0)  32.4 us
    all_to_all x1, blocking collectives, local(): part = lax.all_to_all(part, ('y', 'head'), 0, 0)  30 us
    ppermute x4, starting transfers between devices, shift(): lax.ppermute(block, axis, [(i, (i + by) % count) for i in range(count)])  14.2 us
    pallas_call x8, Pallas kernels, call(): pl.pallas_call(kernel, out_shape=out_shape, in_specs=[pl.BlockSpec(memory...  10 us
    all_to_all x1, starting transfers between devices, local(): query_all = lax.all_to_all(query, 'y', 0, 0)  7.43 us
    all_to_all x1, waiting for transfers between devices, local(): query_all = lax.all_to_all(query, 'y', 0, 0)  3.61 us
  transfers between devices with their start and end apart: 5, of which 2 were waited for; matrix products, arithmetic and copies ran while one was open for 1% of the time, Pallas kernels for 5%

profile of v4, /device:TPU:16, one launch (start us, length us, event | category | flops | bytes accessed | tf_op | source)
XLA Modules:
  0.0 100.6 jit_solution(13497171215636845860)
XLA Ops:
  0.0 2.1 %shard_map.55 = bf16[8,5,72,128]{3,2,1,0:T(8,128)(2,1)} custom-call(bf16[2,4,5120]{2,1,0:T(4,128)(2,1)} %q_hbm.1, bf16[2,16,5120]{2,1,0:T(8,128)(2,1)} %k_hbm.1, bf16[2,16,5120]{2,1,0:T(8,128)(2,1)} %v_hbm.1), custom_call_target="tpu_custom_call" | custom-call | bytes 1474560 | tf_op jit(solution)/shard_map/pallas_call | solution.py:172
  2.1 0.0 copy-start.1
  2.1 32.4 %all_to_all.15.sorted_ref = bf16[8,5,72,128]{3,2,1,0:T(8,128)(2,1)S(1)} all-to-all(bf16[8,5,72,128]{3,2,1,0:T(8,128)(2,1)} %shard_map.55), channel_id=1, replica_groups=mesh['cfg'=2,'head'=8,'x'=4,'y'=8] {'head'}, dimensions={0} | all-to-all | bytes 1474560 | tf_op jit(solution)/shard_map/all_to_all | solution.py:214
  34.5 3.4 %collective-permute-start = (bf16[5,2,256,128]{3,2,1,0:T(8,128)(2,1)S(1)}, bf16[5,2,256,128]{3,2,1,0:T(8,128)(2,1)S(1)}, u32[]{:S(2)}, u32[]{:S(2)}) collective-permute-start(bf16[5,2,256,128]{3,2,1,0:T(8,128)(2,1)S(1)} %shard_map.57.refs_0_), channel_id=1, source_target_pairs={{0,8},{8,16},{16,24},{24,0},{1,9},{9,17},{17,25},{25,1},{2,10},{10... | collective-permute-start | bytes 1966088 | tf_op jit(solution)/shard_map/ppermute | solution.py:185
  37.9 0.1 fusion.1
  38.0 0.1 iota_add_fusion
  38.1 0.1 add.61
  38.2 0.0 copy-done.1
  38.2 0.1 iota_compare_fusion
  38.3 3.6 %collective-permute-start.2 = (bf16[5,2,256,128]{3,2,1,0:T(8,128)(2,1)S(1)}, bf16[5,2,256,128]{3,2,1,0:T(8,128)(2,1)S(1)}, u32[]{:S(2)}, u32[]{:S(2)}) collective-permute-start(bf16[5,2,256,128]{3,2,1,0:T(8,128)(2,1)S(1)} %shard_map.57.refs_0_), channel_id=1, source_target_pairs={{0,24},{8,0},{16,8},{24,16},{1,25},{9,1},{17,9},{25,17},{2,26},{10... | collective-permute-start | bytes 1966088 | tf_op jit(solution)/shard_map/ppermute | solution.py:185
  41.9 0.9 shard_map.56
  42.8 7.4 %all-to-all-start.1 = ((bf16[8,5,64,128]{3,2,1,0:T(8,128)(2,1)}), bf16[8,5,64,128]{3,2,1,0:T(8,128)(2,1)S(1)}, u32[]{:S(2)}, u32[]{:S(2)}) async-start(bf16[8,5,64,128]{3,2,1,0:T(8,128)(2,1)} %shard_map.56), calls=%async_computation.1 | async-start | bytes 1310720 | tf_op jit(solution)/shard_map/all_to_all | solution.py:224
  50.3 2.0 %collective-permute-done.pair_ref.refs_1_ = bf16[5,2,256,128]{3,2,1,0:T(8,128)(2,1)S(1)} collective-permute-done((bf16[5,2,256,128]{3,2,1,0:T(8,128)(2,1)S(1)}, bf16[5,2,256,128]{3,2,1,0:T(8,128)(2,1)S(1)}, u32[]{:S(2)}, u32[]{:S(2)}) %collective-permute-start) | collective-permute-done | bytes 655392 | tf_op jit(solution)/shard_map/ppermute | solution.py:185
  52.3 0.8 shard_map.58
  53.0 0.0 copy-start
  53.0 2.3 %collective-permute-start.1 = (bf16[3,2,256,128]{3,2,1,0:T(8,128)(2,1)}, bf16[3,2,256,128]{3,2,1,0:T(8,128)(2,1)S(1)}, u32[]{:S(2)}, u32[]{:S(2)}) collective-permute-start(bf16[3,2,256,128]{3,2,1,0:T(8,128)(2,1)} %shard_map.58), channel_id=1, source_target_pairs={{0,8},{8,16},{16,24},{24,0},{1,9},{9,17},{17,25},{25,1},{2,10},{10... | collective-permute-start | bytes 1179656 | tf_op jit(solution)/shard_map/ppermute | solution.py:185
  55.4 0.0 collective-permute-done.2.pair_ref.refs_2_
  55.4 0.7 shard_map.59
  56.1 4.9 %collective-permute-start.3 = (bf16[2,2,256,128]{3,2,1,0:T(8,128)(2,1)}, bf16[2,2,256,128]{3,2,1,0:T(8,128)(2,1)S(1)}, u32[]{:S(2)}, u32[]{:S(2)}) collective-permute-start(bf16[2,2,256,128]{3,2,1,0:T(8,128)(2,1)} %shard_map.59), channel_id=1, source_target_pairs={{0,24},{8,0},{16,8},{24,16},{1,25},{9,1},{17,9},{25,17},{2,26},{10... | collective-permute-start | bytes 786440 | tf_op jit(solution)/shard_map/ppermute | solution.py:185
  61.0 0.0 copy-done
  61.0 0.4 and_reduce_fusion
  61.4 3.6 %all-to-all-done.1.q_ref = bf16[8,5,64,128]{3,2,1,0:T(8,128)(2,1)S(1)} async-done(((bf16[8,5,64,128]{3,2,1,0:T(8,128)(2,1)}), bf16[8,5,64,128]{3,2,1,0:T(8,128)(2,1)S(1)}, u32[]{:S(2)}, u32[]{:S(2)}) %all-to-all-start.1) | async-done | bytes 655392 | tf_op jit(solution)/shard_map/all_to_all | solution.py:224
  65.0 2.8 %shard_map.60 = (f32[5,512,128]{2,1,0:T(8,128)S(1)}, f32[5,512,128]{2,1,0:T(8,128)S(1)}, f32[5,512,128]{2,1,0:T(8,128)S(1)}) custom-call(bf16[8,5,64,128]{3,2,1,0:T(8,128)(2,1)S(1)} %all-to-all-done.1.q_ref, f32[64,8]{1,0:T(8,128)S(1)} %bitcast.5, bf16[5,2,256,128]{3,2,1,0:T(8,128)(2,1)S(1)} %shard_map.57.refs_0_, ...), custom_call_target="tpu_custom_call" | custom-call | tf_op jit(solution)/shard_map/pallas_call | solution.py:172
  67.8 0.0 collective-permute-done.3.high_ref
  67.8 0.0 collective-permute-done.1.low_ref
  67.9 1.4 %shard_map.61 = bf16[64,48,128]{2,1,0:T(8,128)(2,1)S(1)} custom-call(bf16[8,5,64,128]{3,2,1,0:T(8,128)(2,1)S(1)} %all-to-all-done.1.q_ref, f32[64,8]{1,0:T(8,128)S(1)} %bitcast.6, bf16[3,2,256,128]{3,2,1,0:T(8,128)(2,1)S(1)} %collective-permute-done.1.low_ref, bf16[2,2,256,128]{3,2,1,0:T(8,128)(2,1)S(1)} %collective-permute-done.3.high_ref, ...), custom_call_target="tpu_custom_call" | custom-call | flops 335544320 | bytes 6031360 | tf_op jit(solution)/shard_map/pallas_call | solution.py:172
  69.3 30.0 %all_to_all.16.part_ref = bf16[64,48,128]{2,1,0:T(8,128)(2,1)S(1)} all-to-all(bf16[64,48,128]{2,1,0:T(8,128)(2,1)S(1)} %shard_map.61), channel_id=1, replica_groups=mesh['cfg'=2,'head'=8,'x'=4,'y'=8] {'y','head'}, dimensions={0} | all-to-all | bytes 1572864 | tf_op jit(solution)/shard_map/all_to_all | solution.py:270
  99.3 1.3 %shard_map.62 = bf16[2,4,5120]{2,1,0:T(4,128)(2,1)} custom-call(bf16[64,48,128]{2,1,0:T(8,128)(2,1)S(1)} %all_to_all.16.part_ref), custom_call_target="tpu_custom_call" | custom-call | bytes 868352 | tf_op jit(solution)/shard_map/pallas_call | solution.py:172
  (3 shorter events, 0.1 us)
Async XLA Ops:
  2.1 36.1 %copy-start.1 = (s32[16]{0:T(128)S(1)}, s32[16]{0:T(128)}, u32[]{:S(2)}) copy-start(s32[16]{0:T(128)} %param.9) | copy-start | bytes 196
  34.5 17.8 %collective-permute-start = (bf16[5,2,256,128]{3,2,1,0:T(8,128)(2,1)S(1)}, bf16[5,2,256,128]{3,2,1,0:T(8,128)(2,1)S(1)}, u32[]{:S(2)}, u32[]{:S(2)}) collective-permute-start(bf16[5,2,256,128]{3,2,1,0:T(8,128)(2,1)S(1)} %shard_map.57.refs_0_), channel_id=1, source_target_pairs={{0,8},{8,16},{16,24},{24,0},{1,9},{9,17},{17,25},{25,1},{2,10},{10... | collective-permute-start | bytes 1966088 | tf_op jit(solution)/shard_map/ppermute | solution.py:185
  38.3 17.1 %collective-permute-start.2 = (bf16[5,2,256,128]{3,2,1,0:T(8,128)(2,1)S(1)}, bf16[5,2,256,128]{3,2,1,0:T(8,128)(2,1)S(1)}, u32[]{:S(2)}, u32[]{:S(2)}) collective-permute-start(bf16[5,2,256,128]{3,2,1,0:T(8,128)(2,1)S(1)} %shard_map.57.refs_0_), channel_id=1, source_target_pairs={{0,24},{8,0},{16,8},{24,16},{1,25},{9,1},{17,9},{25,17},{2,26},{10... | collective-permute-start | bytes 1966088 | tf_op jit(solution)/shard_map/ppermute | solution.py:185
  42.8 22.2 %all-to-all-start.1 = ((bf16[8,5,64,128]{3,2,1,0:T(8,128)(2,1)}), bf16[8,5,64,128]{3,2,1,0:T(8,128)(2,1)S(1)}, u32[]{:S(2)}, u32[]{:S(2)}) async-start(bf16[8,5,64,128]{3,2,1,0:T(8,128)(2,1)} %shard_map.56), calls=%async_computation.1 | async-start | bytes 1310720 | tf_op jit(solution)/shard_map/all_to_all | solution.py:224
  53.0 7.9 %copy-start = (s32[16,32]{1,0:T(8,128)S(1)}, s32[16,32]{1,0:T(8,128)}, u32[]{:S(2)}) copy-start(s32[16,32]{1,0:T(8,128)} %param.8) | copy-start | bytes 6148
  53.0 14.8 %collective-permute-start.1 = (bf16[3,2,256,128]{3,2,1,0:T(8,128)(2,1)}, bf16[3,2,256,128]{3,2,1,0:T(8,128)(2,1)S(1)}, u32[]{:S(2)}, u32[]{:S(2)}) collective-permute-start(bf16[3,2,256,128]{3,2,1,0:T(8,128)(2,1)} %shard_map.58), channel_id=1, source_target_pairs={{0,8},{8,16},{16,24},{24,0},{1,9},{9,17},{17,25},{25,1},{2,10},{10... | collective-permute-start | bytes 1179656 | tf_op jit(solution)/shard_map/ppermute | solution.py:185
  56.1 11.7 %collective-permute-start.3 = (bf16[2,2,256,128]{3,2,1,0:T(8,128)(2,1)}, bf16[2,2,256,128]{3,2,1,0:T(8,128)(2,1)S(1)}, u32[]{:S(2)}, u32[]{:S(2)}) collective-permute-start(bf16[2,2,256,128]{3,2,1,0:T(8,128)(2,1)} %shard_map.59), channel_id=1, source_target_pairs={{0,24},{8,0},{16,8},{24,16},{1,25},{9,1},{17,9},{25,17},{2,26},{10... | collective-permute-start | bytes 786440 | tf_op jit(solution)/shard_map/ppermute | solution.py:185

commit v5 on v4

--- a/solution.py
+++ b/solution.py
@@ -113,12 +113,9 @@
     lane = lax.broadcasted_iota(jnp.int32, (rows, DH), 1)
     tops = jnp.zeros((rows, DH), F32)
     totals = jnp.ones((rows, DH), F32)
-    own = out_ref.shape[1] // (heads + 1)
-
-    def put(h, item):
-        for i in range(rows // own):
-            out_ref[i, pl.ds(h * own, own), :] = item[i * own : (i + 1) * own]
-
+    n_dest, parts, qt, _ = out_ref.shape
+    qb = parts // heads
+    own = qb * qt
     for h in range(heads):
         cut = low_ref.shape[0]
         pair = low_ref.at[h] if h < cut else high_ref.at[h - cut]
@@ -128,8 +125,10 @@
         fade = jnp.exp2((before - top) * SCALE)
         both = weigh(scores, jnp.concatenate([top] * (keys // DH), axis=1), pair[1])
         total = total_ref[h] * fade + both[:, DH:]
-        out = ((sum_ref[h] * fade + both[:, :DH]) / total).astype(BF)
-        put(h, out)
+        out = (sum_ref[h] * fade + both[:, :DH]) / total
+        out = out.reshape(n_dest, own, DH)
+        for b in range(qb):
+            out_ref[:, h * qb + b] = out[:, b * qt : (b + 1) * qt].astype(BF)
         tops = jnp.where(lane == h, top, tops)
         totals = jnp.where(lane == h, total, totals)
     lse = tops * (1.0 / DH**0.5) + jnp.log(totals)
@@ -137,30 +136,31 @@
     rest = lse - high
     middle = rest.astype(BF).astype(F32)
     stats = high + pltpu.roll(middle, heads, 1) + pltpu.roll(rest - middle, 2 * heads, 1)
-    put(heads, stats.astype(BF))
+    stats = stats.reshape(n_dest, own, DH)
+    joined = stats[:, :qt]
+    for b in range(1, qb):
+        joined = joined + pltpu.roll(stats, b * (DH // qb), 2)[:, b * qt : (b + 1) * qt]
+    out_ref[:, heads * qb] = joined.astype(BF)
 
 
 def merge_kernel(n_from, part_ref, out_ref):
     n_z = part_ref.shape[0] // n_from
     qb, qt, _ = out_ref.shape
-    own = qb * qt
-    heads = part_ref.shape[1] // own - 1
+    heads = part_ref.shape[1] // qb
 
     def rows_of(item):
-        rows = part_ref[:, pl.ds(item * own, own), :].astype(F32)
-        return rows.reshape(n_from, n_z * own, DH)
-
-    stats = rows_of(heads)
-    lse = stats + pltpu.roll(stats, DH - heads, 2) + pltpu.roll(stats, DH - 2 * heads, 2)
+        return part_ref[:, item].astype(F32).reshape(n_from, n_z, qt, DH)
+
+    stats = rows_of(heads * qb)
+    lse = stats + pltpu.roll(stats, DH - heads, 3) + pltpu.roll(stats, DH - 2 * heads, 3)
     weight = jnp.exp(lse - jnp.max(lse, axis=0, keepdims=True))
     weight = weight / jnp.sum(weight, axis=0, keepdims=True)
     for h in range(heads):
-        summed = jnp.sum(rows_of(h) * weight[:, :, h : h + 1], axis=0)
-        for z in range(n_z):
-            for i in range(qb):
-                place = pl.ds((z * heads + h) * DH, DH)
-                first = z * own + i * qt
-                out_ref[i, :, place] = summed[first : first + qt].astype(BF)
+        for b in range(qb):
+            lane = b * (DH // qb) + h
+            summed = jnp.sum(rows_of(h * qb + b) * weight[..., lane : lane + 1], axis=0)
+            for z in range(n_z):
+                out_ref[b, :, pl.ds((z * heads + h) * DH, DH)] = summed[z].astype(BF)
 
 
 def call(kernel, out_shape, *args, flops=0, light=False, scratch=(), space=pltpu.VMEM, vmem=VMEM_LIMIT):
@@ -259,7 +259,7 @@
     )
     part = call(
         functools.partial(last_kernel, blocks, tokens, 3),
-        struct((n_y * n_z, (heads + 1) * own, DH), BF),
+        struct((n_y * n_z, heads * qb + 1, qt, DH), BF),
         query_all,
         bias,
         far_low,

time: 101 us -> 100 us (0.990)
  blocking collectives: 62.4 us -> 61.1 us
    all_to_all x1, blocking collectives: 30 us -> 28.8 us  [local(): part = lax.all_to_all(part, ('y', 'head'), 0, 0)]
where the time goes in v5:
time: 100 us; the launch traced here: 99.9 us
  blocking collectives  61.1 us (61%)
  starting transfers between devices  21.6 us (22%)
  Pallas kernels  10.6 us (11%)
  waiting for transfers between devices  5.62 us (6%)
    all_to_all x1, blocking collectives, local(): sorted_ = lax.all_to_all(packed, 'head', 0, 0)  32.4 us
    all_to_all x1, blocking collectives, local(): part = lax.all_to_all(part, ('y', 'head'), 0, 0)  28.8 us
    ppermute x4, starting transfers between devices, shift(): lax.ppermute(block, axis, [(i, (i + by) % count) for i in range(count)])  14.2 us
    pallas_call x8, Pallas kernels, call(): pl.pallas_call(kernel, out_shape=out_shape, in_specs=[pl.BlockSpec(memory...  10.6 us
    all_to_all x1, starting transfers between devices, local(): query_all = lax.all_to_all(query, 'y', 0, 0)  7.43 us
    all_to_all x1, waiting for transfers between devices, local(): query_all = lax.all_to_all(query, 'y', 0, 0)  3.61 us
    ppermute x4, waiting for transfers between devices, shift(): lax.ppermute(block, axis, [(i, (i + by) % count) for i in range(count)])  2.01 us
  transfers between devices with their start and end apart: 5, of which 2 were waited for; matrix products, arithmetic and copies ran while one was open for 1% of the time, Pallas kernels for 5%

profile of v5, /device:TPU:16, one launch (start us, length us, event | category | flops | bytes accessed | tf_op | source)
XLA Modules:
  0.0 99.9 jit_solution(15911856947916072169)
XLA Ops:
  0.0 2.1 %shard_map.55 = bf16[8,5,72,128]{3,2,1,0:T(8,128)(2,1)} custom-call(bf16[2,4,5120]{2,1,0:T(4,128)(2,1)} %q_hbm.1, bf16[2,16,5120]{2,1,0:T(8,128)(2,1)} %k_hbm.1, bf16[2,16,5120]{2,1,0:T(8,128)(2,1)} %v_hbm.1), custom_call_target="tpu_custom_call" | custom-call | bytes 1474560 | tf_op jit(solution)/shard_map/pallas_call | solution.py:172
  2.1 0.0 copy-start.1
  2.1 32.4 %all_to_all.15.sorted_ref = bf16[8,5,72,128]{3,2,1,0:T(8,128)(2,1)S(1)} all-to-all(bf16[8,5,72,128]{3,2,1,0:T(8,128)(2,1)} %shard_map.55), channel_id=1, replica_groups=mesh['cfg'=2,'head'=8,'x'=4,'y'=8] {'head'}, dimensions={0} | all-to-all | bytes 1474560 | tf_op jit(solution)/shard_map/all_to_all | solution.py:214
  34.5 3.4 %collective-permute-start = (bf16[5,2,256,128]{3,2,1,0:T(8,128)(2,1)S(1)}, bf16[5,2,256,128]{3,2,1,0:T(8,128)(2,1)S(1)}, u32[]{:S(2)}, u32[]{:S(2)}) collective-permute-start(bf16[5,2,256,128]{3,2,1,0:T(8,128)(2,1)S(1)} %shard_map.57.refs_0_), channel_id=1, source_target_pairs={{0,8},{8,16},{16,24},{24,0},{1,9},{9,17},{17,25},{25,1},{2,10},{10... | collective-permute-start | bytes 1966088 | tf_op jit(solution)/shard_map/ppermute | solution.py:185
  37.9 0.1 fusion.1
  38.0 0.1 iota_add_fusion
  38.1 0.1 add.61
  38.2 0.0 copy-done.1
  38.2 0.1 iota_compare_fusion
  38.3 3.6 %collective-permute-start.2 = (bf16[5,2,256,128]{3,2,1,0:T(8,128)(2,1)S(1)}, bf16[5,2,256,128]{3,2,1,0:T(8,128)(2,1)S(1)}, u32[]{:S(2)}, u32[]{:S(2)}) collective-permute-start(bf16[5,2,256,128]{3,2,1,0:T(8,128)(2,1)S(1)} %shard_map.57.refs_0_), channel_id=1, source_target_pairs={{0,24},{8,0},{16,8},{24,16},{1,25},{9,1},{17,9},{25,17},{2,26},{10... | collective-permute-start | bytes 1966088 | tf_op jit(solution)/shard_map/ppermute | solution.py:185
  41.9 0.9 shard_map.56
  42.8 7.4 %all-to-all-start.1 = ((bf16[8,5,64,128]{3,2,1,0:T(8,128)(2,1)}), bf16[8,5,64,128]{3,2,1,0:T(8,128)(2,1)S(1)}, u32[]{:S(2)}, u32[]{:S(2)}) async-start(bf16[8,5,64,128]{3,2,1,0:T(8,128)(2,1)} %shard_map.56), calls=%async_computation.1 | async-start | bytes 1310720 | tf_op jit(solution)/shard_map/all_to_all | solution.py:224
  50.3 2.0 %collective-permute-done.pair_ref.refs_1_ = bf16[5,2,256,128]{3,2,1,0:T(8,128)(2,1)S(1)} collective-permute-done((bf16[5,2,256,128]{3,2,1,0:T(8,128)(2,1)S(1)}, bf16[5,2,256,128]{3,2,1,0:T(8,128)(2,1)S(1)}, u32[]{:S(2)}, u32[]{:S(2)}) %collective-permute-start) | collective-permute-done | bytes 655392 | tf_op jit(solution)/shard_map/ppermute | solution.py:185
  52.3 0.8 shard_map.58
  53.0 0.0 copy-start
  53.0 2.3 %collective-permute-start.1 = (bf16[3,2,256,128]{3,2,1,0:T(8,128)(2,1)}, bf16[3,2,256,128]{3,2,1,0:T(8,128)(2,1)S(1)}, u32[]{:S(2)}, u32[]{:S(2)}) collective-permute-start(bf16[3,2,256,128]{3,2,1,0:T(8,128)(2,1)} %shard_map.58), channel_id=1, source_target_pairs={{0,8},{8,16},{16,24},{24,0},{1,9},{9,17},{17,25},{25,1},{2,10},{10... | collective-permute-start | bytes 1179656 | tf_op jit(solution)/shard_map/ppermute | solution.py:185
  55.4 0.0 collective-permute-done.2.pair_ref.refs_2_
  55.4 0.7 shard_map.59
  56.1 4.9 %collective-permute-start.3 = (bf16[2,2,256,128]{3,2,1,0:T(8,128)(2,1)}, bf16[2,2,256,128]{3,2,1,0:T(8,128)(2,1)S(1)}, u32[]{:S(2)}, u32[]{:S(2)}) collective-permute-start(bf16[2,2,256,128]{3,2,1,0:T(8,128)(2,1)} %shard_map.59), channel_id=1, source_target_pairs={{0,24},{8,0},{16,8},{24,16},{1,25},{9,1},{17,9},{25,17},{2,26},{10... | collective-permute-start | bytes 786440 | tf_op jit(solution)/shard_map/ppermute | solution.py:185
  61.0 0.0 copy-done
  61.0 0.4 and_reduce_fusion
  61.4 3.6 %all-to-all-done.1.q_ref = bf16[8,5,64,128]{3,2,1,0:T(8,128)(2,1)S(1)} async-done(((bf16[8,5,64,128]{3,2,1,0:T(8,128)(2,1)}), bf16[8,5,64,128]{3,2,1,0:T(8,128)(2,1)S(1)}, u32[]{:S(2)}, u32[]{:S(2)}) %all-to-all-start.1) | async-done | bytes 655392 | tf_op jit(solution)/shard_map/all_to_all | solution.py:224
  65.0 2.8 %shard_map.60 = (f32[5,512,128]{2,1,0:T(8,128)S(1)}, f32[5,512,128]{2,1,0:T(8,128)S(1)}, f32[5,512,128]{2,1,0:T(8,128)S(1)}) custom-call(bf16[8,5,64,128]{3,2,1,0:T(8,128)(2,1)S(1)} %all-to-all-done.1.q_ref, f32[64,8]{1,0:T(8,128)S(1)} %bitcast.5, bf16[5,2,256,128]{3,2,1,0:T(8,128)(2,1)S(1)} %shard_map.57.refs_0_, ...), custom_call_target="tpu_custom_call" | custom-call | tf_op jit(solution)/shard_map/pallas_call | solution.py:172
  67.8 0.0 collective-permute-done.3.high_ref
  67.8 0.0 collective-permute-done.1.low_ref
  67.9 1.6 %shard_map.61 = bf16[64,11,4,128]{3,2,1,0:T(4,128)(2,1)S(1)} custom-call(bf16[8,5,64,128]{3,2,1,0:T(8,128)(2,1)S(1)} %all-to-all-done.1.q_ref, f32[64,8]{1,0:T(8,128)S(1)} %bitcast.6, bf16[3,2,256,128]{3,2,1,0:T(8,128)(2,1)S(1)} %collective-permute-done.1.low_ref, bf16[2,2,256,128]{3,2,1,0:T(8,128)(2,1)S(1)} %collective-permute-done.3.high_ref, ...), custom_call_target="tpu_custom_call" | custom-call | flops 335544320 | bytes 5965824 | tf_op jit(solution)/shard_map/pallas_call | solution.py:172
  69.5 28.8 %all_to_all.16.part_ref = bf16[64,11,4,128]{3,2,1,0:T(4,128)(2,1)S(1)} all-to-all(bf16[64,11,4,128]{3,2,1,0:T(4,128)(2,1)S(1)} %shard_map.61), channel_id=1, replica_groups=mesh['cfg'=2,'head'=8,'x'=4,'y'=8] {'y','head'}, dimensions={0} | all-to-all | bytes 1441792 | tf_op jit(solution)/shard_map/all_to_all | solution.py:270
  98.2 1.6 %shard_map.62 = bf16[2,4,5120]{2,1,0:T(4,128)(2,1)} custom-call(bf16[64,11,4,128]{3,2,1,0:T(4,128)(2,1)S(1)} %all_to_all.16.part_ref), custom_call_target="tpu_custom_call" | custom-call | bytes 802816 | tf_op jit(solution)/shard_map/pallas_call | solution.py:172
  (3 shorter events, 0.1 us)
Async XLA Ops:
  2.1 36.1 %copy-start.1 = (s32[16]{0:T(128)S(1)}, s32[16]{0:T(128)}, u32[]{:S(2)}) copy-start(s32[16]{0:T(128)} %param.9) | copy-start | bytes 196
  34.5 17.8 %collective-permute-start = (bf16[5,2,256,128]{3,2,1,0:T(8,128)(2,1)S(1)}, bf16[5,2,256,128]{3,2,1,0:T(8,128)(2,1)S(1)}, u32[]{:S(2)}, u32[]{:S(2)}) collective-permute-start(bf16[5,2,256,128]{3,2,1,0:T(8,128)(2,1)S(1)} %shard_map.57.refs_0_), channel_id=1, source_target_pairs={{0,8},{8,16},{16,24},{24,0},{1,9},{9,17},{17,25},{25,1},{2,10},{10... | collective-permute-start | bytes 1966088 | tf_op jit(solution)/shard_map/ppermute | solution.py:185
  38.3 17.1 %collective-permute-start.2 = (bf16[5,2,256,128]{3,2,1,0:T(8,128)(2,1)S(1)}, bf16[5,2,256,128]{3,2,1,0:T(8,128)(2,1)S(1)}, u32[]{:S(2)}, u32[]{:S(2)}) collective-permute-start(bf16[5,2,256,128]{3,2,1,0:T(8,128)(2,1)S(1)} %shard_map.57.refs_0_), channel_id=1, source_target_pairs={{0,24},{8,0},{16,8},{24,16},{1,25},{9,1},{17,9},{25,17},{2,26},{10... | collective-permute-start | bytes 1966088 | tf_op jit(solution)/shard_map/ppermute | solution.py:185
  42.8 22.2 %all-to-all-start.1 = ((bf16[8,5,64,128]{3,2,1,0:T(8,128)(2,1)}), bf16[8,5,64,128]{3,2,1,0:T(8,128)(2,1)S(1)}, u32[]{:S(2)}, u32[]{:S(2)}) async-start(bf16[8,5,64,128]{3,2,1,0:T(8,128)(2,1)} %shard_map.56), calls=%async_computation.1 | async-start | bytes 1310720 | tf_op jit(solution)/shard_map/all_to_all | solution.py:224
  53.0 7.9 %copy-start = (s32[16,32]{1,0:T(8,128)S(1)}, s32[16,32]{1,0:T(8,128)}, u32[]{:S(2)}) copy-start(s32[16,32]{1,0:T(8,128)} %param.8) | copy-start | bytes 6148
  53.0 14.8 %collective-permute-start.1 = (bf16[3,2,256,128]{3,2,1,0:T(8,128)(2,1)}, bf16[3,2,256,128]{3,2,1,0:T(8,128)(2,1)S(1)}, u32[]{:S(2)}, u32[]{:S(2)}) collective-permute-start(bf16[3,2,256,128]{3,2,1,0:T(8,128)(2,1)} %shard_map.58), channel_id=1, source_target_pairs={{0,8},{8,16},{16,24},{24,0},{1,9},{9,17},{17,25},{25,1},{2,10},{10... | collective-permute-start | bytes 1179656 | tf_op jit(solution)/shard_map/ppermute | solution.py:185
  56.1 11.7 %collective-permute-start.3 = (bf16[2,2,256,128]{3,2,1,0:T(8,128)(2,1)}, bf16[2,2,256,128]{3,2,1,0:T(8,128)(2,1)S(1)}, u32[]{:S(2)}, u32[]{:S(2)}) collective-permute-start(bf16[2,2,256,128]{3,2,1,0:T(8,128)(2,1)} %shard_map.59), channel_id=1, source_target_pairs={{0,24},{8,0},{16,8},{24,16},{1,25},{9,1},{17,9},{25,17},{2,26},{10... | collective-permute-start | bytes 786440 | tf_op jit(solution)/shard_map/ppermute | solution.py:185

commit v6 on v5

--- a/solution.py
+++ b/solution.py
@@ -12,7 +12,6 @@
 SCALE = 1.4426950408889634 / DH**0.5
 CLOSED = -1e30
 VMEM_LIMIT = 20 * 1024 * 1024
-STAT_ROWS = 16
 BF = jnp.bfloat16
 F32 = jnp.float32
 
@@ -148,19 +147,21 @@
     qb, qt, _ = out_ref.shape
     heads = part_ref.shape[1] // qb
 
-    def rows_of(item):
-        return part_ref[:, item].astype(F32).reshape(n_from, n_z, qt, DH)
-
-    stats = rows_of(heads * qb)
+    stats = part_ref[:, heads * qb].astype(F32).reshape(n_from, n_z, qt, DH)
     lse = stats + pltpu.roll(stats, DH - heads, 3) + pltpu.roll(stats, DH - 2 * heads, 3)
     weight = jnp.exp(lse - jnp.max(lse, axis=0, keepdims=True))
     weight = weight / jnp.sum(weight, axis=0, keepdims=True)
     for h in range(heads):
-        for b in range(qb):
-            lane = b * (DH // qb) + h
-            summed = jnp.sum(rows_of(h * qb + b) * weight[..., lane : lane + 1], axis=0)
-            for z in range(n_z):
-                out_ref[b, :, pl.ds((z * heads + h) * DH, DH)] = summed[z].astype(BF)
+        summed = jnp.zeros((n_z, qb * qt, DH), F32)
+        for y in range(n_from):
+            lanes = [b * (DH // qb) + h for b in range(qb)]
+            factor = jnp.concatenate([weight[y, :, :, i : i + 1] for i in lanes], axis=1)
+            out = [part_ref[pl.ds(y * n_z, n_z), h * qb + b].astype(F32) for b in range(qb)]
+            summed = summed + jnp.concatenate(out, axis=1) * factor
+        for z in range(n_z):
+            for b in range(qb):
+                rows = summed[z, b * qt : (b + 1) * qt]
+                out_ref[b, :, pl.ds((z * heads + h) * DH, DH)] = rows.astype(BF)
 
 
 def call(kernel, out_shape, *args, flops=0, light=False, scratch=(), space=pltpu.VMEM, vmem=VMEM_LIMIT):

time: 100 us -> 100 us (level)
  no operation moved by 1% of the time
where the time goes in v6:
time: 100 us; the launch traced here: 99.7 us
  blocking collectives  61.1 us (61%)
  starting transfers between devices  21.6 us (22%)
  Pallas kernels  10.4 us (10%)
  waiting for transfers between devices  5.62 us (6%)
    all_to_all x1, blocking collectives, local(): sorted_ = lax.all_to_all(packed, 'head', 0, 0)  32.4 us
    all_to_all x1, blocking collectives, local(): part = lax.all_to_all(part, ('y', 'head'), 0, 0)  28.8 us
    ppermute x4, starting transfers between devices, shift(): lax.ppermute(block, axis, [(i, (i + by) % count) for i in range(count)])  14.2 us
    pallas_call x8, Pallas kernels, call(): pl.pallas_call(kernel, out_shape=out_shape, in_specs=[pl.BlockSpec(memory...  10.4 us
    all_to_all x1, starting transfers between devices, local(): query_all = lax.all_to_all(query, 'y', 0, 0)  7.43 us
    all_to_all x1, waiting for transfers between devices, local(): query_all = lax.all_to_all(query, 'y', 0, 0)  3.61 us
    ppermute x4, waiting for transfers between devices, shift(): lax.ppermute(block, axis, [(i, (i + by) % count) for i in range(count)])  2.01 us
  transfers between devices with their start and end apart: 5, of which 2 were waited for; matrix products, arithmetic and copies ran while one was open for 1% of the time, Pallas kernels for 5%

profile of v6, /device:TPU:16, one launch (start us, length us, event | category | flops | bytes accessed | tf_op | source)
XLA Modules:
  0.0 99.7 jit_solution(4282225261170098909)
XLA Ops:
  0.0 2.1 %shard_map.55 = bf16[8,5,72,128]{3,2,1,0:T(8,128)(2,1)} custom-call(bf16[2,4,5120]{2,1,0:T(4,128)(2,1)} %q_hbm.1, bf16[2,16,5120]{2,1,0:T(8,128)(2,1)} %k_hbm.1, bf16[2,16,5120]{2,1,0:T(8,128)(2,1)} %v_hbm.1), custom_call_target="tpu_custom_call" | custom-call | bytes 1474560 | tf_op jit(solution)/shard_map/pallas_call | solution.py:173
  2.1 0.0 copy-start.1
  2.1 32.4 %all_to_all.15.sorted_ref = bf16[8,5,72,128]{3,2,1,0:T(8,128)(2,1)S(1)} all-to-all(bf16[8,5,72,128]{3,2,1,0:T(8,128)(2,1)} %shard_map.55), channel_id=1, replica_groups=mesh['cfg'=2,'head'=8,'x'=4,'y'=8] {'head'}, dimensions={0} | all-to-all | bytes 1474560 | tf_op jit(solution)/shard_map/all_to_all | solution.py:215
  34.5 3.4 %collective-permute-start = (bf16[5,2,256,128]{3,2,1,0:T(8,128)(2,1)S(1)}, bf16[5,2,256,128]{3,2,1,0:T(8,128)(2,1)S(1)}, u32[]{:S(2)}, u32[]{:S(2)}) collective-permute-start(bf16[5,2,256,128]{3,2,1,0:T(8,128)(2,1)S(1)} %shard_map.57.refs_0_), channel_id=1, source_target_pairs={{0,8},{8,16},{16,24},{24,0},{1,9},{9,17},{17,25},{25,1},{2,10},{10... | collective-permute-start | bytes 1966088 | tf_op jit(solution)/shard_map/ppermute | solution.py:186
  37.9 0.1 fusion.1
  38.0 0.1 iota_add_fusion
  38.1 0.1 add.61
  38.2 0.0 copy-done.1
  38.2 0.1 iota_compare_fusion
  38.3 3.6 %collective-permute-start.2 = (bf16[5,2,256,128]{3,2,1,0:T(8,128)(2,1)S(1)}, bf16[5,2,256,128]{3,2,1,0:T(8,128)(2,1)S(1)}, u32[]{:S(2)}, u32[]{:S(2)}) collective-permute-start(bf16[5,2,256,128]{3,2,1,0:T(8,128)(2,1)S(1)} %shard_map.57.refs_0_), channel_id=1, source_target_pairs={{0,24},{8,0},{16,8},{24,16},{1,25},{9,1},{17,9},{25,17},{2,26},{10... | collective-permute-start | bytes 1966088 | tf_op jit(solution)/shard_map/ppermute | solution.py:186
  41.9 0.9 shard_map.56
  42.8 7.4 %all-to-all-start.1 = ((bf16[8,5,64,128]{3,2,1,0:T(8,128)(2,1)}), bf16[8,5,64,128]{3,2,1,0:T(8,128)(2,1)S(1)}, u32[]{:S(2)}, u32[]{:S(2)}) async-start(bf16[8,5,64,128]{3,2,1,0:T(8,128)(2,1)} %shard_map.56), calls=%async_computation.1 | async-start | bytes 1310720 | tf_op jit(solution)/shard_map/all_to_all | solution.py:225
  50.3 2.0 %collective-permute-done.pair_ref.refs_1_ = bf16[5,2,256,128]{3,2,1,0:T(8,128)(2,1)S(1)} collective-permute-done((bf16[5,2,256,128]{3,2,1,0:T(8,128)(2,1)S(1)}, bf16[5,2,256,128]{3,2,1,0:T(8,128)(2,1)S(1)}, u32[]{:S(2)}, u32[]{:S(2)}) %collective-permute-start) | collective-permute-done | bytes 655392 | tf_op jit(solution)/shard_map/ppermute | solution.py:186
  52.3 0.8 shard_map.58
  53.0 0.0 copy-start
  53.0 2.3 %collective-permute-start.1 = (bf16[3,2,256,128]{3,2,1,0:T(8,128)(2,1)}, bf16[3,2,256,128]{3,2,1,0:T(8,128)(2,1)S(1)}, u32[]{:S(2)}, u32[]{:S(2)}) collective-permute-start(bf16[3,2,256,128]{3,2,1,0:T(8,128)(2,1)} %shard_map.58), channel_id=1, source_target_pairs={{0,8},{8,16},{16,24},{24,0},{1,9},{9,17},{17,25},{25,1},{2,10},{10... | collective-permute-start | bytes 1179656 | tf_op jit(solution)/shard_map/ppermute | solution.py:186
  55.4 0.0 collective-permute-done.2.pair_ref.refs_2_
  55.4 0.7 shard_map.59
  56.1 4.9 %collective-permute-start.3 = (bf16[2,2,256,128]{3,2,1,0:T(8,128)(2,1)}, bf16[2,2,256,128]{3,2,1,0:T(8,128)(2,1)S(1)}, u32[]{:S(2)}, u32[]{:S(2)}) collective-permute-start(bf16[2,2,256,128]{3,2,1,0:T(8,128)(2,1)} %shard_map.59), channel_id=1, source_target_pairs={{0,24},{8,0},{16,8},{24,16},{1,25},{9,1},{17,9},{25,17},{2,26},{10... | collective-permute-start | bytes 786440 | tf_op jit(solution)/shard_map/ppermute | solution.py:186
  61.0 0.0 copy-done
  61.0 0.4 and_reduce_fusion
  61.4 3.6 %all-to-all-done.1.q_ref = bf16[8,5,64,128]{3,2,1,0:T(8,128)(2,1)S(1)} async-done(((bf16[8,5,64,128]{3,2,1,0:T(8,128)(2,1)}), bf16[8,5,64,128]{3,2,1,0:T(8,128)(2,1)S(1)}, u32[]{:S(2)}, u32[]{:S(2)}) %all-to-all-start.1) | async-done | bytes 655392 | tf_op jit(solution)/shard_map/all_to_all | solution.py:225
  65.0 2.8 %shard_map.60 = (f32[5,512,128]{2,1,0:T(8,128)S(1)}, f32[5,512,128]{2,1,0:T(8,128)S(1)}, f32[5,512,128]{2,1,0:T(8,128)S(1)}) custom-call(bf16[8,5,64,128]{3,2,1,0:T(8,128)(2,1)S(1)} %all-to-all-done.1.q_ref, f32[64,8]{1,0:T(8,128)S(1)} %bitcast.5, bf16[5,2,256,128]{3,2,1,0:T(8,128)(2,1)S(1)} %shard_map.57.refs_0_, ...), custom_call_target="tpu_custom_call" | custom-call | tf_op jit(solution)/shard_map/pallas_call | solution.py:173
  67.8 0.0 collective-permute-done.3.high_ref
  67.8 0.0 collective-permute-done.1.low_ref
  67.9 1.6 %shard_map.61 = bf16[64,11,4,128]{3,2,1,0:T(4,128)(2,1)S(1)} custom-call(bf16[8,5,64,128]{3,2,1,0:T(8,128)(2,1)S(1)} %all-to-all-done.1.q_ref, f32[64,8]{1,0:T(8,128)S(1)} %bitcast.6, bf16[3,2,256,128]{3,2,1,0:T(8,128)(2,1)S(1)} %collective-permute-done.1.low_ref, bf16[2,2,256,128]{3,2,1,0:T(8,128)(2,1)S(1)} %collective-permute-done.3.high_ref, ...), custom_call_target="tpu_custom_call" | custom-call | flops 335544320 | bytes 5965824 | tf_op jit(solution)/shard_map/pallas_call | solution.py:173
  69.5 28.8 %all_to_all.16.part_ref = bf16[64,11,4,128]{3,2,1,0:T(4,128)(2,1)S(1)} all-to-all(bf16[64,11,4,128]{3,2,1,0:T(4,128)(2,1)S(1)} %shard_map.61), channel_id=1, replica_groups=mesh['cfg'=2,'head'=8,'x'=4,'y'=8] {'y','head'}, dimensions={0} | all-to-all | bytes 1441792 | tf_op jit(solution)/shard_map/all_to_all | solution.py:271
  98.2 1.4 %shard_map.62 = bf16[2,4,5120]{2,1,0:T(4,128)(2,1)} custom-call(bf16[64,11,4,128]{3,2,1,0:T(4,128)(2,1)S(1)} %all_to_all.16.part_ref), custom_call_target="tpu_custom_call" | custom-call | bytes 802816 | tf_op jit(solution)/shard_map/pallas_call | solution.py:173
  (3 shorter events, 0.1 us)
Async XLA Ops:
  2.1 36.1 %copy-start.1 = (s32[16]{0:T(128)S(1)}, s32[16]{0:T(128)}, u32[]{:S(2)}) copy-start(s32[16]{0:T(128)} %param.9) | copy-start | bytes 196
  34.5 17.8 %collective-permute-start = (bf16[5,2,256,128]{3,2,1,0:T(8,128)(2,1)S(1)}, bf16[5,2,256,128]{3,2,1,0:T(8,128)(2,1)S(1)}, u32[]{:S(2)}, u32[]{:S(2)}) collective-permute-start(bf16[5,2,256,128]{3,2,1,0:T(8,128)(2,1)S(1)} %shard_map.57.refs_0_), channel_id=1, source_target_pairs={{0,8},{8,16},{16,24},{24,0},{1,9},{9,17},{17,25},{25,1},{2,10},{10... | collective-permute-start | bytes 1966088 | tf_op jit(solution)/shard_map/ppermute | solution.py:186
  38.3 17.1 %collective-permute-start.2 = (bf16[5,2,256,128]{3,2,1,0:T(8,128)(2,1)S(1)}, bf16[5,2,256,128]{3,2,1,0:T(8,128)(2,1)S(1)}, u32[]{:S(2)}, u32[]{:S(2)}) collective-permute-start(bf16[5,2,256,128]{3,2,1,0:T(8,128)(2,1)S(1)} %shard_map.57.refs_0_), channel_id=1, source_target_pairs={{0,24},{8,0},{16,8},{24,16},{1,25},{9,1},{17,9},{25,17},{2,26},{10... | collective-permute-start | bytes 1966088 | tf_op jit(solution)/shard_map/ppermute | solution.py:186
  42.8 22.2 %all-to-all-start.1 = ((bf16[8,5,64,128]{3,2,1,0:T(8,128)(2,1)}), bf16[8,5,64,128]{3,2,1,0:T(8,128)(2,1)S(1)}, u32[]{:S(2)}, u32[]{:S(2)}) async-start(bf16[8,5,64,128]{3,2,1,0:T(8,128)(2,1)} %shard_map.56), calls=%async_computation.1 | async-start | bytes 1310720 | tf_op jit(solution)/shard_map/all_to_all | solution.py:225
  53.0 7.9 %copy-start = (s32[16,32]{1,0:T(8,128)S(1)}, s32[16,32]{1,0:T(8,128)}, u32[]{:S(2)}) copy-start(s32[16,32]{1,0:T(8,128)} %param.8) | copy-start | bytes 6148
  53.0 14.8 %collective-permute-start.1 = (bf16[3,2,256,128]{3,2,1,0:T(8,128)(2,1)}, bf16[3,2,256,128]{3,2,1,0:T(8,128)(2,1)S(1)}, u32[]{:S(2)}, u32[]{:S(2)}) collective-permute-start(bf16[3,2,256,128]{3,2,1,0:T(8,128)(2,1)} %shard_map.58), channel_id=1, source_target_pairs={{0,8},{8,16},{16,24},{24,0},{1,9},{9,17},{17,25},{25,1},{2,10},{10... | collective-permute-start | bytes 1179656 | tf_op jit(solution)/shard_map/ppermute | solution.py:186
  56.1 11.7 %collective-permute-start.3 = (bf16[2,2,256,128]{3,2,1,0:T(8,128)(2,1)}, bf16[2,2,256,128]{3,2,1,0:T(8,128)(2,1)S(1)}, u32[]{:S(2)}, u32[]{:S(2)}) collective-permute-start(bf16[2,2,256,128]{3,2,1,0:T(8,128)(2,1)} %shard_map.59), channel_id=1, source_target_pairs={{0,24},{8,0},{16,8},{24,16},{1,25},{9,1},{17,9},{25,17},{2,26},{10... | collective-permute-start | bytes 786440 | tf_op jit(solution)/shard_map/ppermute | solution.py:186

commit v7 on v6

--- a/solution.py
+++ b/solution.py
@@ -63,8 +63,10 @@
             q_ref[to, h] = query
 
 
-def take_kernel(first, pair_ref, out_ref):
-    out_ref[...] = pair_ref[pl.ds(first, out_ref.shape[0])]
+def take_kernel(first, pair_ref, out_hbm, sem):
+    copy = pltpu.make_async_copy(pair_ref.at[pl.ds(first, out_hbm.shape[0])], out_hbm, sem.at[0])
+    copy.start()
+    copy.wait()
 
 
 def block_bias(bias_ref, piece, blocks, tokens, keys):
@@ -115,6 +117,12 @@
     n_dest, parts, qt, _ = out_ref.shape
     qb = parts // heads
     own = qb * qt
+
+    def in_place(item):
+        item = item.reshape(n_to, n_dest // n_to, own, DH)
+        item = jnp.stack([item[n_to - 1 - y] for y in range(n_to)])
+        return item.reshape(n_dest, own, DH)
+
     for h in range(heads):
         cut = low_ref.shape[0]
         pair = low_ref.at[h] if h < cut else high_ref.at[h - cut]
@@ -125,7 +133,7 @@
         both = weigh(scores, jnp.concatenate([top] * (keys // DH), axis=1), pair[1])
         total = total_ref[h] * fade + both[:, DH:]
         out = (sum_ref[h] * fade + both[:, :DH]) / total
-        out = out.reshape(n_dest, own, DH)
+        out = in_place(out)
         for b in range(qb):
             out_ref[:, h * qb + b] = out[:, b * qt : (b + 1) * qt].astype(BF)
         tops = jnp.where(lane == h, top, tops)
@@ -135,7 +143,7 @@
     rest = lse - high
     middle = rest.astype(BF).astype(F32)
     stats = high + pltpu.roll(middle, heads, 1) + pltpu.roll(rest - middle, 2 * heads, 1)
-    stats = stats.reshape(n_dest, own, DH)
+    stats = in_place(stats)
     joined = stats[:, :qt]
     for b in range(1, qb):
         joined = joined + pltpu.roll(stats, b * (DH // qb), 2)[:, b * qt : (b + 1) * qt]
@@ -164,8 +172,8 @@
                 out_ref[b, :, pl.ds((z * heads + h) * DH, DH)] = rows.astype(BF)
 
 
-def call(kernel, out_shape, *args, flops=0, light=False, scratch=(), space=pltpu.VMEM, vmem=VMEM_LIMIT):
-    whole = pl.BlockSpec(memory_space=pltpu.VMEM)
+def call(kernel, out_shape, *args, flops=0, light=False, scratch=(), space=pltpu.VMEM, out_space=pltpu.VMEM, vmem=VMEM_LIMIT):
+    whole = pl.BlockSpec(memory_space=out_space)
     size = sum(a.size * a.dtype.itemsize for a in args)
     size += sum(o.size * o.dtype.itemsize for o in jax.tree.leaves(out_shape))
     if light:
@@ -222,7 +230,7 @@
 
     pair_left = shift(kv, "x", 1)
     pair_right = shift(kv, "x", -1)
-    query_all = lax.all_to_all(query, "y", 0, 0)
+    query_all = lax.all_to_all(query, "y", 0, 0, axis_index_groups=[list(range(n_y))[::-1]])
     cut = (heads + 1) // 2
     far_low, far_high = (
         shift(
@@ -231,6 +239,8 @@
                 struct((count,) + kv.shape[1:], BF),
                 pair,
                 flops=2 * 10**10,
+                scratch=[pltpu.SemaphoreType.DMA((1,))],
+                out_space=pltpu.HBM,
             ),
             "x",
             by,

time: 100 us -> 99.9 us (level)
  waiting for transfers between devices: 5.62 us -> 4.45 us
  blocking collectives: 61.1 us -> 62.2 us
    all_to_all x1, waiting for transfers between devices: 3.61 us -> 2.44 us  [local(): lax.all_to_all(query, 'y', 0, 0, axis_index_groups=[list(range(n_y))[::-1]])]
    all_to_all x1, blocking collectives: 28.8 us -> 29.8 us  [local(): part = lax.all_to_all(part, ('y', 'head'), 0, 0)]
where the time goes in v7:
time: 99.9 us; the launch traced here: 99.5 us
  blocking collectives  62.2 us (62%)
  starting transfers between devices  21.5 us (22%)
  Pallas kernels  10.4 us (10%)
  waiting for transfers between devices  4.45 us (4%)
    all_to_all x1, blocking collectives, local(): sorted_ = lax.all_to_all(packed, 'head', 0, 0)  32.4 us
    all_to_all x1, blocking collectives, local(): part = lax.all_to_all(part, ('y', 'head'), 0, 0)  29.8 us
    ppermute x4, starting transfers between devices, shift(): lax.ppermute(block, axis, [(i, (i + by) % count) for i in range(count)])  14.1 us
    pallas_call x8, Pallas kernels, call(): pl.pallas_call(kernel, out_shape=out_shape, in_specs=[pl.BlockSpec(memory...  10.4 us
    all_to_all x1, starting transfers between devices, local(): lax.all_to_all(query, 'y', 0, 0, axis_index_groups=[list(range(n_y))[::-1]])  7.43 us
    all_to_all x1, waiting for transfers between devices, local(): lax.all_to_all(query, 'y', 0, 0, axis_index_groups=[list(range(n_y))[::-1]])  2.44 us
    ppermute x4, waiting for transfers between devices, shift(): lax.ppermute(block, axis, [(i, (i + by) % count) for i in range(count)])  2.01 us
  transfers between devices with their start and end apart: 5, of which 2 were waited for; matrix products, arithmetic and copies ran while one was open for 1% of the time, Pallas kernels for 5%

profile of v7, /device:TPU:16, one launch (start us, length us, event | category | flops | bytes accessed | tf_op | source)
XLA Modules:
  0.0 99.5 jit_solution(3063917710937823336)
XLA Ops:
  0.0 2.1 %shard_map.55 = bf16[8,5,72,128]{3,2,1,0:T(8,128)(2,1)} custom-call(bf16[2,4,5120]{2,1,0:T(4,128)(2,1)} %q_hbm.1, bf16[2,16,5120]{2,1,0:T(8,128)(2,1)} %k_hbm.1, bf16[2,16,5120]{2,1,0:T(8,128)(2,1)} %v_hbm.1), custom_call_target="tpu_custom_call" | custom-call | bytes 1474560 | tf_op jit(solution)/shard_map/pallas_call | solution.py:181
  2.1 0.0 copy-start.1
  2.1 32.4 %all_to_all.15.sorted_ref = bf16[8,5,72,128]{3,2,1,0:T(8,128)(2,1)S(1)} all-to-all(bf16[8,5,72,128]{3,2,1,0:T(8,128)(2,1)} %shard_map.55), channel_id=1, replica_groups=mesh['cfg'=2,'head'=8,'x'=4,'y'=8] {'head'}, dimensions={0} | all-to-all | bytes 1474560 | tf_op jit(solution)/shard_map/all_to_all | solution.py:223
  34.5 3.4 %collective-permute-start = (bf16[5,2,256,128]{3,2,1,0:T(8,128)(2,1)S(1)}, bf16[5,2,256,128]{3,2,1,0:T(8,128)(2,1)S(1)}, u32[]{:S(2)}, u32[]{:S(2)}) collective-permute-start(bf16[5,2,256,128]{3,2,1,0:T(8,128)(2,1)S(1)} %shard_map.57.refs_0_), channel_id=1, source_target_pairs={{0,8},{8,16},{16,24},{24,0},{1,9},{9,17},{17,25},{25,1},{2,10},{10... | collective-permute-start | bytes 1966088 | tf_op jit(solution)/shard_map/ppermute | solution.py:194
  37.9 0.1 fusion.1
  38.0 0.1 iota_add_fusion
  38.1 0.1 add.61
  38.2 0.0 copy-done.1
  38.2 0.1 iota_compare_fusion
  38.3 3.6 %collective-permute-start.2 = (bf16[5,2,256,128]{3,2,1,0:T(8,128)(2,1)S(1)}, bf16[5,2,256,128]{3,2,1,0:T(8,128)(2,1)S(1)}, u32[]{:S(2)}, u32[]{:S(2)}) collective-permute-start(bf16[5,2,256,128]{3,2,1,0:T(8,128)(2,1)S(1)} %shard_map.57.refs_0_), channel_id=1, source_target_pairs={{0,24},{8,0},{16,8},{24,16},{1,25},{9,1},{17,9},{25,17},{2,26},{10... | collective-permute-start | bytes 1966088 | tf_op jit(solution)/shard_map/ppermute | solution.py:194
  41.9 0.9 shard_map.56
  42.8 7.4 %all-to-all-start.1 = ((bf16[8,5,64,128]{3,2,1,0:T(8,128)(2,1)}), bf16[8,5,64,128]{3,2,1,0:T(8,128)(2,1)S(1)}, u32[]{:S(2)}, u32[]{:S(2)}) async-start(bf16[8,5,64,128]{3,2,1,0:T(8,128)(2,1)} %shard_map.56), calls=%async_computation.1 | async-start | bytes 1310720 | tf_op jit(solution)/shard_map/all_to_all | solution.py:233
  50.3 2.0 %collective-permute-done.pair_ref.refs_1_ = bf16[5,2,256,128]{3,2,1,0:T(8,128)(2,1)S(1)} collective-permute-done((bf16[5,2,256,128]{3,2,1,0:T(8,128)(2,1)S(1)}, bf16[5,2,256,128]{3,2,1,0:T(8,128)(2,1)S(1)}, u32[]{:S(2)}, u32[]{:S(2)}) %collective-permute-start) | collective-permute-done | bytes 655392 | tf_op jit(solution)/shard_map/ppermute | solution.py:194
  52.3 0.8 shard_map.58
  53.0 0.0 copy-start
  53.0 2.2 %collective-permute-start.1 = (bf16[3,2,256,128]{3,2,1,0:T(8,128)(2,1)}, bf16[3,2,256,128]{3,2,1,0:T(8,128)(2,1)S(1)}, u32[]{:S(2)}, u32[]{:S(2)}) collective-permute-start(bf16[3,2,256,128]{3,2,1,0:T(8,128)(2,1)} %shard_map.58), channel_id=1, source_target_pairs={{0,8},{8,16},{16,24},{24,0},{1,9},{9,17},{17,25},{25,1},{2,10},{10... | collective-permute-start | bytes 1179656 | tf_op jit(solution)/shard_map/ppermute | solution.py:194
  55.2 0.0 collective-permute-done.2.pair_ref.refs_2_
  55.3 0.7 shard_map.59
  56.0 4.9 %collective-permute-start.3 = (bf16[2,2,256,128]{3,2,1,0:T(8,128)(2,1)}, bf16[2,2,256,128]{3,2,1,0:T(8,128)(2,1)S(1)}, u32[]{:S(2)}, u32[]{:S(2)}) collective-permute-start(bf16[2,2,256,128]{3,2,1,0:T(8,128)(2,1)} %shard_map.59), channel_id=1, source_target_pairs={{0,24},{8,0},{16,8},{24,16},{1,25},{9,1},{17,9},{25,17},{2,26},{10... | collective-permute-start | bytes 786440 | tf_op jit(solution)/shard_map/ppermute | solution.py:194
  60.9 0.0 copy-done
  60.9 0.4 and_reduce_fusion
  61.3 2.4 %all-to-all-done.1.q_ref = bf16[8,5,64,128]{3,2,1,0:T(8,128)(2,1)S(1)} async-done(((bf16[8,5,64,128]{3,2,1,0:T(8,128)(2,1)}), bf16[8,5,64,128]{3,2,1,0:T(8,128)(2,1)S(1)}, u32[]{:S(2)}, u32[]{:S(2)}) %all-to-all-start.1) | async-done | bytes 655392 | tf_op jit(solution)/shard_map/all_to_all | solution.py:233
  63.7 2.8 %shard_map.60 = (f32[5,512,128]{2,1,0:T(8,128)S(1)}, f32[5,512,128]{2,1,0:T(8,128)S(1)}, f32[5,512,128]{2,1,0:T(8,128)S(1)}) custom-call(bf16[8,5,64,128]{3,2,1,0:T(8,128)(2,1)S(1)} %all-to-all-done.1.q_ref, f32[64,8]{1,0:T(8,128)S(1)} %bitcast.5, bf16[5,2,256,128]{3,2,1,0:T(8,128)(2,1)S(1)} %shard_map.57.refs_0_, ...), custom_call_target="tpu_custom_call" | custom-call | tf_op jit(solution)/shard_map/pallas_call | solution.py:181
  66.6 0.0 collective-permute-done.3.high_ref
  66.6 0.0 collective-permute-done.1.low_ref
  66.6 1.6 %shard_map.61 = bf16[64,11,4,128]{3,2,1,0:T(4,128)(2,1)S(1)} custom-call(bf16[8,5,64,128]{3,2,1,0:T(8,128)(2,1)S(1)} %all-to-all-done.1.q_ref, f32[64,8]{1,0:T(8,128)S(1)} %bitcast.6, bf16[3,2,256,128]{3,2,1,0:T(8,128)(2,1)S(1)} %collective-permute-done.1.low_ref, bf16[2,2,256,128]{3,2,1,0:T(8,128)(2,1)S(1)} %collective-permute-done.3.high_ref, ...), custom_call_target="tpu_custom_call" | custom-call | flops 335544320 | bytes 5965824 | tf_op jit(solution)/shard_map/pallas_call | solution.py:181
  68.2 29.8 %all_to_all.16.part_ref = bf16[64,11,4,128]{3,2,1,0:T(4,128)(2,1)S(1)} all-to-all(bf16[64,11,4,128]{3,2,1,0:T(4,128)(2,1)S(1)} %shard_map.61), channel_id=1, replica_groups=mesh['cfg'=2,'head'=8,'x'=4,'y'=8] {'y','head'}, dimensions={0} | all-to-all | bytes 1441792 | tf_op jit(solution)/shard_map/all_to_all | solution.py:281
  98.0 1.4 %shard_map.62 = bf16[2,4,5120]{2,1,0:T(4,128)(2,1)} custom-call(bf16[64,11,4,128]{3,2,1,0:T(4,128)(2,1)S(1)} %all_to_all.16.part_ref), custom_call_target="tpu_custom_call" | custom-call | bytes 802816 | tf_op jit(solution)/shard_map/pallas_call | solution.py:181
  (3 shorter events, 0.1 us)
Async XLA Ops:
  2.1 36.1 %copy-start.1 = (s32[16]{0:T(128)S(1)}, s32[16]{0:T(128)}, u32[]{:S(2)}) copy-start(s32[16]{0:T(128)} %param.9) | copy-start | bytes 196
  34.5 17.8 %collective-permute-start = (bf16[5,2,256,128]{3,2,1,0:T(8,128)(2,1)S(1)}, bf16[5,2,256,128]{3,2,1,0:T(8,128)(2,1)S(1)}, u32[]{:S(2)}, u32[]{:S(2)}) collective-permute-start(bf16[5,2,256,128]{3,2,1,0:T(8,128)(2,1)S(1)} %shard_map.57.refs_0_), channel_id=1, source_target_pairs={{0,8},{8,16},{16,24},{24,0},{1,9},{9,17},{17,25},{25,1},{2,10},{10... | collective-permute-start | bytes 1966088 | tf_op jit(solution)/shard_map/ppermute | solution.py:194
  38.3 17.0 %collective-permute-start.2 = (bf16[5,2,256,128]{3,2,1,0:T(8,128)(2,1)S(1)}, bf16[5,2,256,128]{3,2,1,0:T(8,128)(2,1)S(1)}, u32[]{:S(2)}, u32[]{:S(2)}) collective-permute-start(bf16[5,2,256,128]{3,2,1,0:T(8,128)(2,1)S(1)} %shard_map.57.refs_0_), channel_id=1, source_target_pairs={{0,24},{8,0},{16,8},{24,16},{1,25},{9,1},{17,9},{25,17},{2,26},{10... | collective-permute-start | bytes 1966088 | tf_op jit(solution)/shard_map/ppermute | solution.py:194
  42.8 20.9 %all-to-all-start.1 = ((bf16[8,5,64,128]{3,2,1,0:T(8,128)(2,1)}), bf16[8,5,64,128]{3,2,1,0:T(8,128)(2,1)S(1)}, u32[]{:S(2)}, u32[]{:S(2)}) async-start(bf16[8,5,64,128]{3,2,1,0:T(8,128)(2,1)} %shard_map.56), calls=%async_computation.1 | async-start | bytes 1310720 | tf_op jit(solution)/shard_map/all_to_all | solution.py:233
  53.0 7.8 %copy-start = (s32[16,32]{1,0:T(8,128)S(1)}, s32[16,32]{1,0:T(8,128)}, u32[]{:S(2)}) copy-start(s32[16,32]{1,0:T(8,128)} %param.8) | copy-start | bytes 6148
  53.0 13.5 %collective-permute-start.1 = (bf16[3,2,256,128]{3,2,1,0:T(8,128)(2,1)}, bf16[3,2,256,128]{3,2,1,0:T(8,128)(2,1)S(1)}, u32[]{:S(2)}, u32[]{:S(2)}) collective-permute-start(bf16[3,2,256,128]{3,2,1,0:T(8,128)(2,1)} %shard_map.58), channel_id=1, source_target_pairs={{0,8},{8,16},{16,24},{24,0},{1,9},{9,17},{17,25},{25,1},{2,10},{10... | collective-permute-start | bytes 1179656 | tf_op jit(solution)/shard_map/ppermute | solution.py:194
  56.0 10.6 %collective-permute-start.3 = (bf16[2,2,256,128]{3,2,1,0:T(8,128)(2,1)}, bf16[2,2,256,128]{3,2,1,0:T(8,128)(2,1)S(1)}, u32[]{:S(2)}, u32[]{:S(2)}) collective-permute-start(bf16[2,2,256,128]{3,2,1,0:T(8,128)(2,1)} %shard_map.59), channel_id=1, source_target_pairs={{0,24},{8,0},{16,8},{24,16},{1,25},{9,1},{17,9},{25,17},{2,26},{10... | collective-permute-start | bytes 786440 | tf_op jit(solution)/shard_map/ppermute | solution.py:194

commit v8 on v7

--- a/solution.py
+++ b/solution.py
@@ -132,7 +132,9 @@
         fade = jnp.exp2((before - top) * SCALE)
         both = weigh(scores, jnp.concatenate([top] * (keys // DH), axis=1), pair[1])
         total = total_ref[h] * fade + both[:, DH:]
-        out = (sum_ref[h] * fade + both[:, :DH]) / total
+        inverse = pl.reciprocal(total, approx=True)
+        inverse = inverse * (2.0 - total * inverse)
+        out = (sum_ref[h] * fade + both[:, :DH]) * inverse
         out = in_place(out)
         for b in range(qb):
             out_ref[:, h * qb + b] = out[:, b * qt : (b + 1) * qt].astype(BF)
@@ -158,7 +160,7 @@
     stats = part_ref[:, heads * qb].astype(F32).reshape(n_from, n_z, qt, DH)
     lse = stats + pltpu.roll(stats, DH - heads, 3) + pltpu.roll(stats, DH - 2 * heads, 3)
     weight = jnp.exp(lse - jnp.max(lse, axis=0, keepdims=True))
-    weight = weight / jnp.sum(weight, axis=0, keepdims=True)
+    weight = weight * (1.0 / jnp.sum(weight, axis=0, keepdims=True))
     for h in range(heads):
         summed = jnp.zeros((n_z, qb * qt, DH), F32)
         for y in range(n_from):

time: 99.9 us -> 100 us (level)
  no operation moved by 1% of the time
where the time goes in v8:
time: 100 us; the launch traced here: 99.6 us
  blocking collectives  62.2 us (62%)
  starting transfers between devices  21.5 us (22%)
  Pallas kernels  10.5 us (10%)
  waiting for transfers between devices  4.45 us (4%)
    all_to_all x1, blocking collectives, local(): sorted_ = lax.all_to_all(packed, 'head', 0, 0)  32.4 us
    all_to_all x1, blocking collectives, local(): part = lax.all_to_all(part, ('y', 'head'), 0, 0)  29.8 us
    ppermute x4, starting transfers between devices, shift(): lax.ppermute(block, axis, [(i, (i + by) % count) for i in range(count)])  14.1 us
    pallas_call x8, Pallas kernels, call(): pl.pallas_call(kernel, out_shape=out_shape, in_specs=[pl.BlockSpec(memory...  10.5 us
    all_to_all x1, starting transfers between devices, local(): lax.all_to_all(query, 'y', 0, 0, axis_index_groups=[list(range(n_y))[::-1]])  7.43 us
    all_to_all x1, waiting for transfers between devices, local(): lax.all_to_all(query, 'y', 0, 0, axis_index_groups=[list(range(n_y))[::-1]])  2.44 us
    ppermute x4, waiting for transfers between devices, shift(): lax.ppermute(block, axis, [(i, (i + by) % count) for i in range(count)])  2.01 us
  transfers between devices with their start and end apart: 5, of which 2 were waited for; matrix products, arithmetic and copies ran while one was open for 1% of the time, Pallas kernels for 5%

profile of v8, /device:TPU:16, one launch (start us, length us, event | category | flops | bytes accessed | tf_op | source)
XLA Modules:
  0.0 99.6 jit_solution(12840302717457523332)
XLA Ops:
  0.0 2.1 %shard_map.55 = bf16[8,5,72,128]{3,2,1,0:T(8,128)(2,1)} custom-call(bf16[2,4,5120]{2,1,0:T(4,128)(2,1)} %q_hbm.1, bf16[2,16,5120]{2,1,0:T(8,128)(2,1)} %k_hbm.1, bf16[2,16,5120]{2,1,0:T(8,128)(2,1)} %v_hbm.1), custom_call_target="tpu_custom_call" | custom-call | bytes 1474560 | tf_op jit(solution)/shard_map/pallas_call | solution.py:183
  2.1 0.0 copy-start.1
  2.1 32.4 %all_to_all.15.sorted_ref = bf16[8,5,72,128]{3,2,1,0:T(8,128)(2,1)S(1)} all-to-all(bf16[8,5,72,128]{3,2,1,0:T(8,128)(2,1)} %shard_map.55), channel_id=1, replica_groups=mesh['cfg'=2,'head'=8,'x'=4,'y'=8] {'head'}, dimensions={0} | all-to-all | bytes 1474560 | tf_op jit(solution)/shard_map/all_to_all | solution.py:225
  34.5 3.4 %collective-permute-start = (bf16[5,2,256,128]{3,2,1,0:T(8,128)(2,1)S(1)}, bf16[5,2,256,128]{3,2,1,0:T(8,128)(2,1)S(1)}, u32[]{:S(2)}, u32[]{:S(2)}) collective-permute-start(bf16[5,2,256,128]{3,2,1,0:T(8,128)(2,1)S(1)} %shard_map.57.refs_0_), channel_id=1, source_target_pairs={{0,8},{8,16},{16,24},{24,0},{1,9},{9,17},{17,25},{25,1},{2,10},{10... | collective-permute-start | bytes 1966088 | tf_op jit(solution)/shard_map/ppermute | solution.py:196
  37.9 0.1 fusion.1
  38.0 0.1 iota_add_fusion
  38.1 0.1 add.61
  38.2 0.0 copy-done.1
  38.2 0.1 iota_compare_fusion
  38.3 3.6 %collective-permute-start.2 = (bf16[5,2,256,128]{3,2,1,0:T(8,128)(2,1)S(1)}, bf16[5,2,256,128]{3,2,1,0:T(8,128)(2,1)S(1)}, u32[]{:S(2)}, u32[]{:S(2)}) collective-permute-start(bf16[5,2,256,128]{3,2,1,0:T(8,128)(2,1)S(1)} %shard_map.57.refs_0_), channel_id=1, source_target_pairs={{0,24},{8,0},{16,8},{24,16},{1,25},{9,1},{17,9},{25,17},{2,26},{10... | collective-permute-start | bytes 1966088 | tf_op jit(solution)/shard_map/ppermute | solution.py:196
  41.9 0.9 shard_map.56
  42.8 7.4 %all-to-all-start.1 = ((bf16[8,5,64,128]{3,2,1,0:T(8,128)(2,1)}), bf16[8,5,64,128]{3,2,1,0:T(8,128)(2,1)S(1)}, u32[]{:S(2)}, u32[]{:S(2)}) async-start(bf16[8,5,64,128]{3,2,1,0:T(8,128)(2,1)} %shard_map.56), calls=%async_computation.1 | async-start | bytes 1310720 | tf_op jit(solution)/shard_map/all_to_all | solution.py:235
  50.3 2.0 %collective-permute-done.pair_ref.refs_1_ = bf16[5,2,256,128]{3,2,1,0:T(8,128)(2,1)S(1)} collective-permute-done((bf16[5,2,256,128]{3,2,1,0:T(8,128)(2,1)S(1)}, bf16[5,2,256,128]{3,2,1,0:T(8,128)(2,1)S(1)}, u32[]{:S(2)}, u32[]{:S(2)}) %collective-permute-start) | collective-permute-done | bytes 655392 | tf_op jit(solution)/shard_map/ppermute | solution.py:196
  52.3 0.8 shard_map.58
  53.0 0.0 copy-start
  53.0 2.2 %collective-permute-start.1 = (bf16[3,2,256,128]{3,2,1,0:T(8,128)(2,1)}, bf16[3,2,256,128]{3,2,1,0:T(8,128)(2,1)S(1)}, u32[]{:S(2)}, u32[]{:S(2)}) collective-permute-start(bf16[3,2,256,128]{3,2,1,0:T(8,128)(2,1)} %shard_map.58), channel_id=1, source_target_pairs={{0,8},{8,16},{16,24},{24,0},{1,9},{9,17},{17,25},{25,1},{2,10},{10... | collective-permute-start | bytes 1179656 | tf_op jit(solution)/shard_map/ppermute | solution.py:196
  55.2 0.0 collective-permute-done.2.pair_ref.refs_2_
  55.3 0.7 shard_map.59
  56.0 4.9 %collective-permute-start.3 = (bf16[2,2,256,128]{3,2,1,0:T(8,128)(2,1)}, bf16[2,2,256,128]{3,2,1,0:T(8,128)(2,1)S(1)}, u32[]{:S(2)}, u32[]{:S(2)}) collective-permute-start(bf16[2,2,256,128]{3,2,1,0:T(8,128)(2,1)} %shard_map.59), channel_id=1, source_target_pairs={{0,24},{8,0},{16,8},{24,16},{1,25},{9,1},{17,9},{25,17},{2,26},{10... | collective-permute-start | bytes 786440 | tf_op jit(solution)/shard_map/ppermute | solution.py:196
  60.9 0.0 copy-done
  60.9 0.4 and_reduce_fusion
  61.3 2.4 %all-to-all-done.1.q_ref = bf16[8,5,64,128]{3,2,1,0:T(8,128)(2,1)S(1)} async-done(((bf16[8,5,64,128]{3,2,1,0:T(8,128)(2,1)}), bf16[8,5,64,128]{3,2,1,0:T(8,128)(2,1)S(1)}, u32[]{:S(2)}, u32[]{:S(2)}) %all-to-all-start.1) | async-done | bytes 655392 | tf_op jit(solution)/shard_map/all_to_all | solution.py:235
  63.7 2.8 %shard_map.60 = (f32[5,512,128]{2,1,0:T(8,128)S(1)}, f32[5,512,128]{2,1,0:T(8,128)S(1)}, f32[5,512,128]{2,1,0:T(8,128)S(1)}) custom-call(bf16[8,5,64,128]{3,2,1,0:T(8,128)(2,1)S(1)} %all-to-all-done.1.q_ref, f32[64,8]{1,0:T(8,128)S(1)} %bitcast.5, bf16[5,2,256,128]{3,2,1,0:T(8,128)(2,1)S(1)} %shard_map.57.refs_0_, ...), custom_call_target="tpu_custom_call" | custom-call | tf_op jit(solution)/shard_map/pallas_call | solution.py:183
  66.6 0.0 collective-permute-done.3.high_ref
  66.6 0.0 collective-permute-done.1.low_ref
  66.6 1.7 %shard_map.61 = bf16[64,11,4,128]{3,2,1,0:T(4,128)(2,1)S(1)} custom-call(bf16[8,5,64,128]{3,2,1,0:T(8,128)(2,1)S(1)} %all-to-all-done.1.q_ref, f32[64,8]{1,0:T(8,128)S(1)} %bitcast.6, bf16[3,2,256,128]{3,2,1,0:T(8,128)(2,1)S(1)} %collective-permute-done.1.low_ref, bf16[2,2,256,128]{3,2,1,0:T(8,128)(2,1)S(1)} %collective-permute-done.3.high_ref, ...), custom_call_target="tpu_custom_call" | custom-call | flops 335544320 | bytes 5965824 | tf_op jit(solution)/shard_map/pallas_call | solution.py:183
  68.3 29.8 %all_to_all.16.part_ref = bf16[64,11,4,128]{3,2,1,0:T(4,128)(2,1)S(1)} all-to-all(bf16[64,11,4,128]{3,2,1,0:T(4,128)(2,1)S(1)} %shard_map.61), channel_id=1, replica_groups=mesh['cfg'=2,'head'=8,'x'=4,'y'=8] {'y','head'}, dimensions={0} | all-to-all | bytes 1441792 | tf_op jit(solution)/shard_map/all_to_all | solution.py:283
  98.1 1.4 %shard_map.62 = bf16[2,4,5120]{2,1,0:T(4,128)(2,1)} custom-call(bf16[64,11,4,128]{3,2,1,0:T(4,128)(2,1)S(1)} %all_to_all.16.part_ref), custom_call_target="tpu_custom_call" | custom-call | bytes 802816 | tf_op jit(solution)/shard_map/pallas_call | solution.py:183
  (3 shorter events, 0.1 us)
Async XLA Ops:
  2.1 36.1 %copy-start.1 = (s32[16]{0:T(128)S(1)}, s32[16]{0:T(128)}, u32[]{:S(2)}) copy-start(s32[16]{0:T(128)} %param.9) | copy-start | bytes 196
  34.5 17.8 %collective-permute-start = (bf16[5,2,256,128]{3,2,1,0:T(8,128)(2,1)S(1)}, bf16[5,2,256,128]{3,2,1,0:T(8,128)(2,1)S(1)}, u32[]{:S(2)}, u32[]{:S(2)}) collective-permute-start(bf16[5,2,256,128]{3,2,1,0:T(8,128)(2,1)S(1)} %shard_map.57.refs_0_), channel_id=1, source_target_pairs={{0,8},{8,16},{16,24},{24,0},{1,9},{9,17},{17,25},{25,1},{2,10},{10... | collective-permute-start | bytes 1966088 | tf_op jit(solution)/shard_map/ppermute | solution.py:196
  38.3 17.0 %collective-permute-start.2 = (bf16[5,2,256,128]{3,2,1,0:T(8,128)(2,1)S(1)}, bf16[5,2,256,128]{3,2,1,0:T(8,128)(2,1)S(1)}, u32[]{:S(2)}, u32[]{:S(2)}) collective-permute-start(bf16[5,2,256,128]{3,2,1,0:T(8,128)(2,1)S(1)} %shard_map.57.refs_0_), channel_id=1, source_target_pairs={{0,24},{8,0},{16,8},{24,16},{1,25},{9,1},{17,9},{25,17},{2,26},{10... | collective-permute-start | bytes 1966088 | tf_op jit(solution)/shard_map/ppermute | solution.py:196
  42.8 20.9 %all-to-all-start.1 = ((bf16[8,5,64,128]{3,2,1,0:T(8,128)(2,1)}), bf16[8,5,64,128]{3,2,1,0:T(8,128)(2,1)S(1)}, u32[]{:S(2)}, u32[]{:S(2)}) async-start(bf16[8,5,64,128]{3,2,1,0:T(8,128)(2,1)} %shard_map.56), calls=%async_computation.1 | async-start | bytes 1310720 | tf_op jit(solution)/shard_map/all_to_all | solution.py:235
  53.0 7.8 %copy-start = (s32[16,32]{1,0:T(8,128)S(1)}, s32[16,32]{1,0:T(8,128)}, u32[]{:S(2)}) copy-start(s32[16,32]{1,0:T(8,128)} %param.8) | copy-start | bytes 6148
  53.0 13.5 %collective-permute-start.1 = (bf16[3,2,256,128]{3,2,1,0:T(8,128)(2,1)}, bf16[3,2,256,128]{3,2,1,0:T(8,128)(2,1)S(1)}, u32[]{:S(2)}, u32[]{:S(2)}) collective-permute-start(bf16[3,2,256,128]{3,2,1,0:T(8,128)(2,1)} %shard_map.58), channel_id=1, source_target_pairs={{0,8},{8,16},{16,24},{24,0},{1,9},{9,17},{17,25},{25,1},{2,10},{10... | collective-permute-start | bytes 1179656 | tf_op jit(solution)/shard_map/ppermute | solution.py:196
  56.0 10.6 %collective-permute-start.3 = (bf16[2,2,256,128]{3,2,1,0:T(8,128)(2,1)}, bf16[2,2,256,128]{3,2,1,0:T(8,128)(2,1)S(1)}, u32[]{:S(2)}, u32[]{:S(2)}) collective-permute-start(bf16[2,2,256,128]{3,2,1,0:T(8,128)(2,1)} %shard_map.59), channel_id=1, source_target_pairs={{0,24},{8,0},{16,8},{24,16},{1,25},{9,1},{17,9},{25,17},{2,26},{10... | collective-permute-start | bytes 786440 | tf_op jit(solution)/shard_map/ppermute | solution.py:196

commit v9 on v7

--- a/solution.py
+++ b/solution.py
@@ -118,11 +118,6 @@
     qb = parts // heads
     own = qb * qt
 
-    def in_place(item):
-        item = item.reshape(n_to, n_dest // n_to, own, DH)
-        item = jnp.stack([item[n_to - 1 - y] for y in range(n_to)])
-        return item.reshape(n_dest, own, DH)
-
     for h in range(heads):
         cut = low_ref.shape[0]
         pair = low_ref.at[h] if h < cut else high_ref.at[h - cut]
@@ -133,7 +128,7 @@
         both = weigh(scores, jnp.concatenate([top] * (keys // DH), axis=1), pair[1])
         total = total_ref[h] * fade + both[:, DH:]
         out = (sum_ref[h] * fade + both[:, :DH]) / total
-        out = in_place(out)
+        out = out.reshape(n_dest, own, DH)
         for b in range(qb):
             out_ref[:, h * qb + b] = out[:, b * qt : (b + 1) * qt].astype(BF)
         tops = jnp.where(lane == h, top, tops)
@@ -143,7 +138,7 @@
     rest = lse - high
     middle = rest.astype(BF).astype(F32)
     stats = high + pltpu.roll(middle, heads, 1) + pltpu.roll(rest - middle, 2 * heads, 1)
-    stats = in_place(stats)
+    stats = stats.reshape(n_dest, own, DH)
     joined = stats[:, :qt]
     for b in range(1, qb):
         joined = joined + pltpu.roll(stats, b * (DH // qb), 2)[:, b * qt : (b + 1) * qt]
@@ -278,7 +273,8 @@
         *state,
         flops=flops,
     )
-    part = lax.all_to_all(part, ("y", "head"), 0, 0)
+    order = [y * n_z + z for y in reversed(range(n_y)) for z in range(n_z)]
+    part = lax.all_to_all(part, ("y", "head"), 0, 0, axis_index_groups=[order])
     return call(functools.partial(merge_kernel, n_y), struct((qb, qt, d), BF), part)
 
 

time: 99.9 us -> 98.4 us (0.985)
  the two profiles are of different devices: /device:TPU:16 before, /device:TPU:8 now
where the time goes in v9:
time: 98.4 us; the launch traced here: 98 us
  blocking collectives  59.9 us (61%)
  starting transfers between devices  21.6 us (22%)
  Pallas kernels  10.4 us (11%)
  waiting for transfers between devices  5.17 us (5%)
    all_to_all x1, blocking collectives, local(): sorted_ = lax.all_to_all(packed, 'head', 0, 0)  32.4 us
    all_to_all x1, blocking collectives, local(): part = lax.all_to_all(part, ('y', 'head'), 0, 0, axis_index_groups=[order])  27.5 us
    ppermute x4, starting transfers between devices, shift(): lax.ppermute(block, axis, [(i, (i + by) % count) for i in range(count)])  14.1 us
    pallas_call x8, Pallas kernels, call(): pl.pallas_call(kernel, out_shape=out_shape, in_specs=[pl.BlockSpec(memory...  10.4 us
    all_to_all x1, starting transfers between devices, local(): lax.all_to_all(query, 'y', 0, 0, axis_index_groups=[list(range(n_y))[::-1]])  7.55 us
    all_to_all x1, waiting for transfers between devices, local(): lax.all_to_all(query, 'y', 0, 0, axis_index_groups=[list(range(n_y))[::-1]])  3.28 us
  transfers between devices with their start and end apart: 5, of which 2 were waited for; matrix products, arithmetic and copies ran while one was open for 1% of the time, Pallas kernels for 5%

profile of v9, /device:TPU:8, one launch (start us, length us, event | category | flops | bytes accessed | tf_op | source)
XLA Modules:
  0.0 98.0 jit_solution(2170763935891887960)
XLA Ops:
  0.0 2.1 %shard_map.55 = bf16[8,5,72,128]{3,2,1,0:T(8,128)(2,1)} custom-call(bf16[2,4,5120]{2,1,0:T(4,128)(2,1)} %q_hbm.1, bf16[2,16,5120]{2,1,0:T(8,128)(2,1)} %k_hbm.1, bf16[2,16,5120]{2,1,0:T(8,128)(2,1)} %v_hbm.1), custom_call_target="tpu_custom_call" | custom-call | bytes 1474560 | tf_op jit(solution)/shard_map/pallas_call | solution.py:176
  2.1 0.0 copy-start.1
  2.1 32.4 %all_to_all.15.sorted_ref = bf16[8,5,72,128]{3,2,1,0:T(8,128)(2,1)S(1)} all-to-all(bf16[8,5,72,128]{3,2,1,0:T(8,128)(2,1)} %shard_map.55), channel_id=1, replica_groups=mesh['cfg'=2,'head'=8,'x'=4,'y'=8] {'head'}, dimensions={0} | all-to-all | bytes 1474560 | tf_op jit(solution)/shard_map/all_to_all | solution.py:218
  34.5 3.4 %collective-permute-start = (bf16[5,2,256,128]{3,2,1,0:T(8,128)(2,1)S(1)}, bf16[5,2,256,128]{3,2,1,0:T(8,128)(2,1)S(1)}, u32[]{:S(2)}, u32[]{:S(2)}) collective-permute-start(bf16[5,2,256,128]{3,2,1,0:T(8,128)(2,1)S(1)} %shard_map.57.refs_0_), channel_id=1, source_target_pairs={{0,8},{8,16},{16,24},{24,0},{1,9},{9,17},{17,25},{25,1},{2,10},{10... | collective-permute-start | bytes 1966088 | tf_op jit(solution)/shard_map/ppermute | solution.py:189
  37.9 0.1 fusion.1
  38.0 0.1 iota_add_fusion
  38.1 0.1 add.61
  38.2 0.0 copy-done.1
  38.2 0.1 iota_compare_fusion
  38.3 3.6 %collective-permute-start.2 = (bf16[5,2,256,128]{3,2,1,0:T(8,128)(2,1)S(1)}, bf16[5,2,256,128]{3,2,1,0:T(8,128)(2,1)S(1)}, u32[]{:S(2)}, u32[]{:S(2)}) collective-permute-start(bf16[5,2,256,128]{3,2,1,0:T(8,128)(2,1)S(1)} %shard_map.57.refs_0_), channel_id=1, source_target_pairs={{0,24},{8,0},{16,8},{24,16},{1,25},{9,1},{17,9},{25,17},{2,26},{10... | collective-permute-start | bytes 1966088 | tf_op jit(solution)/shard_map/ppermute | solution.py:189
  41.9 0.9 shard_map.56
  42.8 7.5 %all-to-all-start.1 = ((bf16[8,5,64,128]{3,2,1,0:T(8,128)(2,1)}), bf16[8,5,64,128]{3,2,1,0:T(8,128)(2,1)S(1)}, u32[]{:S(2)}, u32[]{:S(2)}) async-start(bf16[8,5,64,128]{3,2,1,0:T(8,128)(2,1)} %shard_map.56), calls=%async_computation.1 | async-start | bytes 1310720 | tf_op jit(solution)/shard_map/all_to_all | solution.py:228
  50.4 1.9 %collective-permute-done.pair_ref.refs_1_ = bf16[5,2,256,128]{3,2,1,0:T(8,128)(2,1)S(1)} collective-permute-done((bf16[5,2,256,128]{3,2,1,0:T(8,128)(2,1)S(1)}, bf16[5,2,256,128]{3,2,1,0:T(8,128)(2,1)S(1)}, u32[]{:S(2)}, u32[]{:S(2)}) %collective-permute-start) | collective-permute-done | bytes 655392 | tf_op jit(solution)/shard_map/ppermute | solution.py:189
  52.3 0.8 shard_map.58
  53.0 0.0 copy-start
  53.0 2.2 %collective-permute-start.1 = (bf16[3,2,256,128]{3,2,1,0:T(8,128)(2,1)}, bf16[3,2,256,128]{3,2,1,0:T(8,128)(2,1)S(1)}, u32[]{:S(2)}, u32[]{:S(2)}) collective-permute-start(bf16[3,2,256,128]{3,2,1,0:T(8,128)(2,1)} %shard_map.58), channel_id=1, source_target_pairs={{0,8},{8,16},{16,24},{24,0},{1,9},{9,17},{17,25},{25,1},{2,10},{10... | collective-permute-start | bytes 1179656 | tf_op jit(solution)/shard_map/ppermute | solution.py:189
  55.2 0.0 collective-permute-done.2.pair_ref.refs_2_
  55.3 0.7 shard_map.59
  56.0 4.9 %collective-permute-start.3 = (bf16[2,2,256,128]{3,2,1,0:T(8,128)(2,1)}, bf16[2,2,256,128]{3,2,1,0:T(8,128)(2,1)S(1)}, u32[]{:S(2)}, u32[]{:S(2)}) collective-permute-start(bf16[2,2,256,128]{3,2,1,0:T(8,128)(2,1)} %shard_map.59), channel_id=1, source_target_pairs={{0,24},{8,0},{16,8},{24,16},{1,25},{9,1},{17,9},{25,17},{2,26},{10... | collective-permute-start | bytes 786440 | tf_op jit(solution)/shard_map/ppermute | solution.py:189
  60.9 0.0 copy-done
  60.9 0.4 and_reduce_fusion
  61.3 3.3 %all-to-all-done.1.q_ref = bf16[8,5,64,128]{3,2,1,0:T(8,128)(2,1)S(1)} async-done(((bf16[8,5,64,128]{3,2,1,0:T(8,128)(2,1)}), bf16[8,5,64,128]{3,2,1,0:T(8,128)(2,1)S(1)}, u32[]{:S(2)}, u32[]{:S(2)}) %all-to-all-start.1) | async-done | bytes 655392 | tf_op jit(solution)/shard_map/all_to_all | solution.py:228
  64.6 2.8 %shard_map.60 = (f32[5,512,128]{2,1,0:T(8,128)S(1)}, f32[5,512,128]{2,1,0:T(8,128)S(1)}, f32[5,512,128]{2,1,0:T(8,128)S(1)}) custom-call(bf16[8,5,64,128]{3,2,1,0:T(8,128)(2,1)S(1)} %all-to-all-done.1.q_ref, f32[64,8]{1,0:T(8,128)S(1)} %bitcast.5, bf16[5,2,256,128]{3,2,1,0:T(8,128)(2,1)S(1)} %shard_map.57.refs_0_, ...), custom_call_target="tpu_custom_call" | custom-call | tf_op jit(solution)/shard_map/pallas_call | solution.py:176
  67.4 0.0 collective-permute-done.3.high_ref
  67.4 0.0 collective-permute-done.1.low_ref
  67.4 1.6 %shard_map.61 = bf16[64,11,4,128]{3,2,1,0:T(4,128)(2,1)S(1)} custom-call(bf16[8,5,64,128]{3,2,1,0:T(8,128)(2,1)S(1)} %all-to-all-done.1.q_ref, f32[64,8]{1,0:T(8,128)S(1)} %bitcast.6, bf16[3,2,256,128]{3,2,1,0:T(8,128)(2,1)S(1)} %collective-permute-done.1.low_ref, bf16[2,2,256,128]{3,2,1,0:T(8,128)(2,1)S(1)} %collective-permute-done.3.high_ref, ...), custom_call_target="tpu_custom_call" | custom-call | flops 335544320 | bytes 5965824 | tf_op jit(solution)/shard_map/pallas_call | solution.py:176
  69.0 27.5 %all_to_all.16.part_ref = bf16[64,11,4,128]{3,2,1,0:T(4,128)(2,1)S(1)} all-to-all(bf16[64,11,4,128]{3,2,1,0:T(4,128)(2,1)S(1)} %shard_map.61), channel_id=1, replica_groups={{7,39,71,103,135,167,199,231,6,38,70,102,134,166,198,230,5,37,69,101,13..., dimensions={0} | all-to-all | bytes 1441792 | tf_op jit(solution)/shard_map/all_to_all | solution.py:277
  96.5 1.4 %shard_map.62 = bf16[2,4,5120]{2,1,0:T(4,128)(2,1)} custom-call(bf16[64,11,4,128]{3,2,1,0:T(4,128)(2,1)S(1)} %all_to_all.16.part_ref), custom_call_target="tpu_custom_call" | custom-call | bytes 802816 | tf_op jit(solution)/shard_map/pallas_call | solution.py:176
  (3 shorter events, 0.1 us)
Async XLA Ops:
  2.1 36.1 %copy-start.1 = (s32[16]{0:T(128)S(1)}, s32[16]{0:T(128)}, u32[]{:S(2)}) copy-start(s32[16]{0:T(128)} %param.9) | copy-start | bytes 196
  34.5 17.8 %collective-permute-start = (bf16[5,2,256,128]{3,2,1,0:T(8,128)(2,1)S(1)}, bf16[5,2,256,128]{3,2,1,0:T(8,128)(2,1)S(1)}, u32[]{:S(2)}, u32[]{:S(2)}) collective-permute-start(bf16[5,2,256,128]{3,2,1,0:T(8,128)(2,1)S(1)} %shard_map.57.refs_0_), channel_id=1, source_target_pairs={{0,8},{8,16},{16,24},{24,0},{1,9},{9,17},{17,25},{25,1},{2,10},{10... | collective-permute-start | bytes 1966088 | tf_op jit(solution)/shard_map/ppermute | solution.py:189
  38.3 17.0 %collective-permute-start.2 = (bf16[5,2,256,128]{3,2,1,0:T(8,128)(2,1)S(1)}, bf16[5,2,256,128]{3,2,1,0:T(8,128)(2,1)S(1)}, u32[]{:S(2)}, u32[]{:S(2)}) collective-permute-start(bf16[5,2,256,128]{3,2,1,0:T(8,128)(2,1)S(1)} %shard_map.57.refs_0_), channel_id=1, source_target_pairs={{0,24},{8,0},{16,8},{24,16},{1,25},{9,1},{17,9},{25,17},{2,26},{10... | collective-permute-start | bytes 1966088 | tf_op jit(solution)/shard_map/ppermute | solution.py:189
  42.8 21.7 %all-to-all-start.1 = ((bf16[8,5,64,128]{3,2,1,0:T(8,128)(2,1)}), bf16[8,5,64,128]{3,2,1,0:T(8,128)(2,1)S(1)}, u32[]{:S(2)}, u32[]{:S(2)}) async-start(bf16[8,5,64,128]{3,2,1,0:T(8,128)(2,1)} %shard_map.56), calls=%async_computation.1 | async-start | bytes 1310720 | tf_op jit(solution)/shard_map/all_to_all | solution.py:228
  53.0 7.8 %copy-start = (s32[16,32]{1,0:T(8,128)S(1)}, s32[16,32]{1,0:T(8,128)}, u32[]{:S(2)}) copy-start(s32[16,32]{1,0:T(8,128)} %param.8) | copy-start | bytes 6148
  53.0 14.4 %collective-permute-start.1 = (bf16[3,2,256,128]{3,2,1,0:T(8,128)(2,1)}, bf16[3,2,256,128]{3,2,1,0:T(8,128)(2,1)S(1)}, u32[]{:S(2)}, u32[]{:S(2)}) collective-permute-start(bf16[3,2,256,128]{3,2,1,0:T(8,128)(2,1)} %shard_map.58), channel_id=1, source_target_pairs={{0,8},{8,16},{16,24},{24,0},{1,9},{9,17},{17,25},{25,1},{2,10},{10... | collective-permute-start | bytes 1179656 | tf_op jit(solution)/shard_map/ppermute | solution.py:189
  56.0 11.4 %collective-permute-start.3 = (bf16[2,2,256,128]{3,2,1,0:T(8,128)(2,1)}, bf16[2,2,256,128]{3,2,1,0:T(8,128)(2,1)S(1)}, u32[]{:S(2)}, u32[]{:S(2)}) collective-permute-start(bf16[2,2,256,128]{3,2,1,0:T(8,128)(2,1)} %shard_map.59), channel_id=1, source_target_pairs={{0,24},{8,0},{16,8},{24,16},{1,25},{9,1},{17,9},{25,17},{2,26},{10... | collective-permute-start | bytes 786440 | tf_op jit(solution)/shard_map/ppermute | solution.py:189

commit v10 on v9

--- a/solution.py
+++ b/solution.py
@@ -99,9 +99,8 @@
         query = q_ref[:, h].reshape(rows, DH)
         scores = [scores_of(query, ref[h, 0], item) for ref, item in zip(pieces, bias, strict=True)]
         top = jnp.max(functools.reduce(jnp.maximum, scores), axis=1, keepdims=True)
-        both = jnp.zeros((rows, 2 * DH), F32)
-        for s, ref in zip(scores, pieces, strict=True):
-            both = both + weigh(s, top, ref[h, 1])
+        products = [weigh(s, top, ref[h, 1]) for s, ref in zip(scores, pieces, strict=True)]
+        both = functools.reduce(jnp.add, products)
         top_ref[h] = jnp.broadcast_to(top, (rows, DH))
         sum_ref[h] = both[:, :DH]
         total_ref[h] = both[:, DH:]

time: 98.4 us -> 98.4 us (level)
  no operation moved by 1% of the time
where the time goes in v10:
time: 98.4 us; the launch traced here: 98 us
  blocking collectives  59.8 us (61%)
  starting transfers between devices  21.6 us (22%)
  Pallas kernels  10.4 us (11%)
  waiting for transfers between devices  5.17 us (5%)
    all_to_all x1, blocking collectives, local(): sorted_ = lax.all_to_all(packed, 'head', 0, 0)  32.4 us
    all_to_all x1, blocking collectives, local(): part = lax.all_to_all(part, ('y', 'head'), 0, 0, axis_index_groups=[order])  27.5 us
    ppermute x4, starting transfers between devices, shift(): lax.ppermute(block, axis, [(i, (i + by) % count) for i in range(count)])  14.1 us
    pallas_call x8, Pallas kernels, call(): pl.pallas_call(kernel, out_shape=out_shape, in_specs=[pl.BlockSpec(memory...  10.4 us
    all_to_all x1, starting transfers between devices, local(): lax.all_to_all(query, 'y', 0, 0, axis_index_groups=[list(range(n_y))[::-1]])  7.55 us
    all_to_all x1, waiting for transfers between devices, local(): lax.all_to_all(query, 'y', 0, 0, axis_index_groups=[list(range(n_y))[::-1]])  3.28 us
  transfers between devices with their start and end apart: 5, of which 2 were waited for; matrix products, arithmetic and copies ran while one was open for 1% of the time, Pallas kernels for 5%

profile of v10, /device:TPU:8, one launch (start us, length us, event | category | flops | bytes accessed | tf_op | source)
XLA Modules:
  0.0 98.0 jit_solution(12123329532005612507)
XLA Ops:
  0.0 2.1 %shard_map.55 = bf16[8,5,72,128]{3,2,1,0:T(8,128)(2,1)} custom-call(bf16[2,4,5120]{2,1,0:T(4,128)(2,1)} %q_hbm.1, bf16[2,16,5120]{2,1,0:T(8,128)(2,1)} %k_hbm.1, bf16[2,16,5120]{2,1,0:T(8,128)(2,1)} %v_hbm.1), custom_call_target="tpu_custom_call" | custom-call | bytes 1474560 | tf_op jit(solution)/shard_map/pallas_call | solution.py:175
  2.1 0.0 copy-start.1
  2.1 32.4 %all_to_all.15.sorted_ref = bf16[8,5,72,128]{3,2,1,0:T(8,128)(2,1)S(1)} all-to-all(bf16[8,5,72,128]{3,2,1,0:T(8,128)(2,1)} %shard_map.55), channel_id=1, replica_groups=mesh['cfg'=2,'head'=8,'x'=4,'y'=8] {'head'}, dimensions={0} | all-to-all | bytes 1474560 | tf_op jit(solution)/shard_map/all_to_all | solution.py:217
  34.5 3.4 %collective-permute-start = (bf16[5,2,256,128]{3,2,1,0:T(8,128)(2,1)S(1)}, bf16[5,2,256,128]{3,2,1,0:T(8,128)(2,1)S(1)}, u32[]{:S(2)}, u32[]{:S(2)}) collective-permute-start(bf16[5,2,256,128]{3,2,1,0:T(8,128)(2,1)S(1)} %shard_map.57.refs_0_), channel_id=1, source_target_pairs={{0,8},{8,16},{16,24},{24,0},{1,9},{9,17},{17,25},{25,1},{2,10},{10... | collective-permute-start | bytes 1966088 | tf_op jit(solution)/shard_map/ppermute | solution.py:188
  37.9 0.1 fusion.1
  38.0 0.1 iota_add_fusion
  38.1 0.1 add.61
  38.2 0.0 copy-done.1
  38.2 0.1 iota_compare_fusion
  38.3 3.6 %collective-permute-start.2 = (bf16[5,2,256,128]{3,2,1,0:T(8,128)(2,1)S(1)}, bf16[5,2,256,128]{3,2,1,0:T(8,128)(2,1)S(1)}, u32[]{:S(2)}, u32[]{:S(2)}) collective-permute-start(bf16[5,2,256,128]{3,2,1,0:T(8,128)(2,1)S(1)} %shard_map.57.refs_0_), channel_id=1, source_target_pairs={{0,24},{8,0},{16,8},{24,16},{1,25},{9,1},{17,9},{25,17},{2,26},{10... | collective-permute-start | bytes 1966088 | tf_op jit(solution)/shard_map/ppermute | solution.py:188
  41.9 0.9 shard_map.56
  42.8 7.5 %all-to-all-start.1 = ((bf16[8,5,64,128]{3,2,1,0:T(8,128)(2,1)}), bf16[8,5,64,128]{3,2,1,0:T(8,128)(2,1)S(1)}, u32[]{:S(2)}, u32[]{:S(2)}) async-start(bf16[8,5,64,128]{3,2,1,0:T(8,128)(2,1)} %shard_map.56), calls=%async_computation.1 | async-start | bytes 1310720 | tf_op jit(solution)/shard_map/all_to_all | solution.py:227
  50.4 1.9 %collective-permute-done.pair_ref.refs_1_ = bf16[5,2,256,128]{3,2,1,0:T(8,128)(2,1)S(1)} collective-permute-done((bf16[5,2,256,128]{3,2,1,0:T(8,128)(2,1)S(1)}, bf16[5,2,256,128]{3,2,1,0:T(8,128)(2,1)S(1)}, u32[]{:S(2)}, u32[]{:S(2)}) %collective-permute-start) | collective-permute-done | bytes 655392 | tf_op jit(solution)/shard_map/ppermute | solution.py:188
  52.3 0.8 shard_map.58
  53.0 0.0 copy-start
  53.0 2.2 %collective-permute-start.1 = (bf16[3,2,256,128]{3,2,1,0:T(8,128)(2,1)}, bf16[3,2,256,128]{3,2,1,0:T(8,128)(2,1)S(1)}, u32[]{:S(2)}, u32[]{:S(2)}) collective-permute-start(bf16[3,2,256,128]{3,2,1,0:T(8,128)(2,1)} %shard_map.58), channel_id=1, source_target_pairs={{0,8},{8,16},{16,24},{24,0},{1,9},{9,17},{17,25},{25,1},{2,10},{10... | collective-permute-start | bytes 1179656 | tf_op jit(solution)/shard_map/ppermute | solution.py:188
  55.2 0.0 collective-permute-done.2.pair_ref.refs_2_
  55.3 0.7 shard_map.59
  56.0 4.9 %collective-permute-start.3 = (bf16[2,2,256,128]{3,2,1,0:T(8,128)(2,1)}, bf16[2,2,256,128]{3,2,1,0:T(8,128)(2,1)S(1)}, u32[]{:S(2)}, u32[]{:S(2)}) collective-permute-start(bf16[2,2,256,128]{3,2,1,0:T(8,128)(2,1)} %shard_map.59), channel_id=1, source_target_pairs={{0,24},{8,0},{16,8},{24,16},{1,25},{9,1},{17,9},{25,17},{2,26},{10... | collective-permute-start | bytes 786440 | tf_op jit(solution)/shard_map/ppermute | solution.py:188
  60.9 0.0 copy-done
  60.9 0.4 and_reduce_fusion
  61.3 3.3 %all-to-all-done.1.q_ref = bf16[8,5,64,128]{3,2,1,0:T(8,128)(2,1)S(1)} async-done(((bf16[8,5,64,128]{3,2,1,0:T(8,128)(2,1)}), bf16[8,5,64,128]{3,2,1,0:T(8,128)(2,1)S(1)}, u32[]{:S(2)}, u32[]{:S(2)}) %all-to-all-start.1) | async-done | bytes 655392 | tf_op jit(solution)/shard_map/all_to_all | solution.py:227
  64.6 2.8 %shard_map.60 = (f32[5,512,128]{2,1,0:T(8,128)S(1)}, f32[5,512,128]{2,1,0:T(8,128)S(1)}, f32[5,512,128]{2,1,0:T(8,128)S(1)}) custom-call(bf16[8,5,64,128]{3,2,1,0:T(8,128)(2,1)S(1)} %all-to-all-done.1.q_ref, f32[64,8]{1,0:T(8,128)S(1)} %bitcast.5, bf16[5,2,256,128]{3,2,1,0:T(8,128)(2,1)S(1)} %shard_map.57.refs_0_, ...), custom_call_target="tpu_custom_call" | custom-call | tf_op jit(solution)/shard_map/pallas_call | solution.py:175
  67.4 0.0 collective-permute-done.3.high_ref
  67.4 0.0 collective-permute-done.1.low_ref
  67.4 1.6 %shard_map.61 = bf16[64,11,4,128]{3,2,1,0:T(4,128)(2,1)S(1)} custom-call(bf16[8,5,64,128]{3,2,1,0:T(8,128)(2,1)S(1)} %all-to-all-done.1.q_ref, f32[64,8]{1,0:T(8,128)S(1)} %bitcast.6, bf16[3,2,256,128]{3,2,1,0:T(8,128)(2,1)S(1)} %collective-permute-done.1.low_ref, bf16[2,2,256,128]{3,2,1,0:T(8,128)(2,1)S(1)} %collective-permute-done.3.high_ref, ...), custom_call_target="tpu_custom_call" | custom-call | flops 335544320 | bytes 5965824 | tf_op jit(solution)/shard_map/pallas_call | solution.py:175
  69.1 27.5 %all_to_all.16.part_ref = bf16[64,11,4,128]{3,2,1,0:T(4,128)(2,1)S(1)} all-to-all(bf16[64,11,4,128]{3,2,1,0:T(4,128)(2,1)S(1)} %shard_map.61), channel_id=1, replica_groups={{7,39,71,103,135,167,199,231,6,38,70,102,134,166,198,230,5,37,69,101,13..., dimensions={0} | all-to-all | bytes 1441792 | tf_op jit(solution)/shard_map/all_to_all | solution.py:276
  96.5 1.4 %shard_map.62 = bf16[2,4,5120]{2,1,0:T(4,128)(2,1)} custom-call(bf16[64,11,4,128]{3,2,1,0:T(4,128)(2,1)S(1)} %all_to_all.16.part_ref), custom_call_target="tpu_custom_call" | custom-call | bytes 802816 | tf_op jit(solution)/shard_map/pallas_call | solution.py:175
  (3 shorter events, 0.1 us)
Async XLA Ops:
  2.1 36.1 %copy-start.1 = (s32[16]{0:T(128)S(1)}, s32[16]{0:T(128)}, u32[]{:S(2)}) copy-start(s32[16]{0:T(128)} %param.9) | copy-start | bytes 196
  34.5 17.8 %collective-permute-start = (bf16[5,2,256,128]{3,2,1,0:T(8,128)(2,1)S(1)}, bf16[5,2,256,128]{3,2,1,0:T(8,128)(2,1)S(1)}, u32[]{:S(2)}, u32[]{:S(2)}) collective-permute-start(bf16[5,2,256,128]{3,2,1,0:T(8,128)(2,1)S(1)} %shard_map.57.refs_0_), channel_id=1, source_target_pairs={{0,8},{8,16},{16,24},{24,0},{1,9},{9,17},{17,25},{25,1},{2,10},{10... | collective-permute-start | bytes 1966088 | tf_op jit(solution)/shard_map/ppermute | solution.py:188
  38.3 17.0 %collective-permute-start.2 = (bf16[5,2,256,128]{3,2,1,0:T(8,128)(2,1)S(1)}, bf16[5,2,256,128]{3,2,1,0:T(8,128)(2,1)S(1)}, u32[]{:S(2)}, u32[]{:S(2)}) collective-permute-start(bf16[5,2,256,128]{3,2,1,0:T(8,128)(2,1)S(1)} %shard_map.57.refs_0_), channel_id=1, source_target_pairs={{0,24},{8,0},{16,8},{24,16},{1,25},{9,1},{17,9},{25,17},{2,26},{10... | collective-permute-start | bytes 1966088 | tf_op jit(solution)/shard_map/ppermute | solution.py:188
  42.8 21.7 %all-to-all-start.1 = ((bf16[8,5,64,128]{3,2,1,0:T(8,128)(2,1)}), bf16[8,5,64,128]{3,2,1,0:T(8,128)(2,1)S(1)}, u32[]{:S(2)}, u32[]{:S(2)}) async-start(bf16[8,5,64,128]{3,2,1,0:T(8,128)(2,1)} %shard_map.56), calls=%async_computation.1 | async-start | bytes 1310720 | tf_op jit(solution)/shard_map/all_to_all | solution.py:227
  53.0 7.8 %copy-start = (s32[16,32]{1,0:T(8,128)S(1)}, s32[16,32]{1,0:T(8,128)}, u32[]{:S(2)}) copy-start(s32[16,32]{1,0:T(8,128)} %param.8) | copy-start | bytes 6148
  53.0 14.4 %collective-permute-start.1 = (bf16[3,2,256,128]{3,2,1,0:T(8,128)(2,1)}, bf16[3,2,256,128]{3,2,1,0:T(8,128)(2,1)S(1)}, u32[]{:S(2)}, u32[]{:S(2)}) collective-permute-start(bf16[3,2,256,128]{3,2,1,0:T(8,128)(2,1)} %shard_map.58), channel_id=1, source_target_pairs={{0,8},{8,16},{16,24},{24,0},{1,9},{9,17},{17,25},{25,1},{2,10},{10... | collective-permute-start | bytes 1179656 | tf_op jit(solution)/shard_map/ppermute | solution.py:188
  56.0 11.4 %collective-permute-start.3 = (bf16[2,2,256,128]{3,2,1,0:T(8,128)(2,1)}, bf16[2,2,256,128]{3,2,1,0:T(8,128)(2,1)S(1)}, u32[]{:S(2)}, u32[]{:S(2)}) collective-permute-start(bf16[2,2,256,128]{3,2,1,0:T(8,128)(2,1)} %shard_map.59), channel_id=1, source_target_pairs={{0,24},{8,0},{16,8},{24,16},{1,25},{9,1},{17,9},{25,17},{2,26},{10... | collective-permute-start | bytes 786440 | tf_op jit(solution)/shard_map/ppermute | solution.py:188
